TPU v7x, 256 devices: a whole 4x4x8 slice. The times are simulated.
256 devices in a mesh: path: 64 (over z, x, core), shard: 4 (over y).
Axes of the slice: x: 4, y: 4, z: 8, core: 2. Of those that a mesh axis runs over, the one named last changes fastest.
Arguments:
- pseudo_grad: bfloat16 [256, 16, 64, 1024], P('path', None, 'shard')
- kept_index: int32 [256, 16, 16, 16], P('path'), may hold values from 0 to 63, as said below
- usage: int32 [256, 16], replicated, may hold values from 0 to 15
- module_params: bfloat16 [256, 64, 1024], P('path', 'shard'), may hold values from -6 to 6
- momentum: float32 [256, 64, 1024], P('path', 'shard'), may hold values from -4 to 4
Outputs:
- new_params: bfloat16 [256, 64, 1024], P('path', 'shard')
- new_momentum: float32 [256, 64, 1024], P('path', 'shard')
- path_params: bfloat16 [256, 16, 64, 1024], P('path', None, 'shard')
Inputs may be any that keep to these rules, and one draw needn't show every extreme that they name: `kept_index`: the 16 indices of one block are distinct.
All inputs are finite; a program needn't handle non-finite values.
Results may differ from a plain program's by a relative error of at most 0.0049.
Values may be sent and summed in bfloat16 or wider, within the bound.
No kernel may reach another device: no remote copies, remote signals or barrier semaphores. Data moves between devices by JAX's collectives and lax.ppermute only.
A program may use at most 128 MiB of HBM per device.

v0:
```python
import functools
import math

import jax
import jax.numpy as jnp
import ml_dtypes
import numpy as np
from jax import lax
from jax.experimental import pallas as pl
from jax.experimental.pallas import tpu as pltpu
from jax.sharding import PartitionSpec as P

CH = 64
KEEP = 16
LEVELS = 16
OPTIONS = 16
ROWS = 16
WIDTH = 1024
PATHS = 256
DEVICES = 64
MINE = 4
QUAD = 4
COLS = WIDTH // QUAD
SENT = 40
F32 = jnp.float32
BF16 = jnp.bfloat16
VMEM_LIMIT = 40 * 1024 * 1024


def dct_tables():
    k = np.arange(CH)[:, None]
    n = np.arange(CH)[None, :]
    scale = np.where(k == 0, math.sqrt(1.0 / CH), math.sqrt(2.0 / CH))
    table = np.kron(np.eye(4), scale * np.cos(math.pi * (2.0 * n + 1.0) * k / (2.0 * CH)))
    high = table.astype(ml_dtypes.bfloat16)
    low = (table - high.astype(np.float64)).astype(ml_dtypes.bfloat16)
    inverse = np.stack([high, low])
    return np.ascontiguousarray(inverse.transpose(0, 2, 1)), inverse


def dot2(values, table_ref):
    return jnp.dot(values, table_ref[0], preferred_element_type=F32) + jnp.dot(
        values, table_ref[1], preferred_element_type=F32
    )


def take_lanes(values, index):
    return jnp.take_along_axis(values, index, axis=1, mode="promise_in_bounds")


def lanes(rows):
    return lax.broadcasted_iota(jnp.int32, (rows, 128), 1)


def base_kernel(q_ref, params_ref, momentum_ref, *out_refs):
    for k in range(QUAD):
        at = pl.ds(pl.multiple_of((q_ref[0] ^ k) * COLS, COLS), COLS)
        for i in range(MINE):
            base = params_ref[i, :, at].astype(F32) - 0.567 * momentum_ref[i, :, at]
            out_refs[k][i * ROWS : (i + 1) * ROWS, :] = base.astype(BF16)


def pick_kernel(grad_ref, kept_ref, table_ref, out_ref, spectrum_ref):
    levels = grad_ref.shape[1]
    grad = grad_ref[...].reshape(MINE * levels * ROWS, WIDTH)
    for q in range(QUAD):
        spectrum_ref[q] = dot2(grad[:, q * COLS : (q + 1) * COLS], table_ref)
    lane = lanes(ROWS)
    shift = ((lane // KEEP) % 2) * CH
    for level in range(levels):
        for q in range(QUAD):
            for pair in range(2):
                index = jnp.broadcast_to(kept_ref[level, q, pair : pair + 1, :], (ROWS, 128)) + shift

                def part(half, tile):
                    start = ((pair * 2 + half) * levels + level) * ROWS
                    rows = spectrum_ref[q, start : start + ROWS, tile * 128 : (tile + 1) * 128]
                    return take_lanes(rows, index)

                first = jnp.where(lane < 32, part(0, 0), part(0, 1))
                second = jnp.where(lane < 96, part(1, 0), part(1, 1))
                picked = jnp.where(lane < 64, first, second)
                out_ref[level * QUAD + q, pair * ROWS : (pair + 1) * ROWS, :] = picked.astype(BF16)
            index_rows = jnp.concatenate(
                [kept_ref[level, q].astype(F32), jnp.zeros((6, 128), F32)], axis=0
            )
            out_ref[level * QUAD + q, 32:40, :] = index_rows.astype(BF16)


def sum_kernel(usage_ref, got_ref, avg_ref, square_ref, *rest):
    peer_refs = rest[:3]
    where_ref = rest[3]
    total_refs = rest[4:8]
    count_ref = rest[8]
    lane = lanes(8)
    block = lane // CH
    k = lane % CH
    for total in total_refs:
        total[...] = jnp.zeros_like(total)
    for o in range(OPTIONS):
        count_ref[o] = 0

    def invert(group, carry):
        at = pl.ds(pl.multiple_of(group * 8, 8), 8)
        index = got_ref[at, 32:40, :].astype(F32)
        for pair in range(2):
            rows = index[:, pair, :].astype(jnp.int32)
            for half in range(2):
                for tile in range(2):
                    base = half * 64 + (tile * 2 + block) * KEEP
                    found = jnp.full((8, 128), -1, jnp.int32)
                    for j in range(KEEP):
                        found = jnp.where(take_lanes(rows, base + j) == k, base + j, found)
                    where_ref[pair * 4 + half * 2 + tile, at, :] = found
        return carry

    lax.fori_loop(0, DEVICES // 8, invert, 0)

    def add(s, carry):
        for pair in range(2):
            values = got_ref[s, pair * ROWS : (pair + 1) * ROWS, :].astype(F32)
            for half in range(2):
                o = usage_ref[s * MINE + pair * 2 + half]
                count_ref[o] += 1
                rows = pl.ds(pl.multiple_of(o * ROWS, ROWS), ROWS)
                total = total_refs[pair * 2 + half]
                for tile in range(2):
                    index = jnp.broadcast_to(
                        where_ref[pair * 4 + half * 2 + tile, pl.ds(s, 1), :], (ROWS, 128)
                    )
                    spread = jnp.where(index >= 0, take_lanes(values, jnp.maximum(index, 0)), 0.0)
                    total[rows, tile * 128 : (tile + 1) * 128] += spread
        return carry

    lax.fori_loop(0, DEVICES, add, 0, unroll=2)

    squares = jnp.zeros((1, 128), F32)
    for o in range(OPTIONS):
        at = slice(o * ROWS, (o + 1) * ROWS)
        summed = (total_refs[0][at, :] + total_refs[1][at, :]) + (
            total_refs[2][at, :] + total_refs[3][at, :]
        )
        average = summed / jnp.maximum(count_ref[o], 1).astype(F32)
        avg_ref[o // MINE, (o % MINE) * ROWS : (o % MINE + 1) * ROWS, :] = average.astype(BF16)
        square = jnp.sum(average * average, axis=(0, 1), keepdims=True)
        squares = jnp.where(lanes(1) == o, square, squares)
    square_ref[...] = jnp.broadcast_to(squares, (8, 128))
    high = squares.astype(BF16).astype(F32)
    middle = (squares - high).astype(BF16).astype(F32)
    low = squares - high - middle
    row = lax.broadcasted_iota(jnp.int32, (16, 128), 0)
    split = jnp.where(row == 0, high, jnp.where(row == 1, middle, jnp.where(row == 2, low, 0.0)))
    for i, peer_ref in enumerate(peer_refs):
        peer_ref[0:64, :] = avg_ref[usage_ref[PATHS] ^ (i + 1)]
        peer_ref[64:80, 0:128] = split.astype(BF16)
        peer_ref[64:80, 128:256] = jnp.zeros((16, 128), BF16)


def clip_factor(square_refs):
    total = (square_refs[0][0:1, :] + square_refs[1][0:1, :]) + (
        square_refs[2][0:1, :] + square_refs[3][0:1, :]
    )
    entries = 4.0 * ROWS * WIDTH
    return jnp.minimum(1.0, 0.3 / jnp.sqrt(total / entries + 1e-06))


def factor_of(factors, module):
    return jnp.sum(jnp.where(lanes(1) == module, factors, 0.0), axis=1, keepdims=True)


def reply_kernel(usage_ref, avg_ref, table_ref, *rest):
    base_refs = rest[:4]
    square_refs = rest[4:8]
    out_ref, fresh_ref = rest[8:]
    step = pl.program_id(0)

    @pl.when(step == 0)
    def _():
        factors = clip_factor(square_refs)
        for k in range(QUAD):
            owner = usage_ref[PATHS] ^ k
            delta = dot2(avg_ref[owner], table_ref)
            for i in range(MINE):
                module = owner * MINE + i
                at = slice(i * ROWS, (i + 1) * ROWS)
                change = (1.33 * factor_of(factors, module)) * delta[at, :]
                fresh = base_refs[k][at, :].astype(F32) - change
                fresh_ref[pl.ds(pl.multiple_of(module * ROWS, ROWS), ROWS), :] = fresh.astype(BF16)

    targets = out_ref.shape[0]
    for d in range(targets):
        for p in range(MINE):
            o = usage_ref[(step * targets + d) * MINE + p]
            out_ref[d, p] = fresh_ref[pl.ds(pl.multiple_of(o * ROWS, ROWS), ROWS), :]


def owner_kernel(usage_ref, avg_ref, table_ref, params_ref, momentum_ref, *rest):
    peer_refs = rest[:3]
    square_refs = rest[3:7]
    new_params_ref, new_momentum_ref = rest[7:]
    q = usage_ref[PATHS]
    factors = clip_factor(square_refs)
    for k in range(QUAD):
        at = pl.ds(pl.multiple_of((q ^ k) * COLS, COLS), COLS)
        average = avg_ref[q] if k == 0 else peer_refs[k - 1][0:64, :]
        delta = dot2(average, table_ref)
        for i in range(MINE):
            clipped = delta[i * ROWS : (i + 1) * ROWS, :] * factor_of(factors, q * MINE + i)
            momentum = 0.9 * momentum_ref[i, :, at] + clipped
            new_momentum_ref[i, :, at] = momentum
            new = params_ref[i, :, at].astype(F32) - 0.7 * (clipped + 0.9 * momentum)
            new_params_ref[i, :, at] = new.astype(BF16)


def place_kernel(got_ref, out_ref):
    for level in range(out_ref.shape[1]):
        for q in range(QUAD):
            for p in range(MINE):
                out_ref[p, level, :, q * COLS : (q + 1) * COLS] = got_ref[level * QUAD + q, p]


def call(kernel, out_shape, **kwargs):
    return pl.pallas_call(
        kernel,
        out_shape=out_shape,
        compiler_params=pltpu.CompilerParams(vmem_limit_bytes=VMEM_LIMIT),
        **kwargs,
    )


def shaped(shape, dtype):
    return jax.ShapeDtypeStruct(shape, dtype)


def swap(values, k):
    return lax.ppermute(values, "path", [(i, i ^ k) for i in range(DEVICES)])


def turn(values, k):
    return lax.ppermute(values, "shard", [(i, (i + k) % 4) for i in range(4)])


def local(pseudo_grad, kept_index, usage, module_params, momentum):
    forward, inverse = dct_tables()
    smem = pl.BlockSpec(memory_space=pltpu.SMEM)
    vmem = pl.BlockSpec(memory_space=pltpu.VMEM)
    device = lax.axis_index("path")
    level, q = device // QUAD, device % QUAD
    used = lax.dynamic_slice_in_dim(usage, level, 1, 1).reshape(PATHS)
    used = jnp.concatenate([used, jnp.full((8,), q, jnp.int32)])

    bases = call(
        base_kernel,
        [shaped((MINE * ROWS, COLS), BF16)] * QUAD,
        in_specs=[smem, vmem, vmem],
        out_specs=[vmem] * QUAD,
    )(jnp.full((1,), q, jnp.int32), module_params, momentum)
    bases = [bases[0]] + [swap(bases[k], k) for k in range(1, QUAD)]

    kept = kept_index.reshape(2, 2, LEVELS, QUAD, 4, KEEP).transpose(2, 3, 0, 1, 4, 5)
    kept = kept.reshape(LEVELS, QUAD, 2, 128)
    span = 4
    outgoing = call(
        pick_kernel,
        shaped((DEVICES, SENT, 128), BF16),
        grid=(LEVELS // span,),
        in_specs=[
            pl.BlockSpec((MINE, span, ROWS, WIDTH), lambda i: (0, i, 0, 0)),
            pl.BlockSpec((span, QUAD, 2, 128), lambda i: (i, 0, 0, 0)),
            pl.BlockSpec((2, COLS, COLS), lambda i: (0, 0, 0)),
        ],
        out_specs=pl.BlockSpec((span * QUAD, SENT, 128), lambda i: (i, 0, 0)),
        scratch_shapes=[pltpu.VMEM((QUAD, MINE * span * ROWS, COLS), F32)],
    )(pseudo_grad, kept, forward)
    got = lax.all_to_all(outgoing, "path", 0, 0, tiled=True)

    average, squares, *pieces = call(
        sum_kernel,
        [shaped((QUAD, MINE * ROWS, COLS), BF16), shaped((8, 128), F32)]
        + [shaped((MINE * ROWS + 16, COLS), BF16)] * 3,
        in_specs=[smem, vmem],
        out_specs=[vmem] * 5,
        scratch_shapes=[pltpu.VMEM((8, DEVICES, 128), jnp.int32)]
        + [pltpu.VMEM((OPTIONS * ROWS, COLS), F32)] * 4
        + [pltpu.SMEM((OPTIONS,), jnp.int32)],
    )(used, got)
    pieces = [swap(piece, k + 1) for k, piece in enumerate(pieces)]
    for piece in pieces:
        squares = squares + jnp.sum(piece[64:67, 0:128].astype(F32), axis=0, keepdims=True)
    all_squares = [squares] + [turn(squares, k) for k in range(1, 4)]

    targets = 8
    replies = call(
        reply_kernel,
        shaped((DEVICES, MINE, ROWS, COLS), BF16),
        grid=(DEVICES // targets,),
        in_specs=[smem] + [vmem] * 10,
        out_specs=pl.BlockSpec((targets, MINE, ROWS, COLS), lambda i: (i, 0, 0, 0)),
        scratch_shapes=[pltpu.VMEM((OPTIONS * ROWS, COLS), BF16)],
    )(used, average, inverse, *bases, *all_squares)
    returned = lax.all_to_all(replies, "path", 0, 0, tiled=True)

    new_params, new_momentum = call(
        owner_kernel,
        [shaped((MINE, ROWS, WIDTH), BF16), shaped((MINE, ROWS, WIDTH), F32)],
        in_specs=[smem] + [vmem] * 11,
        out_specs=[vmem] * 2,
    )(used, average, inverse, module_params, momentum, *pieces, *all_squares)

    span = 2
    path_params = call(
        place_kernel,
        shaped((MINE, LEVELS, ROWS, WIDTH), BF16),
        grid=(LEVELS // span,),
        in_specs=[pl.BlockSpec((span * QUAD, MINE, ROWS, COLS), lambda i: (i, 0, 0, 0))],
        out_specs=pl.BlockSpec((MINE, span, ROWS, WIDTH), lambda i: (0, i, 0, 0)),
    )(returned)
    return (new_params, new_momentum, path_params)


def solution(mesh):
    return jax.shard_map(
        local,
        mesh=mesh,
        in_specs=(
            P("path", None, "shard", None),
            P("path", None, None, None),
            P(),
            P("path", "shard", None),
            P("path", "shard", None),
        ),
        out_specs=(
            P("path", "shard", None),
            P("path", "shard", None),
            P("path", None, "shard", None),
        ),
        check_vma=False,
    )
```

profile of v0, /device:TPU:1, one launch (start us, length us, event | category | flops | bytes accessed | tf_op | source)
XLA Modules:
  0.0 126.3 jit_solution(11961640890447973380)
XLA Ops:
  0.6 0.0 copy-start
  0.6 1.2 copy.12
  1.8 0.4 reshape.20.kept_ref
  2.2 0.0 copy-start.2
  2.3 1.6 %copy-done.2 = bf16[4,16,16,1024]{3,2,1,0:T(8,128)(2,1)S(1)} copy-done((bf16[4,16,16,1024]{3,2,1,0:T(8,128)(2,1)S(1)}, bf16[4,16,16,1024]{3,2,1,0:T(8,128)(2,1)}, u32[]{:S(2)}) %copy-start.2) | copy-done | bytes 2097176
  3.8 0.0 copy-start.6
  3.8 0.9 copy-done.6
  4.8 0.0 copy-start.4
  4.8 0.0 copy-start.5
  4.8 0.0 copy-start.3
  4.8 3.4 %shard_map.94 = bf16[64,40,128]{2,1,0:T(8,128)(2,1)} custom-call(bf16[4,16,16,1024]{3,2,1,0:T(8,128)(2,1)S(1)} %copy-done.2, s32[16,4,2,128]{3,2,1,0:T(2,128)S(1)} %reshape.20.kept_ref, bf16[2,256,256]{2,1,0:T(8,128)(2,1)S(1)} %copy-done.6), custom_call_target="tpu_custom_call" | custom-call | tf_op jit(solution)/shard_map/pallas_call | solution.py:263
  8.2 13.0 %all-to-all-start = ((bf16[64,40,128]{2,1,0:T(8,128)(2,1)}), bf16[64,40,128]{2,1,0:T(8,128)(2,1)S(1)}, u32[]{:S(2)}, u32[]{:S(2)}) async-start(bf16[64,40,128]{2,1,0:T(8,128)(2,1)} %shard_map.94), calls=%async_computation | async-start | bytes 1310720 | tf_op jit(solution)/shard_map/all_to_all | solution.py:275
  21.2 0.0 copy-done
  21.3 20.3 %all-to-all-done.got_ref = bf16[64,40,128]{2,1,0:T(8,128)(2,1)S(1)} async-done(((bf16[64,40,128]{2,1,0:T(8,128)(2,1)}), bf16[64,40,128]{2,1,0:T(8,128)(2,1)S(1)}, u32[]{:S(2)}, u32[]{:S(2)}) %all-to-all-start) | async-done | bytes 655392 | tf_op jit(solution)/shard_map/all_to_all | solution.py:275
  41.6 8.0 %shard_map.95 = (bf16[4,64,256]{2,1,0:T(8,128)(2,1)S(1)}, f32[8,128]{1,0:T(8,128)S(1)}, bf16[80,256]{1,0:T(8,128)(2,1)S(1)}, bf16[80,256]{1,0:T(8,128)(2,1)S(1)}, bf16[80,256]{1,0:T(8,128)(2,1)S(1)}) custom-call(s32[264]{0:T(512)S(1)} %concatenate.3.usage_ref, bf16[64,40,128]{2,1,0:T(8,128)(2,1)S(1)} %all-to-all-done.got_ref), custom_call_target="tpu_custom_call" | custom-call | tf_op jit(solution)/shard_map/pallas_call | solution.py:277
  49.5 1.7 %collective-permute-start.2 = (bf16[80,256]{1,0:T(8,128)(2,1)S(1)}, bf16[80,256]{1,0:T(8,128)(2,1)S(1)}, u32[]{:S(2)}, u32[]{:S(2)}) collective-permute-start(bf16[80,256]{1,0:T(8,128)(2,1)S(1)} %get-tuple-element.17), channel_id=1, source_target_pairs={{0,12},{4,8},{8,4},{12,0},{16,28},{20,24},{24,20},{28,16},{32,44},... | collective-permute-start | bytes 122888 | tf_op jit(solution)/shard_map/ppermute | solution.py:236
  51.3 0.0 copy-done.4
  51.3 0.0 copy-done.5
  51.3 0.1 collective-permute-start.6
  51.4 0.4 collective-permute-start.7
  51.8 1.8 %collective-permute-start.8 = (bf16[64,256]{1,0:T(8,128)(2,1)S(1)}, bf16[64,256]{1,0:T(8,128)(2,1)S(1)}, u32[]{:S(2)}, u32[]{:S(2)}) collective-permute-start(bf16[64,256]{1,0:T(8,128)(2,1)S(1)} %get-tuple-element.24), channel_id=1, source_target_pairs={{0,12},{4,8},{8,4},{12,0},{16,28},{20,24},{24,20},{28,16},{32,44},... | collective-permute-start | bytes 98312 | tf_op jit(solution)/shard_map/ppermute | solution.py:236
  53.5 0.3 collective-permute-start.1
  53.8 0.0 collective-permute-done.2.rest_2_
  53.8 0.2 collective-permute-start
  54.0 2.9 %collective-permute-done.1.rest_1_ = bf16[80,256]{1,0:T(8,128)(2,1)S(1)} collective-permute-done((bf16[80,256]{1,0:T(8,128)(2,1)S(1)}, bf16[80,256]{1,0:T(8,128)(2,1)S(1)}, u32[]{:S(2)}, u32[]{:S(2)}) %collective-permute-start.1) | collective-permute-done | bytes 40992 | tf_op jit(solution)/shard_map/ppermute | solution.py:236
  56.9 0.0 collective-permute-done.rest_0_
  56.9 1.4 %collective-permute-start.3 = (f32[8,128]{1,0:T(8,128)S(1)}, f32[8,128]{1,0:T(8,128)S(1)}, u32[]{:S(2)}, u32[]{:S(2)}) collective-permute-start(f32[8,128]{1,0:T(8,128)S(1)} %add_add_fusion.rest_3_.rest_4_), channel_id=1, source_target_pairs={{0,1},{1,2},{2,3},{3,0},{4,5},{5,6},{6,7},{7,4},{8,9},{9,10},{10,1... | collective-permute-start | bytes 12296 | tf_op jit(solution)/shard_map/ppermute | solution.py:240
  58.3 2.6 %collective-permute-start.4 = (f32[8,128]{1,0:T(8,128)S(1)}, f32[8,128]{1,0:T(8,128)S(1)}, u32[]{:S(2)}, u32[]{:S(2)}) collective-permute-start(f32[8,128]{1,0:T(8,128)S(1)} %add_add_fusion.rest_3_.rest_4_), channel_id=1, source_target_pairs={{0,2},{1,3},{2,0},{3,1},{4,6},{5,7},{6,4},{7,5},{8,10},{9,11},{10,... | collective-permute-start | bytes 12296 | tf_op jit(solution)/shard_map/ppermute | solution.py:240
  60.9 0.0 collective-permute-done.6.rest_1_
  60.9 1.1 collective-permute-start.5
  62.0 0.0 collective-permute-done.7.rest_2_
  62.0 0.0 collective-permute-done.8.rest_3_
  62.0 0.0 collective-permute-done.3.rest_4_.rest_5_
  62.0 0.3 collective-permute-done.4.rest_5_.rest_6_
  62.3 1.4 %collective-permute-done.5.rest_6_.rest_7_ = f32[8,128]{1,0:T(8,128)S(1)} collective-permute-done((f32[8,128]{1,0:T(8,128)S(1)}, f32[8,128]{1,0:T(8,128)S(1)}, u32[]{:S(2)}, u32[]{:S(2)}) %collective-permute-start.5) | collective-permute-done | bytes 4128 | tf_op jit(solution)/shard_map/ppermute | solution.py:240
  63.7 0.0 copy-done.3
  63.7 1.3 %shard_map.98 = bf16[64,4,16,256]{3,2,1,0:T(8,128)(2,1)S(1)} custom-call(s32[264]{0:T(512)S(1)} %concatenate.3.usage_ref, bf16[4,64,256]{2,1,0:T(8,128)(2,1)S(1)} %get-tuple-element.14.avg_ref, bf16[2,256,256]{2,1,0:T(8,128)(2,1)S(1)} %copy-done.3, bf16[64,256]{1,0:T(8,128)(2,1)S(1)} %get-tuple-element.21.rest_0_, ...), custom_call_target="tpu_custom_call" | custom-call | tf_op jit(solution)/shard_map/pallas_call | solution.py:293
  65.0 0.0 copy-start.1
  65.0 1.3 %copy-done.1 = bf16[64,4,16,256]{3,2,1,0:T(8,128)(2,1)} copy-done((bf16[64,4,16,256]{3,2,1,0:T(8,128)(2,1)}, bf16[64,4,16,256]{3,2,1,0:T(8,128)(2,1)S(1)}, u32[]{:S(2)}) %copy-start.1) | copy-done | bytes 2097176
  66.3 7.4 %all-to-all-start.1 = ((bf16[64,4,16,256]{3,2,1,0:T(8,128)(2,1)}), bf16[64,4,16,256]{3,2,1,0:T(8,128)(2,1)S(1)}, u32[]{:S(2)}, u32[]{:S(2)}) async-start(bf16[64,4,16,256]{3,2,1,0:T(8,128)(2,1)} %copy-done.1), calls=%async_computation.1 | async-start | bytes 4194304 | tf_op jit(solution)/shard_map/all_to_all | solution.py:301
  73.7 1.6 %shard_map.96 = (bf16[4,16,1024]{2,1,0:T(8,128)(2,1)}, f32[4,16,1024]{2,1,0:T(8,128)}) custom-call(s32[264]{0:T(512)S(1)} %concatenate.3.usage_ref, bf16[4,64,256]{2,1,0:T(8,128)(2,1)S(1)} %get-tuple-element.14.avg_ref, bf16[2,256,256]{2,1,0:T(8,128)(2,1)S(1)} %copy-done.3, bf16[4,16,1024]{2,1,0:T(8,128)(2,1)S(1)} %copy-done.5, ...), custom_call_target="tpu_custom_call" | custom-call | tf_op jit(solution)/shard_map/pallas_call | solution.py:303
  75.3 48.1 %all-to-all-done.1.got_ref = bf16[64,4,16,256]{3,2,1,0:T(8,128)(2,1)S(1)} async-done(((bf16[64,4,16,256]{3,2,1,0:T(8,128)(2,1)}), bf16[64,4,16,256]{3,2,1,0:T(8,128)(2,1)S(1)}, u32[]{:S(2)}, u32[]{:S(2)}) %all-to-all-start.1) | async-done | bytes 2097184 | tf_op jit(solution)/shard_map/all_to_all | solution.py:301
  123.4 3.0 %shard_map.99 = bf16[4,16,16,1024]{3,2,1,0:T(8,128)(2,1)} custom-call(bf16[64,4,16,256]{3,2,1,0:T(8,128)(2,1)S(1)} %all-to-all-done.1.got_ref), custom_call_target="tpu_custom_call" | custom-call | tf_op jit(solution)/shard_map/pallas_call | solution.py:311
  (7 shorter events, 0.1 us)
Async XLA Ops:
  0.6 20.6 %copy-start = (s32[256,16]{0,1:T(8,128)S(1)}, s32[256,16]{0,1:T(8,128)}, u32[]{:S(2)}) copy-start(s32[256,16]{0,1:T(8,128)} %param.9) | copy-start | bytes 49156
  2.2 1.6 %copy-start.2 = (bf16[4,16,16,1024]{3,2,1,0:T(8,128)(2,1)S(1)}, bf16[4,16,16,1024]{3,2,1,0:T(8,128)(2,1)}, u32[]{:S(2)}) copy-start(bf16[4,16,16,1024]{3,2,1,0:T(8,128)(2,1)} %grad_ref.1) | copy-start | bytes 6291460
  3.8 0.9 copy-start.6
  4.8 46.5 %copy-start.4 = (f32[4,16,1024]{2,1,0:T(8,128)S(1)}, f32[4,16,1024]{2,1,0:T(8,128)}, u32[]{:S(2)}) copy-start(f32[4,16,1024]{2,1,0:T(8,128)} %momentum_ref.3) | copy-start | bytes 786436
  4.8 46.5 %copy-start.5 = (bf16[4,16,1024]{2,1,0:T(8,128)(2,1)S(1)}, bf16[4,16,1024]{2,1,0:T(8,128)(2,1)}, u32[]{:S(2)}) copy-start(bf16[4,16,1024]{2,1,0:T(8,128)(2,1)} %params_ref.3) | copy-start | bytes 393220
  4.8 58.9 %copy-start.3 = (bf16[2,256,256]{2,1,0:T(8,128)(2,1)S(1)}, bf16[2,256,256]{2,1,0:T(8,128)(2,1)}, u32[]{:S(2)}) copy-start(bf16[2,256,256]{2,1,0:T(8,128)(2,1)} %constant.42.clone.table_ref) | copy-start | bytes 786436
  8.2 33.4 %all-to-all-start = ((bf16[64,40,128]{2,1,0:T(8,128)(2,1)}), bf16[64,40,128]{2,1,0:T(8,128)(2,1)S(1)}, u32[]{:S(2)}, u32[]{:S(2)}) async-start(bf16[64,40,128]{2,1,0:T(8,128)(2,1)} %shard_map.94), calls=%async_computation | async-start | bytes 1310720 | tf_op jit(solution)/shard_map/all_to_all | solution.py:275
  49.5 4.3 %collective-permute-start.2 = (bf16[80,256]{1,0:T(8,128)(2,1)S(1)}, bf16[80,256]{1,0:T(8,128)(2,1)S(1)}, u32[]{:S(2)}, u32[]{:S(2)}) collective-permute-start(bf16[80,256]{1,0:T(8,128)(2,1)S(1)} %get-tuple-element.17), channel_id=1, source_target_pairs={{0,12},{4,8},{8,4},{12,0},{16,28},{20,24},{24,20},{28,16},{32,44},... | collective-permute-start | bytes 122888 | tf_op jit(solution)/shard_map/ppermute | solution.py:236
  51.3 9.6 %collective-permute-start.6 = (bf16[64,256]{1,0:T(8,128)(2,1)S(1)}, bf16[64,256]{1,0:T(8,128)(2,1)S(1)}, u32[]{:S(2)}, u32[]{:S(2)}) collective-permute-start(bf16[64,256]{1,0:T(8,128)(2,1)S(1)} %get-tuple-element.22), channel_id=1, source_target_pairs={{0,4},{4,0},{8,12},{12,8},{16,20},{20,16},{24,28},{28,24},{32,36},... | collective-permute-start | bytes 98312 | tf_op jit(solution)/shard_map/ppermute | solution.py:236
  51.4 10.6 %collective-permute-start.7 = (bf16[64,256]{1,0:T(8,128)(2,1)S(1)}, bf16[64,256]{1,0:T(8,128)(2,1)S(1)}, u32[]{:S(2)}, u32[]{:S(2)}) collective-permute-start(bf16[64,256]{1,0:T(8,128)(2,1)S(1)} %get-tuple-element.23), channel_id=1, source_target_pairs={{0,8},{4,12},{8,0},{12,4},{16,24},{20,28},{24,16},{28,20},{32,40},... | collective-permute-start | bytes 98312 | tf_op jit(solution)/shard_map/ppermute | solution.py:236
  51.8 10.2 %collective-permute-start.8 = (bf16[64,256]{1,0:T(8,128)(2,1)S(1)}, bf16[64,256]{1,0:T(8,128)(2,1)S(1)}, u32[]{:S(2)}, u32[]{:S(2)}) collective-permute-start(bf16[64,256]{1,0:T(8,128)(2,1)S(1)} %get-tuple-element.24), channel_id=1, source_target_pairs={{0,12},{4,8},{8,4},{12,0},{16,28},{20,24},{24,20},{28,16},{32,44},... | collective-permute-start | bytes 98312 | tf_op jit(solution)/shard_map/ppermute | solution.py:236
  53.5 3.3 %collective-permute-start.1 = (bf16[80,256]{1,0:T(8,128)(2,1)S(1)}, bf16[80,256]{1,0:T(8,128)(2,1)S(1)}, u32[]{:S(2)}, u32[]{:S(2)}) collective-permute-start(bf16[80,256]{1,0:T(8,128)(2,1)S(1)} %get-tuple-element.16), channel_id=1, source_target_pairs={{0,8},{4,12},{8,0},{12,4},{16,24},{20,28},{24,16},{28,20},{32,40},... | collective-permute-start | bytes 122888 | tf_op jit(solution)/shard_map/ppermute | solution.py:236
  53.8 3.1 %collective-permute-start = (bf16[80,256]{1,0:T(8,128)(2,1)S(1)}, bf16[80,256]{1,0:T(8,128)(2,1)S(1)}, u32[]{:S(2)}, u32[]{:S(2)}) collective-permute-start(bf16[80,256]{1,0:T(8,128)(2,1)S(1)} %get-tuple-element.15), channel_id=1, source_target_pairs={{0,4},{4,0},{8,12},{12,8},{16,20},{20,16},{24,28},{28,24},{32,36},... | collective-permute-start | bytes 122888 | tf_op jit(solution)/shard_map/ppermute | solution.py:236
  56.9 5.1 %collective-permute-start.3 = (f32[8,128]{1,0:T(8,128)S(1)}, f32[8,128]{1,0:T(8,128)S(1)}, u32[]{:S(2)}, u32[]{:S(2)}) collective-permute-start(f32[8,128]{1,0:T(8,128)S(1)} %add_add_fusion.rest_3_.rest_4_), channel_id=1, source_target_pairs={{0,1},{1,2},{2,3},{3,0},{4,5},{5,6},{6,7},{7,4},{8,9},{9,10},{10,1... | collective-permute-start | bytes 12296 | tf_op jit(solution)/shard_map/ppermute | solution.py:240
  58.3 4.0 %collective-permute-start.4 = (f32[8,128]{1,0:T(8,128)S(1)}, f32[8,128]{1,0:T(8,128)S(1)}, u32[]{:S(2)}, u32[]{:S(2)}) collective-permute-start(f32[8,128]{1,0:T(8,128)S(1)} %add_add_fusion.rest_3_.rest_4_), channel_id=1, source_target_pairs={{0,2},{1,3},{2,0},{3,1},{4,6},{5,7},{6,4},{7,5},{8,10},{9,11},{10,... | collective-permute-start | bytes 12296 | tf_op jit(solution)/shard_map/ppermute | solution.py:240
  60.9 2.8 %collective-permute-start.5 = (f32[8,128]{1,0:T(8,128)S(1)}, f32[8,128]{1,0:T(8,128)S(1)}, u32[]{:S(2)}, u32[]{:S(2)}) collective-permute-start(f32[8,128]{1,0:T(8,128)S(1)} %add_add_fusion.rest_3_.rest_4_), channel_id=1, source_target_pairs={{0,3},{1,0},{2,1},{3,2},{4,7},{5,4},{6,5},{7,6},{8,11},{9,8},{10,9... | collective-permute-start | bytes 12296 | tf_op jit(solution)/shard_map/ppermute | solution.py:240
  65.0 1.3 %copy-start.1 = (bf16[64,4,16,256]{3,2,1,0:T(8,128)(2,1)}, bf16[64,4,16,256]{3,2,1,0:T(8,128)(2,1)S(1)}, u32[]{:S(2)}) copy-start(bf16[64,4,16,256]{3,2,1,0:T(8,128)(2,1)S(1)} %shard_map.98) | copy-start | bytes 6291460
  66.3 57.0 %all-to-all-start.1 = ((bf16[64,4,16,256]{3,2,1,0:T(8,128)(2,1)}), bf16[64,4,16,256]{3,2,1,0:T(8,128)(2,1)S(1)}, u32[]{:S(2)}, u32[]{:S(2)}) async-start(bf16[64,4,16,256]{3,2,1,0:T(8,128)(2,1)} %copy-done.1), calls=%async_computation.1 | async-start | bytes 4194304 | tf_op jit(solution)/shard_map/all_to_all | solution.py:301
where the time goes:
time: 127 us; the launch traced here: 126 us
  waiting for transfers between devices  72.9 us (57%)
  starting transfers between devices  29.8 us (23%)
  Pallas kernels  17.3 us (14%)
  local copies, waits for them, and re-layouts  5.46 us (4%)
    all_to_all x1, waiting for transfers between devices, local(): returned = lax.all_to_all(replies, 'path', 0, 0, tiled=True)  48.1 us
    all_to_all x1, waiting for transfers between devices, local(): got = lax.all_to_all(outgoing, 'path', 0, 0, tiled=True)  20.3 us
    all_to_all x1, starting transfers between devices, local(): got = lax.all_to_all(outgoing, 'path', 0, 0, tiled=True)  13 us
    pallas_call x1, Pallas kernels, local(): call(sum_kernel, [shaped((QUAD, MINE * ROWS, COLS), BF16), shaped((8, 128...  7.97 us
    all_to_all x1, starting transfers between devices, local(): returned = lax.all_to_all(replies, 'path', 0, 0, tiled=True)  7.35 us
    ppermute x3, starting transfers between devices, turn(): return lax.ppermute(values, 'shard', [(i, (i + k) % 4) for i in range(4)])  5.06 us
    ppermute x6, starting transfers between devices, swap(): return lax.ppermute(values, 'path', [(i, i ^ k) for i in range(DEVICES)])  4.39 us
    unnamed x14, local copies, waits for them, and re-layouts  3.87 us
  transfers between devices with their start and end apart: 11, of which 5 were waited for; matrix products, arithmetic and copies ran while one was open for 0% of the time, Pallas kernels for 1%

commit v1 on v0

v1 whole, which is shorter than its diff:
```python
import functools
import math

import jax
import jax.numpy as jnp
import ml_dtypes
import numpy as np
from jax import lax
from jax.experimental import pallas as pl
from jax.experimental.pallas import tpu as pltpu
from jax.sharding import Mesh
from jax.sharding import PartitionSpec as P

CH = 64
KEEP = 16
LEVELS = 16
OPTIONS = 16
ROWS = 16
WIDTH = 1024
PATHS = 256
DEVICES = 64
MINE = 4
QUAD = 4
COLS = WIDTH // QUAD
SENT = 40
F32 = jnp.float32
BF16 = jnp.bfloat16
CHUNKS = 4
VMEM_LIMIT = 40 * 1024 * 1024
STREAM_LIMIT = 56 * 1024 * 1024
PATH = ("level", "quad")
SQUARE_GROUP = ("quad", "shard")


def dct_tables():
    k = np.arange(CH)[:, None]
    n = np.arange(CH)[None, :]
    scale = np.where(k == 0, math.sqrt(1.0 / CH), math.sqrt(2.0 / CH))
    table = np.kron(np.eye(4), scale * np.cos(math.pi * (2.0 * n + 1.0) * k / (2.0 * CH)))
    high = table.astype(ml_dtypes.bfloat16)
    low = (table - high.astype(np.float64)).astype(ml_dtypes.bfloat16)
    inverse = np.stack([high, low])
    return np.ascontiguousarray(inverse.transpose(0, 2, 1)), inverse


def dot2(values, table_ref):
    return jnp.dot(values, table_ref[0], preferred_element_type=F32) + jnp.dot(
        values, table_ref[1], preferred_element_type=F32
    )


def take_lanes(values, index):
    return jnp.take_along_axis(values, index, axis=1, mode="promise_in_bounds")


def lanes(rows):
    return lax.broadcasted_iota(jnp.int32, (rows, 128), 1)


def base_kernel(q_ref, params_ref, momentum_ref, *out_refs):
    for k in range(QUAD):
        at = pl.ds(pl.multiple_of((q_ref[0] ^ k) * COLS, COLS), COLS)
        for i in range(MINE):
            base = params_ref[i, :, at].astype(F32) - 0.567 * momentum_ref[i, :, at]
            out_refs[k][i * ROWS : (i + 1) * ROWS, :] = base


def sort_groups(values):
    lane = lanes(values.shape[0])
    size = 2
    while size <= KEEP:
        distance = size // 2
        while distance >= 1:
            other = take_lanes(values, lane ^ distance)
            upward = (lane & size) == 0 if size < KEEP else lane >= 0
            first = (lane & distance) == 0
            keep_least = first == upward
            values = jnp.where(keep_least, jnp.minimum(values, other), jnp.maximum(values, other))
            distance //= 2
        size *= 2
    return values


def gather_kept(kept_ref, pair):
    rows = LEVELS * 16
    repeat = (lanes(KEEP) % KEEP == lax.broadcasted_iota(jnp.int32, (KEEP, 128), 0)).astype(BF16)
    block = lax.broadcasted_iota(jnp.int32, (rows, 128), 0) % 4
    lane = lanes(rows)
    total = jnp.zeros((rows, 128), F32)
    for half in range(2):
        kept = kept_ref[pair * 2 + half].reshape(rows, KEEP).astype(F32).astype(BF16)
        spread = jnp.dot(kept, repeat, preferred_element_type=F32)
        total = jnp.where(lane // KEEP == half * 4 + block, spread, total)
    row = lax.broadcasted_iota(jnp.int32, (LEVELS * QUAD, rows), 0)
    column = lax.broadcasted_iota(jnp.int32, (LEVELS * QUAD, rows), 1)
    fold = (column // 4 == row).astype(BF16)
    return jnp.dot(fold, total.astype(BF16), preferred_element_type=F32).astype(jnp.int32)


def pick_kernel(
    grad_any,
    kept_any,
    table_any,
    out_any,
    grad_ref,
    kept_ref,
    table_ref,
    spectrum_ref,
    sorted_ref,
    out_ref,
    sems,
):
    kept = pltpu.make_async_copy(kept_any, kept_ref, sems.at[0])
    table = pltpu.make_async_copy(table_any, table_ref, sems.at[1])
    grads = [
        pltpu.make_async_copy(grad_any.at[p], grad_ref.at[p], sems.at[2 + p]) for p in range(MINE)
    ]
    emits = [
        pltpu.make_async_copy(out_ref.at[:, q], out_any.at[:, q], sems.at[2 + MINE + q])
        for q in range(QUAD)
    ]
    for copy in [kept, table] + grads:
        copy.start()
    kept.wait()
    for pair in range(2):
        sorted_ref[pair] = sort_groups(gather_kept(kept_ref, pair))
    lane = lanes(ROWS)
    shift = ((lane // KEEP) % 2) * CH
    for copy in [table] + grads:
        copy.wait()

    for q in range(QUAD):
        grad = grad_ref[:, :, :, q * COLS : (q + 1) * COLS].reshape(MINE * LEVELS * ROWS, COLS)
        spectrum_ref[q] = dot2(grad, table_ref)

        def pick(level, carry):
            for pair in range(2):
                row = sorted_ref[pair, pl.ds(level * QUAD + q, 1), :]
                index = jnp.broadcast_to(row, (ROWS, 128)) + shift

                def part(half, tile):
                    start = ((pair * 2 + half) * LEVELS + level) * ROWS
                    rows = pl.ds(pl.multiple_of(start, ROWS), ROWS)
                    return take_lanes(spectrum_ref[q, rows, tile * 128 : (tile + 1) * 128], index)

                first = jnp.where(lane < 32, part(0, 0), part(0, 1))
                second = jnp.where(lane < 96, part(1, 0), part(1, 1))
                picked = jnp.where(lane < 64, first, second)
                out_ref[level, q, pair * ROWS : (pair + 1) * ROWS, :] = picked.astype(BF16)
            rows = [sorted_ref[i, pl.ds(level * QUAD + q, 1), :].astype(F32) for i in range(2)]
            rows = jnp.concatenate(rows + [jnp.zeros((6, 128), F32)], axis=0)
            out_ref[level, q, 32:40, :] = rows.astype(BF16)
            return carry

        lax.fori_loop(0, LEVELS, pick, 0, unroll=True)
        emits[q].start()
    for copy in emits:
        copy.wait()


def sum_kernel(usage_ref, got_ref, avg_ref, square_ref, *rest):
    peer_refs = rest[:3]
    where_ref = rest[3]
    total_refs = rest[4:8]
    count_ref = rest[8]
    lane = lanes(8)
    block = lane // CH
    k = lane % CH
    for total in total_refs:
        total[...] = jnp.zeros_like(total)
    for o in range(OPTIONS):
        count_ref[o] = 0

    def invert(group, carry):
        at = pl.ds(pl.multiple_of(group * 8, 8), 8)
        index = got_ref[at, 32:40, :].astype(F32)
        for pair in range(2):
            rows = index[:, pair, :].astype(jnp.int32)
            for half in range(2):
                for tile in range(2):
                    place = half * 64 + (tile * 2 + block) * KEEP
                    held = take_lanes(rows, place)
                    for step in (8, 4, 2, 1):
                        probe = take_lanes(rows, place + step)
                        below = probe <= k
                        place = jnp.where(below, place + step, place)
                        held = jnp.where(below, probe, held)
                    found = jnp.where(held == k, place, -1)
                    where_ref[pair * 4 + half * 2 + tile, at, :] = found
        return carry

    lax.fori_loop(0, DEVICES // 8, invert, 0, unroll=4)

    def add(s, carry):
        for pair in range(2):
            values = got_ref[s, pair * ROWS : (pair + 1) * ROWS, :].astype(F32)
            for half in range(2):
                o = usage_ref[s * MINE + pair * 2 + half]
                count_ref[o] += 1
                rows = pl.ds(pl.multiple_of(o * ROWS, ROWS), ROWS)
                total = total_refs[pair * 2 + half]
                for tile in range(2):
                    index = jnp.broadcast_to(
                        where_ref[pair * 4 + half * 2 + tile, pl.ds(s, 1), :], (ROWS, 128)
                    )
                    spread = jnp.where(index >= 0, take_lanes(values, jnp.maximum(index, 0)), 0.0)
                    total[rows, tile * 128 : (tile + 1) * 128] += spread
        return carry

    lax.fori_loop(0, DEVICES, add, 0, unroll=16)

    squares = []
    for o in range(OPTIONS):
        at = slice(o * ROWS, (o + 1) * ROWS)
        summed = (total_refs[0][at, :] + total_refs[1][at, :]) + (
            total_refs[2][at, :] + total_refs[3][at, :]
        )
        average = summed / jnp.maximum(count_ref[o], 1).astype(F32)
        avg_ref[o // MINE, (o % MINE) * ROWS : (o % MINE + 1) * ROWS, :] = average.astype(BF16)
        square = average * average
        squares.append(jnp.sum(square[:, :128] + square[:, 128:], axis=0, keepdims=True))
    squares = jnp.sum(jnp.concatenate(squares, axis=0), axis=1, keepdims=True)
    square_ref[...] = jnp.broadcast_to(squares[None], square_ref.shape)
    for i, peer_ref in enumerate(peer_refs):
        peer_ref[...] = avg_ref[usage_ref[PATHS] ^ (i + 1)]


def clip_factor(square_ref):
    total = jnp.sum(square_ref[...], axis=0)
    entries = 4.0 * ROWS * WIDTH
    return jnp.minimum(1.0, 0.3 / jnp.sqrt(total / entries + 1e-06))


def reply_kernel(usage_ref, avg_ref, square_ref, table_ref, *rest):
    base_refs = rest[:4]
    out_any, factor_ref, fresh_ref, reply_ref, sems = rest[4:]
    factor_ref[...] = clip_factor(square_ref)
    for k in range(QUAD):
        owner = usage_ref[PATHS] ^ k
        delta = dot2(avg_ref[owner], table_ref)
        for i in range(MINE):
            module = owner * MINE + i
            at = slice(i * ROWS, (i + 1) * ROWS)
            change = (1.33 * factor_ref[pl.ds(module, 1), 0:1]) * delta[at, :]
            fresh = (base_refs[k][at, :] - change).astype(BF16)
            fresh_ref[pl.ds(pl.multiple_of(module * ROWS, ROWS), ROWS), :] = fresh

    chunks = sems.shape[0]
    targets = DEVICES // chunks

    def emit(c):
        at = pl.ds(c * targets, targets)
        return pltpu.make_async_copy(reply_ref.at[at], out_any.at[at], sems.at[c])

    def chunk(c, carry):
        for d in range(targets):
            target = c * targets + d
            for p in range(MINE):
                o = usage_ref[target * MINE + p]
                rows = pl.ds(pl.multiple_of(o * ROWS, ROWS), ROWS)
                reply_ref[target, p] = fresh_ref[rows, :]
        emit(c).start()
        return carry

    lax.fori_loop(0, chunks, chunk, 0)
    for c in range(chunks):
        emit(c).wait()


def owner_kernel(usage_ref, avg_ref, square_ref, table_ref, params_ref, momentum_ref, *rest):
    peer_refs = rest[:3]
    new_params_ref, new_momentum_ref, factor_ref = rest[3:]
    q = usage_ref[PATHS]
    factor_ref[...] = clip_factor(square_ref)
    for k in range(QUAD):
        at = pl.ds(pl.multiple_of((q ^ k) * COLS, COLS), COLS)
        average = avg_ref[q] if k == 0 else peer_refs[k - 1][...]
        delta = dot2(average, table_ref)
        for i in range(MINE):
            factor = factor_ref[pl.ds(q * MINE + i, 1), 0:1]
            clipped = delta[i * ROWS : (i + 1) * ROWS, :] * factor
            momentum = 0.9 * momentum_ref[i, :, at] + clipped
            new_momentum_ref[i, :, at] = momentum
            new = params_ref[i, :, at].astype(F32) - 0.7 * (clipped + 0.9 * momentum)
            new_params_ref[i, :, at] = new.astype(BF16)


def place_kernel(got_ref, out_ref, sems):
    copies = []
    for q in range(QUAD):
        for p in range(MINE):
            copies.append(
                pltpu.make_async_copy(
                    got_ref.at[:, q, p],
                    out_ref.at[p, :, :, pl.ds(q * COLS, COLS)],
                    sems.at[q * MINE + p],
                )
            )
    for copy in copies:
        copy.start()
    for copy in copies:
        copy.wait()


def call(kernel, out_shape, limit=VMEM_LIMIT, **kwargs):
    return pl.pallas_call(
        kernel,
        out_shape=out_shape,
        compiler_params=pltpu.CompilerParams(vmem_limit_bytes=limit),
        **kwargs,
    )


def shaped(shape, dtype):
    return jax.ShapeDtypeStruct(shape, dtype)


def swap(values, k):
    return lax.ppermute(values, "quad", [(i, i ^ k) for i in range(QUAD)])


def local(pseudo_grad, kept_index, usage, module_params, momentum):
    forward, inverse = dct_tables()
    smem = pl.BlockSpec(memory_space=pltpu.SMEM)
    vmem = pl.BlockSpec(memory_space=pltpu.VMEM)
    level, q = lax.axis_index("level"), lax.axis_index("quad")
    used = lax.dynamic_slice_in_dim(usage, level, 1, 1).reshape(PATHS)
    used = jnp.concatenate([used, jnp.full((8,), q, jnp.int32)])

    bases = call(
        base_kernel,
        [shaped((MINE * ROWS, COLS), F32)] * QUAD,
        in_specs=[smem, vmem, vmem],
        out_specs=[vmem] * QUAD,
    )(jnp.full((1,), q, jnp.int32), module_params, momentum)
    bases = [bases[0]] + [swap(bases[k], k) for k in range(1, QUAD)]

    anywhere = pl.BlockSpec(memory_space=pl.ANY)
    outgoing = call(
        pick_kernel,
        shaped((LEVELS, QUAD, SENT, 128), BF16),
        in_specs=[anywhere] * 3,
        out_specs=anywhere,
        scratch_shapes=[
            pltpu.VMEM((MINE, LEVELS, ROWS, WIDTH), BF16),
            pltpu.VMEM((MINE, LEVELS, 16, KEEP), jnp.int32),
            pltpu.VMEM((2, COLS, COLS), BF16),
            pltpu.VMEM((QUAD, MINE * LEVELS * ROWS, COLS), F32),
            pltpu.VMEM((2, LEVELS * QUAD, 128), jnp.int32),
            pltpu.VMEM((LEVELS, QUAD, SENT, 128), BF16),
            pltpu.SemaphoreType.DMA((2 + MINE + QUAD,)),
        ],
        limit=STREAM_LIMIT,
    )(pseudo_grad, kept_index, forward)
    got = lax.all_to_all(outgoing.reshape(DEVICES, SENT, 128), PATH, 0, 0, tiled=True)
    got, bases = lax.optimization_barrier((got, bases))

    average, squares, *pieces = call(
        sum_kernel,
        [shaped((QUAD, MINE * ROWS, COLS), BF16), shaped((16, OPTIONS, 128), F32)]
        + [shaped((MINE * ROWS, COLS), BF16)] * 3,
        in_specs=[smem, vmem],
        out_specs=[vmem] * 5,
        scratch_shapes=[pltpu.VMEM((8, DEVICES, 128), jnp.int32)]
        + [pltpu.VMEM((OPTIONS * ROWS, COLS), F32)] * 4
        + [pltpu.SMEM((OPTIONS,), jnp.int32)],
    )(used, got)
    squares = lax.all_to_all(squares, SQUARE_GROUP, 0, 0, tiled=True)

    replies = call(
        reply_kernel,
        shaped((DEVICES, MINE, ROWS, COLS), BF16),
        in_specs=[smem] + [vmem] * 7,
        out_specs=anywhere,
        scratch_shapes=[
            pltpu.VMEM((OPTIONS, 128), F32),
            pltpu.VMEM((OPTIONS * ROWS, COLS), BF16),
            pltpu.VMEM((DEVICES, MINE, ROWS, COLS), BF16),
            pltpu.SemaphoreType.DMA((CHUNKS,)),
        ],
        limit=STREAM_LIMIT,
    )(used, average, squares, inverse, *bases)
    returned = lax.all_to_all(replies, PATH, 0, 0, tiled=True)

    pieces, replies = lax.optimization_barrier((pieces, replies))
    pieces = [swap(piece, k + 1) for k, piece in enumerate(pieces)]

    new_params, new_momentum = call(
        owner_kernel,
        [shaped((MINE, ROWS, WIDTH), BF16), shaped((MINE, ROWS, WIDTH), F32)],
        in_specs=[smem] + [vmem] * 8,
        out_specs=[vmem] * 2,
        scratch_shapes=[pltpu.VMEM((OPTIONS, 128), F32)],
    )(used, average, squares, inverse, module_params, momentum, *pieces)

    path_params = call(
        place_kernel,
        shaped((MINE, LEVELS, ROWS, WIDTH), BF16),
        in_specs=[anywhere],
        out_specs=anywhere,
        scratch_shapes=[pltpu.SemaphoreType.DMA((QUAD * MINE,))],
    )(returned.reshape(LEVELS, QUAD, MINE, ROWS, COLS))
    return (new_params, new_momentum, path_params)


def solution(mesh):
    mesh = Mesh(mesh.devices.reshape(LEVELS, QUAD, 4), PATH + ("shard",))
    return jax.shard_map(
        local,
        mesh=mesh,
        in_specs=(
            P(PATH, None, "shard", None),
            P(PATH, None, None, None),
            P(),
            P(PATH, "shard", None),
            P(PATH, "shard", None),
        ),
        out_specs=(
            P(PATH, "shard", None),
            P(PATH, "shard", None),
            P(PATH, None, "shard", None),
        ),
        check_vma=False,
    )
```

time: 127 us -> 116 us (0.913)
  blocking collectives: 0 us -> 12 us
  waiting for transfers between devices: 72.9 us -> 63.2 us
  starting transfers between devices: 29.8 us -> 23.3 us
  local copies, waits for them, and re-layouts: 5.46 us -> 1.35 us
  Pallas kernels: 17.3 us -> 14.6 us
    all_to_all x2, waiting for transfers between devices: 68.3 us -> 49.9 us  [the longest x1 38.4 us: local(): returned = lax.all_to_all(replies, PATH, 0, 0, tiled=True)]
    all_to_all x0 -> x1, blocking collectives: none -> 12 us  [local(): squares = lax.all_to_all(squares, SQUARE_GROUP, 0, 0, tiled=True)]
    ppermute x9 -> x6, waiting for transfers between devices: 4.55 us -> 13.3 us  [swap(): return lax.ppermute(values, 'quad', [(i, i ^ k) for i in range(QUAD)])]
    ppermute x9 -> x6, starting transfers between devices: 9.45 us -> 4.41 us  [swap(): return lax.ppermute(values, 'quad', [(i, i ^ k) for i in range(QUAD)])]
    pallas_call x5, Pallas kernels: 15.7 us -> 13 us  [the longest x1 4.95 us: local(): call(pick_kernel, shaped((LEVELS, QUAD, SENT, 128), BF16), in_specs=[anyw...]
    unnamed x14 -> x26, local copies, waits for them, and re-layouts: 3.87 us -> 1.34 us
    reshape x2 -> x0, local copies, waits for them, and re-layouts: 1.58 us -> none  [the longest x1 1.17 us: local(): kept_index.reshape(2, 2, LEVELS, QUAD, 4, KEEP).transpose(2, 3, 0, 1, 4, 5)]
    all_to_all x2, starting transfers between devices: 20.3 us -> 18.9 us  [the longest x1 13 us: local(): lax.all_to_all(outgoing.reshape(DEVICES, SENT, 128), PATH, 0, 0, tiled=True)]
  transfers between devices with their start and end apart: 11 -> 8, of which waited for: 5 -> 6; matrix products, arithmetic and copies ran while one was open for 0% -> 0% of each run, Pallas kernels for 1% -> 1%
where the time goes in v1:
time: 116 us; the launch traced here: 115 us
  waiting for transfers between devices  63.2 us (54%)
  starting transfers between devices  23.3 us (20%)
  Pallas kernels  14.6 us (13%)
  blocking collectives  12 us (10%)
  local copies, waits for them, and re-layouts  1.35 us (1%)
    all_to_all x1, waiting for transfers between devices, local(): returned = lax.all_to_all(replies, PATH, 0, 0, tiled=True)  38.4 us
    ppermute x6, waiting for transfers between devices, swap(): return lax.ppermute(values, 'quad', [(i, i ^ k) for i in range(QUAD)])  13.3 us
    all_to_all x1, starting transfers between devices, local(): lax.all_to_all(outgoing.reshape(DEVICES, SENT, 128), PATH, 0, 0, tiled=True)  13 us
    all_to_all x1, blocking collectives, local(): squares = lax.all_to_all(squares, SQUARE_GROUP, 0, 0, tiled=True)  12 us
    all_to_all x1, waiting for transfers between devices, local(): lax.all_to_all(outgoing.reshape(DEVICES, SENT, 128), PATH, 0, 0, tiled=True)  11.6 us
    all_to_all x1, starting transfers between devices, local(): returned = lax.all_to_all(replies, PATH, 0, 0, tiled=True)  5.88 us
    pallas_call x1, Pallas kernels, local(): call(pick_kernel, shaped((LEVELS, QUAD, SENT, 128), BF16), in_specs=[anyw...  4.95 us
    ppermute x6, starting transfers between devices, swap(): return lax.ppermute(values, 'quad', [(i, i ^ k) for i in range(QUAD)])  4.41 us
  transfers between devices with their start and end apart: 8, of which 6 were waited for; matrix products, arithmetic and copies ran while one was open for 0% of the time, Pallas kernels for 1%

profile of v1, /device:TPU:1, one launch (start us, length us, event | category | flops | bytes accessed | tf_op | source)
XLA Modules:
  0.0 115.3 jit_solution(12560911613286080085)
XLA Ops:
  0.6 0.0 copy-start
  0.6 0.0 copy-start.3
  0.7 0.0 copy-start.6
  0.7 5.0 %shard_map.94 = bf16[16,4,40,128]{3,2,1,0:T(8,128)(2,1)} custom-call(bf16[4,16,16,1024]{3,2,1,0:T(8,128)(2,1)} %grad_any.1, s32[4,16,16,16]{3,2,1,0:T(8,128)} %kept_any.1, bf16[2,256,256]{2,1,0:T(8,128)(2,1)} %constant.18.clone.table_any), custom_call_target="tpu_custom_call" | custom-call | tf_op jit(solution)/shard_map/pallas_call | solution.py:339
  5.6 13.0 %all-to-all-start = ((bf16[64,40,128]{2,1,0:T(8,128)(2,1)}), bf16[64,40,128]{2,1,0:T(8,128)(2,1)S(1)}, u32[]{:S(2)}, u32[]{:S(2)}) async-start(bf16[64,40,128]{2,1,0:T(8,128)(2,1)} %bitcast.5), calls=%async_computation | async-start | bytes 1310720 | tf_op jit(solution)/shard_map/all_to_all | solution.py:355
  18.6 0.0 copy-done.3
  18.6 0.0 copy-done.6
  18.7 0.0 copy-start.7
  18.7 0.6 copy-done.7
  19.3 0.5 collective-permute-start
  19.8 1.3 %collective-permute-start.1 = (f32[64,256]{1,0:T(8,128)S(1)}, f32[64,256]{1,0:T(8,128)S(1)}, u32[]{:S(2)}, u32[]{:S(2)}) collective-permute-start(f32[64,256]{1,0:T(8,128)S(1)} %get-tuple-element.24), channel_id=1, source_target_pairs={{0,8},{4,12},{8,0},{12,4},{1,9},{5,13},{9,1},{13,5},{2,10},{6,14},... | collective-permute-start | bytes 196616 | tf_op jit(solution)/shard_map/ppermute | solution.py:319
  21.1 0.4 collective-permute-start.2
  21.5 0.0 copy-done
  21.5 0.0 copy-start.8
  21.5 0.0 collective-permute-done.rest_1_
  21.5 0.0 copy-start.10
  21.5 2.4 %collective-permute-done.1.rest_2_ = f32[64,256]{1,0:T(8,128)S(1)} collective-permute-done((f32[64,256]{1,0:T(8,128)S(1)}, f32[64,256]{1,0:T(8,128)S(1)}, u32[]{:S(2)}, u32[]{:S(2)}) %collective-permute-start.1) | collective-permute-done | bytes 65568 | tf_op jit(solution)/shard_map/ppermute | solution.py:319
  24.0 0.0 copy-start.11
  24.0 3.5 %collective-permute-done.2.rest_3_ = f32[64,256]{1,0:T(8,128)S(1)} collective-permute-done((f32[64,256]{1,0:T(8,128)S(1)}, f32[64,256]{1,0:T(8,128)S(1)}, u32[]{:S(2)}, u32[]{:S(2)}) %collective-permute-start.2) | collective-permute-done | bytes 65568 | tf_op jit(solution)/shard_map/ppermute | solution.py:319
  27.4 0.0 copy-start.12
  27.4 11.6 %all-to-all-done.got_ref = bf16[64,40,128]{2,1,0:T(8,128)(2,1)S(1)} async-done(((bf16[64,40,128]{2,1,0:T(8,128)(2,1)}), bf16[64,40,128]{2,1,0:T(8,128)(2,1)S(1)}, u32[]{:S(2)}, u32[]{:S(2)}) %all-to-all-start) | async-done | bytes 655392 | tf_op jit(solution)/shard_map/all_to_all | solution.py:355
  39.0 3.7 %shard_map.96 = (bf16[4,64,256]{2,1,0:T(8,128)(2,1)S(1)}, f32[16,16,128]{2,1,0:T(8,128)S(1)}, bf16[64,256]{1,0:T(8,128)(2,1)S(1)}, bf16[64,256]{1,0:T(8,128)(2,1)S(1)}, bf16[64,256]{1,0:T(8,128)(2,1)S(1)}) custom-call(s32[264]{0:T(512)S(1)} %concatenate.3.usage_ref, bf16[64,40,128]{2,1,0:T(8,128)(2,1)S(1)} %all-to-all-done.got_ref), custom_call_target="tpu_custom_call" | custom-call | tf_op jit(solution)/shard_map/pallas_call | solution.py:358
  42.7 0.0 copy-start.4
  42.7 0.7 copy-done.4
  43.3 12.0 %all_to_all.15.square_ref = f32[16,16,128]{2,1,0:T(8,128)} all-to-all(f32[16,16,128]{2,1,0:T(8,128)S(1)} %get-tuple-element.28), channel_id=1, replica_groups=mesh['level'=16,'quad'=4,'shard'=4] {'quad','shard'}, dimensions={0} | all-to-all | bytes 262144 | tf_op jit(solution)/shard_map/all_to_all | solution.py:368
  55.3 0.0 copy-done.8
  55.3 0.0 copy-done.10
  55.3 0.0 copy-done.11
  55.3 0.0 copy-done.12
  55.3 2.9 %shard_map.97 = bf16[64,4,16,256]{3,2,1,0:T(8,128)(2,1)} custom-call(s32[264]{0:T(512)} %copy-done.8, bf16[4,64,256]{2,1,0:T(8,128)(2,1)} %copy-done.4, f32[16,16,128]{2,1,0:T(8,128)} %all_to_all.15.square_ref, bf16[2,256,256]{2,1,0:T(8,128)(2,1)} %constant.19.clone.table_ref, f32[64,256]{1,0:T(8,128)} %copy-done.7, f32[64,256]{1,0:T(8,128)} %copy-done.10, ...), custom_call_target="tpu_custom_call" | custom-call | tf_op jit(solution)/shard_map/pallas_call | solution.py:370
  58.2 0.0 copy-start.1
  58.2 0.0 copy-start.2
  58.3 0.0 copy-start.5
  58.3 0.0 copy-start.9
  58.3 5.9 %all-to-all-start.2 = ((bf16[64,4,16,256]{3,2,1,0:T(8,128)(2,1)}), bf16[64,4,16,256]{3,2,1,0:T(8,128)(2,1)S(1)}, u32[]{:S(2)}, u32[]{:S(2)}) async-start(bf16[64,4,16,256]{3,2,1,0:T(8,128)(2,1)} %shard_map.97), calls=%async_computation.2 | async-start | bytes 4194304 | tf_op jit(solution)/shard_map/all_to_all | solution.py:383
  64.2 0.5 collective-permute-start.3
  64.7 1.3 %collective-permute-start.4 = (bf16[64,256]{1,0:T(8,128)(2,1)S(1)}, bf16[64,256]{1,0:T(8,128)(2,1)S(1)}, u32[]{:S(2)}, u32[]{:S(2)}) collective-permute-start(bf16[64,256]{1,0:T(8,128)(2,1)S(1)} %get-tuple-element.37), channel_id=1, source_target_pairs={{0,8},{4,12},{8,0},{12,4},{1,9},{5,13},{9,1},{13,5},{2,10},{6,14},... | collective-permute-start | bytes 98312 | tf_op jit(solution)/shard_map/ppermute | solution.py:319
  66.0 0.4 collective-permute-start.5
  66.4 0.0 collective-permute-done.3.rest_0_
  66.4 5.0 %collective-permute-done.4.rest_1_ = bf16[64,256]{1,0:T(8,128)(2,1)S(1)} collective-permute-done((bf16[64,256]{1,0:T(8,128)(2,1)S(1)}, bf16[64,256]{1,0:T(8,128)(2,1)S(1)}, u32[]{:S(2)}, u32[]{:S(2)}) %collective-permute-start.4) | collective-permute-done | bytes 32800 | tf_op jit(solution)/shard_map/ppermute | solution.py:319
  71.5 2.3 %collective-permute-done.5.rest_2_ = bf16[64,256]{1,0:T(8,128)(2,1)S(1)} collective-permute-done((bf16[64,256]{1,0:T(8,128)(2,1)S(1)}, bf16[64,256]{1,0:T(8,128)(2,1)S(1)}, u32[]{:S(2)}, u32[]{:S(2)}) %collective-permute-start.5) | collective-permute-done | bytes 32800 | tf_op jit(solution)/shard_map/ppermute | solution.py:319
  73.8 0.0 copy-done.1
  73.8 0.0 copy-done.2
  73.8 0.0 copy-done.5
  73.8 0.0 copy-done.9
  73.8 1.6 %shard_map.98 = (bf16[4,16,1024]{2,1,0:T(8,128)(2,1)}, f32[4,16,1024]{2,1,0:T(8,128)}) custom-call(s32[264]{0:T(512)S(1)} %copy-done.9, bf16[4,64,256]{2,1,0:T(8,128)(2,1)S(1)} %copy-done.5, f32[16,16,128]{2,1,0:T(8,128)S(1)} %copy-done.1, bf16[2,256,256]{2,1,0:T(8,128)(2,1)S(1)} %copy-done.2, bf16[4,16,1024]{2,1,0:T(8,128)(2,1)S(1)} %copy-done.6, ...), custom_call_target="tpu_custom_call" | custom-call | tf_op jit(solution)/shard_map/pallas_call | solution.py:388
  75.4 38.4 %all-to-all-done.2 = bf16[64,4,16,256]{3,2,1,0:T(8,128)(2,1)S(1)} async-done(((bf16[64,4,16,256]{3,2,1,0:T(8,128)(2,1)}), bf16[64,4,16,256]{3,2,1,0:T(8,128)(2,1)S(1)}, u32[]{:S(2)}, u32[]{:S(2)}) %all-to-all-start.2) | async-done | bytes 2097184 | tf_op jit(solution)/shard_map/all_to_all | solution.py:383
  113.8 1.4 %shard_map.99 = bf16[4,16,16,1024]{3,2,1,0:T(8,128)(2,1)} custom-call(bf16[16,4,4,16,256]{4,3,2,1,0:T(8,128)(2,1)S(1)} %bitcast.4), custom_call_target="tpu_custom_call" | custom-call | tf_op jit(solution)/shard_map/pallas_call | solution.py:396
  (3 shorter events, 0.1 us)
Async XLA Ops:
  0.6 20.9 %copy-start = (s32[256,16]{0,1:T(8,128)S(1)}, s32[256,16]{0,1:T(8,128)}, u32[]{:S(2)}) copy-start(s32[256,16]{0,1:T(8,128)} %param.9) | copy-start | bytes 49156
  0.6 18.0 %copy-start.3 = (f32[4,16,1024]{2,1,0:T(8,128)S(1)}, f32[4,16,1024]{2,1,0:T(8,128)}, u32[]{:S(2)}) copy-start(f32[4,16,1024]{2,1,0:T(8,128)} %momentum_ref.3) | copy-start | bytes 786436
  0.7 18.0 %copy-start.6 = (bf16[4,16,1024]{2,1,0:T(8,128)(2,1)S(1)}, bf16[4,16,1024]{2,1,0:T(8,128)(2,1)}, u32[]{:S(2)}) copy-start(bf16[4,16,1024]{2,1,0:T(8,128)(2,1)} %params_ref.3) | copy-start | bytes 393220
  5.6 33.4 %all-to-all-start = ((bf16[64,40,128]{2,1,0:T(8,128)(2,1)}), bf16[64,40,128]{2,1,0:T(8,128)(2,1)S(1)}, u32[]{:S(2)}, u32[]{:S(2)}) async-start(bf16[64,40,128]{2,1,0:T(8,128)(2,1)} %bitcast.5), calls=%async_computation | async-start | bytes 1310720 | tf_op jit(solution)/shard_map/all_to_all | solution.py:355
  18.7 0.6 copy-start.7
  19.3 2.2 %collective-permute-start = (f32[64,256]{1,0:T(8,128)S(1)}, f32[64,256]{1,0:T(8,128)S(1)}, u32[]{:S(2)}, u32[]{:S(2)}) collective-permute-start(f32[64,256]{1,0:T(8,128)S(1)} %get-tuple-element.23), channel_id=1, source_target_pairs={{0,4},{4,0},{8,12},{12,8},{1,5},{5,1},{9,13},{13,9},{2,6},{6,2},{1... | collective-permute-start | bytes 196616 | tf_op jit(solution)/shard_map/ppermute | solution.py:319
  19.8 4.2 %collective-permute-start.1 = (f32[64,256]{1,0:T(8,128)S(1)}, f32[64,256]{1,0:T(8,128)S(1)}, u32[]{:S(2)}, u32[]{:S(2)}) collective-permute-start(f32[64,256]{1,0:T(8,128)S(1)} %get-tuple-element.24), channel_id=1, source_target_pairs={{0,8},{4,12},{8,0},{12,4},{1,9},{5,13},{9,1},{13,5},{2,10},{6,14},... | collective-permute-start | bytes 196616 | tf_op jit(solution)/shard_map/ppermute | solution.py:319
  21.1 6.3 %collective-permute-start.2 = (f32[64,256]{1,0:T(8,128)S(1)}, f32[64,256]{1,0:T(8,128)S(1)}, u32[]{:S(2)}, u32[]{:S(2)}) collective-permute-start(f32[64,256]{1,0:T(8,128)S(1)} %get-tuple-element.25), channel_id=1, source_target_pairs={{0,12},{4,8},{8,4},{12,0},{1,13},{5,9},{9,5},{13,1},{2,14},{6,10},... | collective-permute-start | bytes 196616 | tf_op jit(solution)/shard_map/ppermute | solution.py:319
  21.5 33.8 %copy-start.8 = (s32[264]{0:T(512)}, s32[264]{0:T(512)S(1)}, u32[]{:S(2)}) copy-start(s32[264]{0:T(512)S(1)} %concatenate.3.usage_ref) | copy-start | bytes 3172
  21.5 33.8 %copy-start.10 = (f32[64,256]{1,0:T(8,128)}, f32[64,256]{1,0:T(8,128)S(1)}, u32[]{:S(2)}) copy-start(f32[64,256]{1,0:T(8,128)S(1)} %collective-permute-done.rest_1_) | copy-start | bytes 196612
  24.0 31.4 %copy-start.11 = (f32[64,256]{1,0:T(8,128)}, f32[64,256]{1,0:T(8,128)S(1)}, u32[]{:S(2)}) copy-start(f32[64,256]{1,0:T(8,128)S(1)} %collective-permute-done.1.rest_2_) | copy-start | bytes 196612
  27.4 27.9 %copy-start.12 = (f32[64,256]{1,0:T(8,128)}, f32[64,256]{1,0:T(8,128)S(1)}, u32[]{:S(2)}) copy-start(f32[64,256]{1,0:T(8,128)S(1)} %collective-permute-done.2.rest_3_) | copy-start | bytes 196612
  42.7 0.7 copy-start.4
  58.2 15.6 %copy-start.1 = (f32[16,16,128]{2,1,0:T(8,128)S(1)}, f32[16,16,128]{2,1,0:T(8,128)}, u32[]{:S(2)}) copy-start(f32[16,16,128]{2,1,0:T(8,128)} %all_to_all.15.square_ref) | copy-start | bytes 393220
  58.2 15.6 %copy-start.2 = (bf16[2,256,256]{2,1,0:T(8,128)(2,1)S(1)}, bf16[2,256,256]{2,1,0:T(8,128)(2,1)}, u32[]{:S(2)}) copy-start(bf16[2,256,256]{2,1,0:T(8,128)(2,1)} %constant.19.clone.table_ref) | copy-start | bytes 786436
  58.3 15.5 %copy-start.5 = (bf16[4,64,256]{2,1,0:T(8,128)(2,1)S(1)}, bf16[4,64,256]{2,1,0:T(8,128)(2,1)}, u32[]{:S(2)}) copy-start(bf16[4,64,256]{2,1,0:T(8,128)(2,1)} %copy-done.4) | copy-start | bytes 393220
  58.3 15.5 %copy-start.9 = (s32[264]{0:T(512)S(1)}, s32[264]{0:T(512)}, u32[]{:S(2)}) copy-start(s32[264]{0:T(512)} %copy-done.8) | copy-start | bytes 3172
  58.3 55.6 %all-to-all-start.2 = ((bf16[64,4,16,256]{3,2,1,0:T(8,128)(2,1)}), bf16[64,4,16,256]{3,2,1,0:T(8,128)(2,1)S(1)}, u32[]{:S(2)}, u32[]{:S(2)}) async-start(bf16[64,4,16,256]{3,2,1,0:T(8,128)(2,1)} %shard_map.97), calls=%async_computation.2 | async-start | bytes 4194304 | tf_op jit(solution)/shard_map/all_to_all | solution.py:383
  64.2 2.3 %collective-permute-start.3 = (bf16[64,256]{1,0:T(8,128)(2,1)S(1)}, bf16[64,256]{1,0:T(8,128)(2,1)S(1)}, u32[]{:S(2)}, u32[]{:S(2)}) collective-permute-start(bf16[64,256]{1,0:T(8,128)(2,1)S(1)} %get-tuple-element.36), channel_id=1, source_target_pairs={{0,4},{4,0},{8,12},{12,8},{1,5},{5,1},{9,13},{13,9},{2,6},{6,2},{1... | collective-permute-start | bytes 98312 | tf_op jit(solution)/shard_map/ppermute | solution.py:319
  64.7 6.8 %collective-permute-start.4 = (bf16[64,256]{1,0:T(8,128)(2,1)S(1)}, bf16[64,256]{1,0:T(8,128)(2,1)S(1)}, u32[]{:S(2)}, u32[]{:S(2)}) collective-permute-start(bf16[64,256]{1,0:T(8,128)(2,1)S(1)} %get-tuple-element.37), channel_id=1, source_target_pairs={{0,8},{4,12},{8,0},{12,4},{1,9},{5,13},{9,1},{13,5},{2,10},{6,14},... | collective-permute-start | bytes 98312 | tf_op jit(solution)/shard_map/ppermute | solution.py:319
  66.0 7.8 %collective-permute-start.5 = (bf16[64,256]{1,0:T(8,128)(2,1)S(1)}, bf16[64,256]{1,0:T(8,128)(2,1)S(1)}, u32[]{:S(2)}, u32[]{:S(2)}) collective-permute-start(bf16[64,256]{1,0:T(8,128)(2,1)S(1)} %get-tuple-element.38), channel_id=1, source_target_pairs={{0,12},{4,8},{8,4},{12,0},{1,13},{5,9},{9,5},{13,1},{2,14},{6,10},... | collective-permute-start | bytes 98312 | tf_op jit(solution)/shard_map/ppermute | solution.py:319

commit v2 on v1

--- a/solution.py
+++ b/solution.py
@@ -28,7 +28,11 @@
 CHUNKS = 4
 VMEM_LIMIT = 40 * 1024 * 1024
 STREAM_LIMIT = 56 * 1024 * 1024
-PATH = ("level", "quad")
+PATH = ("z", "half", "quad")
+ROW = ("half", "quad")
+DEPTH = 8
+NEAR = (0, -1, 1, -2, 2)
+FAR = (-3, 3, 4)
 SQUARE_GROUP = ("quad", "shard")
 
 
@@ -231,9 +235,9 @@
     return jnp.minimum(1.0, 0.3 / jnp.sqrt(total / entries + 1e-06))
 
 
-def reply_kernel(usage_ref, avg_ref, square_ref, table_ref, *rest):
+def fresh_kernel(usage_ref, avg_ref, square_ref, table_ref, *rest):
     base_refs = rest[:4]
-    out_any, factor_ref, fresh_ref, reply_ref, sems = rest[4:]
+    fresh_ref, factor_ref = rest[4:]
     factor_ref[...] = clip_factor(square_ref)
     for k in range(QUAD):
         owner = usage_ref[PATHS] ^ k
@@ -245,26 +249,22 @@
             fresh = (base_refs[k][at, :] - change).astype(BF16)
             fresh_ref[pl.ds(pl.multiple_of(module * ROWS, ROWS), ROWS), :] = fresh
 
-    chunks = sems.shape[0]
-    targets = DEVICES // chunks
-
-    def emit(c):
-        at = pl.ds(c * targets, targets)
-        return pltpu.make_async_copy(reply_ref.at[at], out_any.at[at], sems.at[c])
-
-    def chunk(c, carry):
-        for d in range(targets):
-            target = c * targets + d
+
+def pack_kernel(steps, row_ref, *rest):
+    block_refs = rest[: len(steps)]
+    out_any, out_ref, sems = rest[len(steps) :]
+    copies = []
+    for b, step in enumerate(steps):
+        origin = (row_ref[PATHS] + (step + DEPTH)) % DEPTH
+        for target in range(8):
             for p in range(MINE):
-                o = usage_ref[target * MINE + p]
+                o = row_ref[origin * 32 + target * MINE + p]
                 rows = pl.ds(pl.multiple_of(o * ROWS, ROWS), ROWS)
-                reply_ref[target, p] = fresh_ref[rows, :]
-        emit(c).start()
-        return carry
-
-    lax.fori_loop(0, chunks, chunk, 0)
-    for c in range(chunks):
-        emit(c).wait()
+                out_ref[target, b, p] = block_refs[b][rows, :]
+        copies.append(pltpu.make_async_copy(out_ref.at[:, b], out_any.at[:, b], sems.at[b]))
+        copies[-1].start()
+    for copy in copies:
+        copy.wait()
 
 
 def owner_kernel(usage_ref, avg_ref, square_ref, table_ref, params_ref, momentum_ref, *rest):
@@ -285,17 +285,20 @@
             new_params_ref[i, :, at] = new.astype(BF16)
 
 
-def place_kernel(got_ref, out_ref, sems):
+def place_kernel(steps, row_ref, got_ref, *rest):
+    out_ref, sems = rest[-2:]
     copies = []
-    for q in range(QUAD):
-        for p in range(MINE):
-            copies.append(
-                pltpu.make_async_copy(
-                    got_ref.at[:, q, p],
-                    out_ref.at[p, :, :, pl.ds(q * COLS, COLS)],
-                    sems.at[q * MINE + p],
+    for b, step in enumerate(steps):
+        origin = (row_ref[PATHS] + (step + DEPTH)) % DEPTH
+        for half in range(2):
+            for q in range(QUAD):
+                copies.append(
+                    pltpu.make_async_copy(
+                        got_ref.at[half * QUAD + q, b],
+                        out_ref.at[:, origin * 2 + half, :, pl.ds(q * COLS, COLS)],
+                        sems.at[len(copies)],
+                    )
                 )
-            )
     for copy in copies:
         copy.start()
     for copy in copies:
@@ -319,13 +322,45 @@
     return lax.ppermute(values, "quad", [(i, i ^ k) for i in range(QUAD)])
 
 
+def along(values, k):
+    return lax.ppermute(values, "z", [(i, (i + k) % DEPTH) for i in range(DEPTH)])
+
+
+def pack_row(steps, row, blocks):
+    shape = (8, len(steps), MINE, ROWS, COLS)
+    return call(
+        functools.partial(pack_kernel, steps),
+        shaped(shape, BF16),
+        in_specs=[pl.BlockSpec(memory_space=pltpu.SMEM)]
+        + [pl.BlockSpec(memory_space=pltpu.VMEM)] * len(steps),
+        out_specs=pl.BlockSpec(memory_space=pltpu.HBM),
+        scratch_shapes=[pltpu.VMEM(shape, BF16), pltpu.SemaphoreType.DMA((len(steps),))],
+    )(row, *blocks)
+
+
+def place_row(steps, row, got, rest):
+    anywhere = pl.BlockSpec(memory_space=pl.ANY)
+    return call(
+        functools.partial(place_kernel, steps),
+        shaped((MINE, LEVELS, ROWS, WIDTH), BF16),
+        in_specs=[pl.BlockSpec(memory_space=pltpu.SMEM)] + [anywhere] * (1 + len(rest)),
+        out_specs=anywhere,
+        scratch_shapes=[pltpu.SemaphoreType.DMA((8 * len(steps),))],
+        input_output_aliases={2: 0} if rest else {},
+    )(row, got, *rest)
+
+
 def local(pseudo_grad, kept_index, usage, module_params, momentum):
     forward, inverse = dct_tables()
     smem = pl.BlockSpec(memory_space=pltpu.SMEM)
     vmem = pl.BlockSpec(memory_space=pltpu.VMEM)
-    level, q = lax.axis_index("level"), lax.axis_index("quad")
+    z, half, q = lax.axis_index("z"), lax.axis_index("half"), lax.axis_index("quad")
+    level = 2 * z + half
     used = lax.dynamic_slice_in_dim(usage, level, 1, 1).reshape(PATHS)
     used = jnp.concatenate([used, jnp.full((8,), q, jnp.int32)])
+    row = lax.dynamic_slice_in_dim(usage, 32 * z, 32, 0).reshape(32, DEPTH, 2)
+    row = lax.dynamic_index_in_dim(row, half, 2, keepdims=False).T.reshape(PATHS)
+    row = jnp.concatenate([row, jnp.full((8,), z, jnp.int32)])
 
     bases = call(
         base_kernel,
@@ -353,7 +388,7 @@
         limit=STREAM_LIMIT,
     )(pseudo_grad, kept_index, forward)
     got = lax.all_to_all(outgoing.reshape(DEVICES, SENT, 128), PATH, 0, 0, tiled=True)
-    got, bases = lax.optimization_barrier((got, bases))
+    got, bases, row = lax.optimization_barrier((got, bases, row))
 
     average, squares, *pieces = call(
         sum_kernel,
@@ -366,24 +401,27 @@
         + [pltpu.SMEM((OPTIONS,), jnp.int32)],
     )(used, got)
     squares = lax.all_to_all(squares, SQUARE_GROUP, 0, 0, tiled=True)
-
-    replies = call(
-        reply_kernel,
-        shaped((DEVICES, MINE, ROWS, COLS), BF16),
+    pieces = [swap(piece, k + 1) for k, piece in enumerate(pieces)]
+    squares, pieces = lax.optimization_barrier((squares, pieces))
+
+    fresh = call(
+        fresh_kernel,
+        shaped((OPTIONS * ROWS, COLS), BF16),
         in_specs=[smem] + [vmem] * 7,
-        out_specs=anywhere,
-        scratch_shapes=[
-            pltpu.VMEM((OPTIONS, 128), F32),
-            pltpu.VMEM((OPTIONS * ROWS, COLS), BF16),
-            pltpu.VMEM((DEVICES, MINE, ROWS, COLS), BF16),
-            pltpu.SemaphoreType.DMA((CHUNKS,)),
-        ],
-        limit=STREAM_LIMIT,
+        out_specs=vmem,
+        scratch_shapes=[pltpu.VMEM((OPTIONS, 128), F32)],
     )(used, average, squares, inverse, *bases)
-    returned = lax.all_to_all(replies, PATH, 0, 0, tiled=True)
-
-    pieces, replies = lax.optimization_barrier((pieces, replies))
-    pieces = [swap(piece, k + 1) for k, piece in enumerate(pieces)]
+    before, after = [fresh], [fresh]
+    for _ in range(2):
+        before.append(along(before[-1], 1))
+        after.append(along(after[-1], -1))
+    packed = pack_row(NEAR, row, [fresh, before[1], after[1], before[2], after[2]])
+    packed, before2, after2 = lax.optimization_barrier((packed, before[2], after[2]))
+    near = lax.all_to_all(packed, ROW, 0, 0, tiled=True)
+    before3, after3 = along(before2, 1), along(after2, -1)
+    packed = pack_row(FAR, row, [before3, after3, along(before3, 1)])
+    packed, near, pieces = lax.optimization_barrier((packed, near, pieces))
+    far = lax.all_to_all(packed, ROW, 0, 0, tiled=True)
 
     new_params, new_momentum = call(
         owner_kernel,
@@ -393,18 +431,13 @@
         scratch_shapes=[pltpu.VMEM((OPTIONS, 128), F32)],
     )(used, average, squares, inverse, module_params, momentum, *pieces)
 
-    path_params = call(
-        place_kernel,
-        shaped((MINE, LEVELS, ROWS, WIDTH), BF16),
-        in_specs=[anywhere],
-        out_specs=anywhere,
-        scratch_shapes=[pltpu.SemaphoreType.DMA((QUAD * MINE,))],
-    )(returned.reshape(LEVELS, QUAD, MINE, ROWS, COLS))
+    path_params = place_row(NEAR, row, near, [])
+    path_params = place_row(FAR, row, far, [path_params])
     return (new_params, new_momentum, path_params)
 
 
 def solution(mesh):
-    mesh = Mesh(mesh.devices.reshape(LEVELS, QUAD, 4), PATH + ("shard",))
+    mesh = Mesh(mesh.devices.reshape(DEPTH, 2, QUAD, 4), PATH + ("shard",))
     return jax.shard_map(
         local,
         mesh=mesh,

time: 116 us -> 112 us (0.966)
  starting transfers between devices: 23.3 us -> 42.5 us
  waiting for transfers between devices: 63.2 us -> 49.7 us
  blocking collectives: 12 us -> 0 us
  Pallas kernels: 14.6 us -> 18.6 us
    all_to_all x1 -> x3, waiting for transfers between devices: 38.4 us -> 13.4 us  [the longest x1 8.72 us: local(): far = lax.all_to_all(packed, ROW, 0, 0, tiled=True)]
    ppermute x0 -> x7, waiting for transfers between devices: none -> 15.1 us  [along(): lax.ppermute(values, 'z', [(i, (i + k) % DEPTH) for i in range(DEPTH)])]
    all_to_all x1 -> x0, blocking collectives: 12 us -> none  [local(): squares = lax.all_to_all(squares, SQUARE_GROUP, 0, 0, tiled=True)]
    all_to_all x1 -> x3, starting transfers between devices: 5.88 us -> 16.6 us  [the longest x1 6.33 us: local(): near = lax.all_to_all(packed, ROW, 0, 0, tiled=True)]
    ppermute x0 -> x7, starting transfers between devices: none -> 8.39 us  [along(): lax.ppermute(values, 'z', [(i, (i + k) % DEPTH) for i in range(DEPTH)])]
    ppermute x6, waiting for transfers between devices: 13.3 us -> 9.03 us  [swap(): return lax.ppermute(values, 'quad', [(i, i ^ k) for i in range(QUAD)])]
    pallas_call x2 -> x5, Pallas kernels: 4.32 us -> 7.65 us  [the longest x2 3.58 us: place_row(): call(functools.partial(place_kernel, steps), shaped((MINE, LEVELS, ROWS,...]
    unnamed x26 -> x8, local copies, waits for them, and re-layouts: 1.34 us -> 0.02 us
  transfers between devices with their start and end apart: 8 -> 17, of which waited for: 6 -> 12; matrix products, arithmetic and copies ran while one was open for 0% -> 0% of each run, Pallas kernels for 1% -> 5%
where the time goes in v2:
time: 112 us
  waiting for transfers between devices  49.7 us (44%)
  starting transfers between devices  42.5 us (38%)
  Pallas kernels  18.6 us (17%)
    ppermute x7, waiting for transfers between devices, along(): lax.ppermute(values, 'z', [(i, (i + k) % DEPTH) for i in range(DEPTH)])  15.1 us
    all_to_all x1, starting transfers between devices, local(): lax.all_to_all(outgoing.reshape(DEVICES, SENT, 128), PATH, 0, 0, tiled=True)  13.1 us
    all_to_all x1, waiting for transfers between devices, local(): lax.all_to_all(outgoing.reshape(DEVICES, SENT, 128), PATH, 0, 0, tiled=True)  12.3 us
    ppermute x6, waiting for transfers between devices, swap(): return lax.ppermute(values, 'quad', [(i, i ^ k) for i in range(QUAD)])  9.03 us
    all_to_all x1, waiting for transfers between devices, local(): far = lax.all_to_all(packed, ROW, 0, 0, tiled=True)  8.72 us
    ppermute x7, starting transfers between devices, along(): lax.ppermute(values, 'z', [(i, (i + k) % DEPTH) for i in range(DEPTH)])  8.39 us
    all_to_all x1, starting transfers between devices, local(): near = lax.all_to_all(packed, ROW, 0, 0, tiled=True)  6.33 us
    all_to_all x1, starting transfers between devices, local(): squares = lax.all_to_all(squares, SQUARE_GROUP, 0, 0, tiled=True)  5.94 us
  transfers between devices with their start and end apart: 17, of which 12 were waited for; matrix products, arithmetic and copies ran while one was open for 0% of the time, Pallas kernels for 5%

profile of v2, /device:TPU:1, one launch (start us, length us, event | category | flops | bytes accessed | tf_op | source)
XLA Modules:
  0.0 112.0 jit_solution(13450182927075771730)
XLA Ops:
  0.6 0.0 copy-start
  0.6 0.0 copy-start.3
  0.7 0.0 copy-start.2
  0.7 5.0 %shard_map.94 = bf16[16,4,40,128]{3,2,1,0:T(8,128)(2,1)} custom-call(bf16[4,16,16,1024]{3,2,1,0:T(8,128)(2,1)} %grad_any.1, s32[4,16,16,16]{3,2,1,0:T(8,128)} %kept_any.1, bf16[2,256,256]{2,1,0:T(8,128)(2,1)} %constant.35.clone.table_any), custom_call_target="tpu_custom_call" | custom-call | tf_op jit(solution)/shard_map/pallas_call | solution.py:374
  5.6 0.0 copy-start.1
  5.6 13.1 %all-to-all-start = ((bf16[64,40,128]{2,1,0:T(8,128)(2,1)}), bf16[64,40,128]{2,1,0:T(8,128)(2,1)S(1)}, u32[]{:S(2)}, u32[]{:S(2)}) async-start(bf16[64,40,128]{2,1,0:T(8,128)(2,1)} %bitcast.7), calls=%async_computation | async-start | bytes 1310720 | tf_op jit(solution)/shard_map/all_to_all | solution.py:390
  18.9 0.5 collective-permute-start
  19.4 1.3 %collective-permute-start.1 = (f32[64,256]{1,0:T(8,128)S(1)}, f32[64,256]{1,0:T(8,128)S(1)}, u32[]{:S(2)}, u32[]{:S(2)}) collective-permute-start(f32[64,256]{1,0:T(8,128)S(1)} %get-tuple-element.34), channel_id=1, source_target_pairs={{0,8},{4,12},{8,0},{12,4},{1,9},{5,13},{9,1},{13,5},{2,10},{6,14},... | collective-permute-start | bytes 196616 | tf_op jit(solution)/shard_map/ppermute | solution.py:322
  20.7 0.4 collective-permute-start.2
  21.1 0.1 constant_dynamic-slice_fusion.1
  21.2 0.1 reshape.21
  21.3 0.0 collective-permute-done.rest_1_
  21.3 2.4 %collective-permute-done.1.rest_2_ = f32[64,256]{1,0:T(8,128)S(1)} collective-permute-done((f32[64,256]{1,0:T(8,128)S(1)}, f32[64,256]{1,0:T(8,128)S(1)}, u32[]{:S(2)}, u32[]{:S(2)}) %collective-permute-start.1) | collective-permute-done | bytes 65568 | tf_op jit(solution)/shard_map/ppermute | solution.py:322
  23.8 3.1 %collective-permute-done.2.rest_3_ = f32[64,256]{1,0:T(8,128)S(1)} collective-permute-done((f32[64,256]{1,0:T(8,128)S(1)}, f32[64,256]{1,0:T(8,128)S(1)}, u32[]{:S(2)}, u32[]{:S(2)}) %collective-permute-start.2) | collective-permute-done | bytes 65568 | tf_op jit(solution)/shard_map/ppermute | solution.py:322
  26.9 12.3 %all-to-all-done.got_ref = bf16[64,40,128]{2,1,0:T(8,128)(2,1)S(1)} async-done(((bf16[64,40,128]{2,1,0:T(8,128)(2,1)}), bf16[64,40,128]{2,1,0:T(8,128)(2,1)S(1)}, u32[]{:S(2)}, u32[]{:S(2)}) %all-to-all-start) | async-done | bytes 655392 | tf_op jit(solution)/shard_map/all_to_all | solution.py:390
  39.1 4.3 %shard_map.96 = (bf16[4,64,256]{2,1,0:T(8,128)(2,1)S(1)}, f32[16,16,128]{2,1,0:T(8,128)}, bf16[64,256]{1,0:T(8,128)(2,1)S(1)}, bf16[64,256]{1,0:T(8,128)(2,1)S(1)}, bf16[64,256]{1,0:T(8,128)(2,1)S(1)}) custom-call(s32[264]{0:T(512)S(1)} %concatenate.6.usage_ref, bf16[64,40,128]{2,1,0:T(8,128)(2,1)S(1)} %all-to-all-done.got_ref), custom_call_target="tpu_custom_call" | custom-call | tf_op jit(solution)/shard_map/pallas_call | solution.py:393
  43.5 5.9 %all-to-all-start.1 = ((f32[16,16,128]{2,1,0:T(8,128)}), f32[16,16,128]{2,1,0:T(8,128)S(1)}, u32[]{:S(2)}, u32[]{:S(2)}) async-start(f32[16,16,128]{2,1,0:T(8,128)} %get-tuple-element.38), calls=%async_computation.1 | async-start | bytes 262144 | tf_op jit(solution)/shard_map/all_to_all | solution.py:403
  49.4 0.2 collective-permute-start.3
  49.6 1.6 %collective-permute-start.4 = (bf16[64,256]{1,0:T(8,128)(2,1)S(1)}, bf16[64,256]{1,0:T(8,128)(2,1)S(1)}, u32[]{:S(2)}, u32[]{:S(2)}) collective-permute-start(bf16[64,256]{1,0:T(8,128)(2,1)S(1)} %get-tuple-element.40), channel_id=1, source_target_pairs={{0,8},{4,12},{8,0},{12,4},{1,9},{5,13},{9,1},{13,5},{2,10},{6,14},... | collective-permute-start | bytes 98312 | tf_op jit(solution)/shard_map/ppermute | solution.py:322
  51.2 0.4 collective-permute-start.5
  51.5 0.0 collective-permute-done.3.rest_0_
  51.5 2.3 %collective-permute-done.4.rest_1_ = bf16[64,256]{1,0:T(8,128)(2,1)S(1)} collective-permute-done((bf16[64,256]{1,0:T(8,128)(2,1)S(1)}, bf16[64,256]{1,0:T(8,128)(2,1)S(1)}, u32[]{:S(2)}, u32[]{:S(2)}) %collective-permute-start.4) | collective-permute-done | bytes 32800 | tf_op jit(solution)/shard_map/ppermute | solution.py:322
  53.9 1.2 %collective-permute-done.5.rest_2_ = bf16[64,256]{1,0:T(8,128)(2,1)S(1)} collective-permute-done((bf16[64,256]{1,0:T(8,128)(2,1)S(1)}, bf16[64,256]{1,0:T(8,128)(2,1)S(1)}, u32[]{:S(2)}, u32[]{:S(2)}) %collective-permute-start.5) | collective-permute-done | bytes 32800 | tf_op jit(solution)/shard_map/ppermute | solution.py:322
  55.0 0.7 all-to-all-done.1.square_ref
  55.7 0.9 shard_map.97.rest_0_
  56.6 0.4 collective-permute-start.6
  57.0 2.3 %collective-permute-start.7 = (bf16[256,256]{1,0:T(8,128)(2,1)S(1)}, bf16[256,256]{1,0:T(8,128)(2,1)S(1)}, u32[]{:S(2)}, u32[]{:S(2)}) collective-permute-start(bf16[256,256]{1,0:T(8,128)(2,1)S(1)} %shard_map.97.rest_0_), channel_id=1, source_target_pairs={{0,224},{32,0},{64,32},{96,64},{128,96},{160,128},{192,160},{224,1... | collective-permute-start | bytes 393224 | tf_op jit(solution)/shard_map/ppermute | solution.py:326
  59.3 3.2 %collective-permute-done.6.rest_1_ = bf16[256,256]{1,0:T(8,128)(2,1)S(1)} collective-permute-done((bf16[256,256]{1,0:T(8,128)(2,1)S(1)}, bf16[256,256]{1,0:T(8,128)(2,1)S(1)}, u32[]{:S(2)}, u32[]{:S(2)}) %collective-permute-start.6) | collective-permute-done | bytes 131104 | tf_op jit(solution)/shard_map/ppermute | solution.py:326
  62.6 0.0 collective-permute-start.8
  62.6 0.0 collective-permute-done.7.rest_2_
  62.6 2.7 %collective-permute-start.9 = (bf16[256,256]{1,0:T(8,128)(2,1)S(1)}, bf16[256,256]{1,0:T(8,128)(2,1)S(1)}, u32[]{:S(2)}, u32[]{:S(2)}) collective-permute-start(bf16[256,256]{1,0:T(8,128)(2,1)S(1)} %collective-permute-done.7.rest_2_), channel_id=1, source_target_pairs={{0,224},{32,0},{64,32},{96,64},{128,96},{160,128},{192,160},{224,1... | collective-permute-start | bytes 393224 | tf_op jit(solution)/shard_map/ppermute | solution.py:326
  65.3 2.3 %collective-permute-done.8.rest_3_ = bf16[256,256]{1,0:T(8,128)(2,1)S(1)} collective-permute-done((bf16[256,256]{1,0:T(8,128)(2,1)S(1)}, bf16[256,256]{1,0:T(8,128)(2,1)S(1)}, u32[]{:S(2)}, u32[]{:S(2)}) %collective-permute-start.8) | collective-permute-done | bytes 131104 | tf_op jit(solution)/shard_map/ppermute | solution.py:326
  67.6 0.0 collective-permute-done.9.rest_4_
  67.6 1.7 %shard_map.98 = bf16[8,5,4,16,256]{4,3,2,1,0:T(8,128)(2,1)} custom-call(s32[264]{0:T(512)S(1)} %concatenate.7.row_ref, bf16[256,256]{1,0:T(8,128)(2,1)S(1)} %shard_map.97.rest_0_, bf16[256,256]{1,0:T(8,128)(2,1)S(1)} %collective-permute-done.6.rest_1_, bf16[256,256]{1,0:T(8,128)(2,1)S(1)} %collective-permute-done.7.rest_2_, ...), custom_call_target="tpu_custom_call" | custom-call | tf_op jit(solution)/shard_map/pallas_call | solution.py:331
  69.3 6.3 %all-to-all-start.2 = ((bf16[8,5,4,16,256]{4,3,2,1,0:T(8,128)(2,1)}), bf16[8,5,4,16,256]{4,3,2,1,0:T(8,128)(2,1)S(1)}, u32[]{:S(2)}, u32[]{:S(2)}) async-start(bf16[8,5,4,16,256]{4,3,2,1,0:T(8,128)(2,1)} %shard_map.98), calls=%async_computation.2 | async-start | bytes 2621440 | tf_op jit(solution)/shard_map/all_to_all | solution.py:420
  75.7 0.0 collective-permute-start.10
  75.7 3.0 %collective-permute-start.11 = (bf16[256,256]{1,0:T(8,128)(2,1)S(1)}, bf16[256,256]{1,0:T(8,128)(2,1)S(1)}, u32[]{:S(2)}, u32[]{:S(2)}) collective-permute-start(bf16[256,256]{1,0:T(8,128)(2,1)S(1)} %collective-permute-done.9.rest_4_), channel_id=1, source_target_pairs={{0,224},{32,0},{64,32},{96,64},{128,96},{160,128},{192,160},{224,1... | collective-permute-start | bytes 393224 | tf_op jit(solution)/shard_map/ppermute | solution.py:326
  78.6 3.8 %collective-permute-done.10.rest_0_ = bf16[256,256]{1,0:T(8,128)(2,1)S(1)} collective-permute-done((bf16[256,256]{1,0:T(8,128)(2,1)S(1)}, bf16[256,256]{1,0:T(8,128)(2,1)S(1)}, u32[]{:S(2)}, u32[]{:S(2)}) %collective-permute-start.10) | collective-permute-done | bytes 131104 | tf_op jit(solution)/shard_map/ppermute | solution.py:326
  82.4 0.0 collective-permute-start.12
  82.4 0.0 collective-permute-done.11.rest_1_
  82.4 5.6 %collective-permute-done.12.rest_2_ = bf16[256,256]{1,0:T(8,128)(2,1)S(1)} collective-permute-done((bf16[256,256]{1,0:T(8,128)(2,1)S(1)}, bf16[256,256]{1,0:T(8,128)(2,1)S(1)}, u32[]{:S(2)}, u32[]{:S(2)}) %collective-permute-start.12) | collective-permute-done | bytes 131104 | tf_op jit(solution)/shard_map/ppermute | solution.py:326
  88.1 1.5 %shard_map.99 = bf16[8,3,4,16,256]{4,3,2,1,0:T(8,128)(2,1)} custom-call(s32[264]{0:T(512)S(1)} %concatenate.7.row_ref, bf16[256,256]{1,0:T(8,128)(2,1)S(1)} %collective-permute-done.10.rest_0_, bf16[256,256]{1,0:T(8,128)(2,1)S(1)} %collective-permute-done.11.rest_1_, bf16[256,256]{1,0:T(8,128)(2,1)S(1)} %collective-permute-done.12.rest_2_), custom_call_target="tpu_custom_call" | custom-call | tf_op jit(solution)/shard_map/pallas_call | solution.py:331
  89.6 4.0 %all-to-all-done.2.got_ref = bf16[8,5,4,16,256]{4,3,2,1,0:T(8,128)(2,1)S(1)} async-done(((bf16[8,5,4,16,256]{4,3,2,1,0:T(8,128)(2,1)}), bf16[8,5,4,16,256]{4,3,2,1,0:T(8,128)(2,1)S(1)}, u32[]{:S(2)}, u32[]{:S(2)}) %all-to-all-start.2) | async-done | bytes 1310752 | tf_op jit(solution)/shard_map/all_to_all | solution.py:420
  93.6 4.3 %all-to-all-start.3 = ((bf16[8,3,4,16,256]{4,3,2,1,0:T(8,128)(2,1)}), bf16[8,3,4,16,256]{4,3,2,1,0:T(8,128)(2,1)S(1)}, u32[]{:S(2)}, u32[]{:S(2)}) async-start(bf16[8,3,4,16,256]{4,3,2,1,0:T(8,128)(2,1)} %shard_map.99), calls=%async_computation.3 | async-start | bytes 1572864 | tf_op jit(solution)/shard_map/all_to_all | solution.py:424
  97.9 1.9 %shard_map.101.rest_0_ = bf16[4,16,16,1024]{3,2,1,0:T(8,128)(2,1)} custom-call(s32[264]{0:T(512)S(1)} %concatenate.7.row_ref, bf16[8,5,4,16,256]{4,3,2,1,0:T(8,128)(2,1)S(1)} %all-to-all-done.2.got_ref), custom_call_target="tpu_custom_call" | custom-call | tf_op jit(solution)/shard_map/pallas_call | solution.py:343
  99.8 1.6 %shard_map.100 = (bf16[4,16,1024]{2,1,0:T(8,128)(2,1)}, f32[4,16,1024]{2,1,0:T(8,128)}) custom-call(s32[264]{0:T(512)S(1)} %concatenate.6.usage_ref, bf16[4,64,256]{2,1,0:T(8,128)(2,1)S(1)} %get-tuple-element.37.avg_ref, f32[16,16,128]{2,1,0:T(8,128)S(1)} %all-to-all-done.1.square_ref, bf16[2,256,256]{2,1,0:T(8,128)(2,1)S(1)} %copy-done.1, ...), custom_call_target="tpu_custom_call" | custom-call | tf_op jit(solution)/shard_map/pallas_call | solution.py:426
  101.5 8.7 %all-to-all-done.3.got_ref = bf16[8,3,4,16,256]{4,3,2,1,0:T(8,128)(2,1)S(1)} async-done(((bf16[8,3,4,16,256]{4,3,2,1,0:T(8,128)(2,1)}), bf16[8,3,4,16,256]{4,3,2,1,0:T(8,128)(2,1)S(1)}, u32[]{:S(2)}, u32[]{:S(2)}) %all-to-all-start.3) | async-done | bytes 786464 | tf_op jit(solution)/shard_map/all_to_all | solution.py:424
  110.2 1.6 %shard_map.102 = bf16[4,16,16,1024]{3,2,1,0:T(8,128)(2,1)} custom-call(s32[264]{0:T(512)S(1)} %concatenate.7.row_ref, bf16[8,3,4,16,256]{4,3,2,1,0:T(8,128)(2,1)S(1)} %all-to-all-done.3.got_ref, bf16[4,16,16,1024]{3,2,1,0:T(8,128)(2,1)} %shard_map.101.rest_0_), custom_call_target="tpu_custom_call", output_to_operand_aliasing={{}: (2, {})} | custom-call | tf_op jit(solution)/shard_map/pallas_call | solution.py:343
  (9 shorter events, 0.1 us)
Async XLA Ops:
  0.6 20.5 %copy-start = (s32[256,16]{0,1:T(8,128)S(1)}, s32[256,16]{0,1:T(8,128)}, u32[]{:S(2)}) copy-start(s32[256,16]{0,1:T(8,128)} %param.9) | copy-start | bytes 49156
  0.6 18.1 %copy-start.3 = (bf16[4,16,1024]{2,1,0:T(8,128)(2,1)S(1)}, bf16[4,16,1024]{2,1,0:T(8,128)(2,1)}, u32[]{:S(2)}) copy-start(bf16[4,16,1024]{2,1,0:T(8,128)(2,1)} %params_ref.3) | copy-start | bytes 393220
  0.7 18.1 %copy-start.2 = (f32[4,16,1024]{2,1,0:T(8,128)S(1)}, f32[4,16,1024]{2,1,0:T(8,128)}, u32[]{:S(2)}) copy-start(f32[4,16,1024]{2,1,0:T(8,128)} %momentum_ref.3) | copy-start | bytes 786436
  5.6 50.1 %copy-start.1 = (bf16[2,256,256]{2,1,0:T(8,128)(2,1)S(1)}, bf16[2,256,256]{2,1,0:T(8,128)(2,1)}, u32[]{:S(2)}) copy-start(bf16[2,256,256]{2,1,0:T(8,128)(2,1)} %constant.36.clone.table_ref) | copy-start | bytes 786436
  5.6 33.5 %all-to-all-start = ((bf16[64,40,128]{2,1,0:T(8,128)(2,1)}), bf16[64,40,128]{2,1,0:T(8,128)(2,1)S(1)}, u32[]{:S(2)}, u32[]{:S(2)}) async-start(bf16[64,40,128]{2,1,0:T(8,128)(2,1)} %bitcast.7), calls=%async_computation | async-start | bytes 1310720 | tf_op jit(solution)/shard_map/all_to_all | solution.py:390
  18.9 2.5 %collective-permute-start = (f32[64,256]{1,0:T(8,128)S(1)}, f32[64,256]{1,0:T(8,128)S(1)}, u32[]{:S(2)}, u32[]{:S(2)}) collective-permute-start(f32[64,256]{1,0:T(8,128)S(1)} %get-tuple-element.33), channel_id=1, source_target_pairs={{0,4},{4,0},{8,12},{12,8},{1,5},{5,1},{9,13},{13,9},{2,6},{6,2},{1... | collective-permute-start | bytes 196616 | tf_op jit(solution)/shard_map/ppermute | solution.py:322
  19.4 4.4 %collective-permute-start.1 = (f32[64,256]{1,0:T(8,128)S(1)}, f32[64,256]{1,0:T(8,128)S(1)}, u32[]{:S(2)}, u32[]{:S(2)}) collective-permute-start(f32[64,256]{1,0:T(8,128)S(1)} %get-tuple-element.34), channel_id=1, source_target_pairs={{0,8},{4,12},{8,0},{12,4},{1,9},{5,13},{9,1},{13,5},{2,10},{6,14},... | collective-permute-start | bytes 196616 | tf_op jit(solution)/shard_map/ppermute | solution.py:322
  20.7 6.2 %collective-permute-start.2 = (f32[64,256]{1,0:T(8,128)S(1)}, f32[64,256]{1,0:T(8,128)S(1)}, u32[]{:S(2)}, u32[]{:S(2)}) collective-permute-start(f32[64,256]{1,0:T(8,128)S(1)} %get-tuple-element.35), channel_id=1, source_target_pairs={{0,12},{4,8},{8,4},{12,0},{1,13},{5,9},{9,5},{13,1},{2,14},{6,10},... | collective-permute-start | bytes 196616 | tf_op jit(solution)/shard_map/ppermute | solution.py:322
  43.5 12.3 %all-to-all-start.1 = ((f32[16,16,128]{2,1,0:T(8,128)}), f32[16,16,128]{2,1,0:T(8,128)S(1)}, u32[]{:S(2)}, u32[]{:S(2)}) async-start(f32[16,16,128]{2,1,0:T(8,128)} %get-tuple-element.38), calls=%async_computation.1 | async-start | bytes 262144 | tf_op jit(solution)/shard_map/all_to_all | solution.py:403
  49.4 2.1 %collective-permute-start.3 = (bf16[64,256]{1,0:T(8,128)(2,1)S(1)}, bf16[64,256]{1,0:T(8,128)(2,1)S(1)}, u32[]{:S(2)}, u32[]{:S(2)}) collective-permute-start(bf16[64,256]{1,0:T(8,128)(2,1)S(1)} %get-tuple-element.39), channel_id=1, source_target_pairs={{0,4},{4,0},{8,12},{12,8},{1,5},{5,1},{9,13},{13,9},{2,6},{6,2},{1... | collective-permute-start | bytes 98312 | tf_op jit(solution)/shard_map/ppermute | solution.py:322
  49.6 4.3 %collective-permute-start.4 = (bf16[64,256]{1,0:T(8,128)(2,1)S(1)}, bf16[64,256]{1,0:T(8,128)(2,1)S(1)}, u32[]{:S(2)}, u32[]{:S(2)}) collective-permute-start(bf16[64,256]{1,0:T(8,128)(2,1)S(1)} %get-tuple-element.40), channel_id=1, source_target_pairs={{0,8},{4,12},{8,0},{12,4},{1,9},{5,13},{9,1},{13,5},{2,10},{6,14},... | collective-permute-start | bytes 98312 | tf_op jit(solution)/shard_map/ppermute | solution.py:322
  51.2 3.9 %collective-permute-start.5 = (bf16[64,256]{1,0:T(8,128)(2,1)S(1)}, bf16[64,256]{1,0:T(8,128)(2,1)S(1)}, u32[]{:S(2)}, u32[]{:S(2)}) collective-permute-start(bf16[64,256]{1,0:T(8,128)(2,1)S(1)} %get-tuple-element.41), channel_id=1, source_target_pairs={{0,12},{4,8},{8,4},{12,0},{1,13},{5,9},{9,5},{13,1},{2,14},{6,10},... | collective-permute-start | bytes 98312 | tf_op jit(solution)/shard_map/ppermute | solution.py:322
  56.6 6.0 %collective-permute-start.6 = (bf16[256,256]{1,0:T(8,128)(2,1)S(1)}, bf16[256,256]{1,0:T(8,128)(2,1)S(1)}, u32[]{:S(2)}, u32[]{:S(2)}) collective-permute-start(bf16[256,256]{1,0:T(8,128)(2,1)S(1)} %shard_map.97.rest_0_), channel_id=1, source_target_pairs={{0,32},{32,64},{64,96},{96,128},{128,160},{160,192},{192,224},{224... | collective-permute-start | bytes 393224 | tf_op jit(solution)/shard_map/ppermute | solution.py:326
  57.0 5.6 %collective-permute-start.7 = (bf16[256,256]{1,0:T(8,128)(2,1)S(1)}, bf16[256,256]{1,0:T(8,128)(2,1)S(1)}, u32[]{:S(2)}, u32[]{:S(2)}) collective-permute-start(bf16[256,256]{1,0:T(8,128)(2,1)S(1)} %shard_map.97.rest_0_), channel_id=1, source_target_pairs={{0,224},{32,0},{64,32},{96,64},{128,96},{160,128},{192,160},{224,1... | collective-permute-start | bytes 393224 | tf_op jit(solution)/shard_map/ppermute | solution.py:326
  62.6 5.0 %collective-permute-start.8 = (bf16[256,256]{1,0:T(8,128)(2,1)S(1)}, bf16[256,256]{1,0:T(8,128)(2,1)S(1)}, u32[]{:S(2)}, u32[]{:S(2)}) collective-permute-start(bf16[256,256]{1,0:T(8,128)(2,1)S(1)} %collective-permute-done.6.rest_1_), channel_id=1, source_target_pairs={{0,32},{32,64},{64,96},{96,128},{128,160},{160,192},{192,224},{224... | collective-permute-start | bytes 393224 | tf_op jit(solution)/shard_map/ppermute | solution.py:326
  62.6 5.0 %collective-permute-start.9 = (bf16[256,256]{1,0:T(8,128)(2,1)S(1)}, bf16[256,256]{1,0:T(8,128)(2,1)S(1)}, u32[]{:S(2)}, u32[]{:S(2)}) collective-permute-start(bf16[256,256]{1,0:T(8,128)(2,1)S(1)} %collective-permute-done.7.rest_2_), channel_id=1, source_target_pairs={{0,224},{32,0},{64,32},{96,64},{128,96},{160,128},{192,160},{224,1... | collective-permute-start | bytes 393224 | tf_op jit(solution)/shard_map/ppermute | solution.py:326
  69.3 24.2 %all-to-all-start.2 = ((bf16[8,5,4,16,256]{4,3,2,1,0:T(8,128)(2,1)}), bf16[8,5,4,16,256]{4,3,2,1,0:T(8,128)(2,1)S(1)}, u32[]{:S(2)}, u32[]{:S(2)}) async-start(bf16[8,5,4,16,256]{4,3,2,1,0:T(8,128)(2,1)} %shard_map.98), calls=%async_computation.2 | async-start | bytes 2621440 | tf_op jit(solution)/shard_map/all_to_all | solution.py:420
  75.7 6.8 %collective-permute-start.10 = (bf16[256,256]{1,0:T(8,128)(2,1)S(1)}, bf16[256,256]{1,0:T(8,128)(2,1)S(1)}, u32[]{:S(2)}, u32[]{:S(2)}) collective-permute-start(bf16[256,256]{1,0:T(8,128)(2,1)S(1)} %collective-permute-done.8.rest_3_), channel_id=1, source_target_pairs={{0,32},{32,64},{64,96},{96,128},{128,160},{160,192},{192,224},{224... | collective-permute-start | bytes 393224 | tf_op jit(solution)/shard_map/ppermute | solution.py:326
  75.7 6.8 %collective-permute-start.11 = (bf16[256,256]{1,0:T(8,128)(2,1)S(1)}, bf16[256,256]{1,0:T(8,128)(2,1)S(1)}, u32[]{:S(2)}, u32[]{:S(2)}) collective-permute-start(bf16[256,256]{1,0:T(8,128)(2,1)S(1)} %collective-permute-done.9.rest_4_), channel_id=1, source_target_pairs={{0,224},{32,0},{64,32},{96,64},{128,96},{160,128},{192,160},{224,1... | collective-permute-start | bytes 393224 | tf_op jit(solution)/shard_map/ppermute | solution.py:326
  82.4 5.6 %collective-permute-start.12 = (bf16[256,256]{1,0:T(8,128)(2,1)S(1)}, bf16[256,256]{1,0:T(8,128)(2,1)S(1)}, u32[]{:S(2)}, u32[]{:S(2)}) collective-permute-start(bf16[256,256]{1,0:T(8,128)(2,1)S(1)} %collective-permute-done.10.rest_0_), channel_id=1, source_target_pairs={{0,32},{32,64},{64,96},{96,128},{128,160},{160,192},{192,224},{224... | collective-permute-start | bytes 393224 | tf_op jit(solution)/shard_map/ppermute | solution.py:326
  93.6 16.6 %all-to-all-start.3 = ((bf16[8,3,4,16,256]{4,3,2,1,0:T(8,128)(2,1)}), bf16[8,3,4,16,256]{4,3,2,1,0:T(8,128)(2,1)S(1)}, u32[]{:S(2)}, u32[]{:S(2)}) async-start(bf16[8,3,4,16,256]{4,3,2,1,0:T(8,128)(2,1)} %shard_map.99), calls=%async_computation.3 | async-start | bytes 1572864 | tf_op jit(solution)/shard_map/all_to_all | solution.py:424

commit v3 on v2

--- a/solution.py
+++ b/solution.py
@@ -224,6 +224,8 @@
         square = average * average
         squares.append(jnp.sum(square[:, :128] + square[:, 128:], axis=0, keepdims=True))
     squares = jnp.sum(jnp.concatenate(squares, axis=0), axis=1, keepdims=True)
+    diagonal = lax.broadcasted_iota(jnp.int32, (OPTIONS, 128), 0) == lanes(OPTIONS)
+    squares = jnp.sum(jnp.where(diagonal, squares, 0.0), axis=0, keepdims=True)
     square_ref[...] = jnp.broadcast_to(squares[None], square_ref.shape)
     for i, peer_ref in enumerate(peer_refs):
         peer_ref[...] = avg_ref[usage_ref[PATHS] ^ (i + 1)]
@@ -232,7 +234,10 @@
 def clip_factor(square_ref):
     total = jnp.sum(square_ref[...], axis=0)
     entries = 4.0 * ROWS * WIDTH
-    return jnp.minimum(1.0, 0.3 / jnp.sqrt(total / entries + 1e-06))
+    factors = jnp.minimum(1.0, 0.3 / jnp.sqrt(total / entries + 1e-06))
+    diagonal = lax.broadcasted_iota(jnp.int32, (OPTIONS, 128), 0) == lanes(OPTIONS)
+    factors = jnp.sum(jnp.where(diagonal, factors, 0.0), axis=1, keepdims=True)
+    return jnp.broadcast_to(factors, (OPTIONS, 128))
 
 
 def fresh_kernel(usage_ref, avg_ref, square_ref, table_ref, *rest):
@@ -250,9 +255,26 @@
             fresh_ref[pl.ds(pl.multiple_of(module * ROWS, ROWS), ROWS), :] = fresh
 
 
+def neighbour(own, shift):
+    chip = ((own >> 1) + (shift >> 1)) & 3
+    return chip * 2 + ((own & 1) ^ (shift & 1))
+
+
 def pack_kernel(steps, row_ref, *rest):
+    block_refs, out_refs = rest[: len(steps)], rest[len(steps) :]
+    for shift in range(8):
+        target = neighbour(row_ref[PATHS + 1], shift)
+        for b, step in enumerate(steps):
+            origin = (row_ref[PATHS] + (step + DEPTH)) % DEPTH
+            for p in range(MINE):
+                o = row_ref[origin * 32 + target * MINE + p]
+                rows = pl.ds(pl.multiple_of(o * ROWS, ROWS), ROWS)
+                out_refs[shift][b, p] = block_refs[b][rows, :]
+
+
+def pack_all_kernel(steps, first, row_ref, *rest):
     block_refs = rest[: len(steps)]
-    out_any, out_ref, sems = rest[len(steps) :]
+    out_any, out_ref, sems = rest[-3:]
     copies = []
     for b, step in enumerate(steps):
         origin = (row_ref[PATHS] + (step + DEPTH)) % DEPTH
@@ -261,7 +283,7 @@
                 o = row_ref[origin * 32 + target * MINE + p]
                 rows = pl.ds(pl.multiple_of(o * ROWS, ROWS), ROWS)
                 out_ref[target, b, p] = block_refs[b][rows, :]
-        copies.append(pltpu.make_async_copy(out_ref.at[:, b], out_any.at[:, b], sems.at[b]))
+        copies.append(pltpu.make_async_copy(out_ref.at[:, b], out_any.at[:, first + b], sems.at[b]))
         copies[-1].start()
     for copy in copies:
         copy.wait()
@@ -285,7 +307,28 @@
             new_params_ref[i, :, at] = new.astype(BF16)
 
 
-def place_kernel(steps, row_ref, got_ref, *rest):
+def place_kernel(steps, row_ref, *rest):
+    got_refs = rest[:8]
+    out_ref, sems = rest[-2:]
+    copies = []
+    for shift, got_ref in enumerate(got_refs):
+        source = neighbour(row_ref[PATHS + 1], 8 - (shift & 6) + (shift & 1))
+        columns = pl.ds(pl.multiple_of((source & 3) * COLS, COLS), COLS)
+        for b, step in enumerate(steps):
+            origin = (row_ref[PATHS] + (step + DEPTH)) % DEPTH
+            level = origin * 2 + (source >> 2)
+            copies.append(
+                pltpu.make_async_copy(
+                    got_ref.at[b], out_ref.at[:, level, :, columns], sems.at[len(copies)]
+                )
+            )
+    for copy in copies:
+        copy.start()
+    for copy in copies:
+        copy.wait()
+
+
+def place_all_kernel(steps, row_ref, got_ref, *rest):
     out_ref, sems = rest[-2:]
     copies = []
     for b, step in enumerate(steps):
@@ -326,28 +369,48 @@
     return lax.ppermute(values, "z", [(i, (i + k) % DEPTH) for i in range(DEPTH)])
 
 
-def pack_row(steps, row, blocks):
+def pack_all(steps, row, blocks, first, rest):
     shape = (8, len(steps), MINE, ROWS, COLS)
     return call(
-        functools.partial(pack_kernel, steps),
-        shaped(shape, BF16),
+        functools.partial(pack_all_kernel, steps, first),
+        shaped((8, len(NEAR), MINE, ROWS, COLS), BF16),
         in_specs=[pl.BlockSpec(memory_space=pltpu.SMEM)]
-        + [pl.BlockSpec(memory_space=pltpu.VMEM)] * len(steps),
+        + [pl.BlockSpec(memory_space=pltpu.VMEM)] * len(steps)
+        + [pl.BlockSpec(memory_space=pltpu.HBM)] * len(rest),
         out_specs=pl.BlockSpec(memory_space=pltpu.HBM),
         scratch_shapes=[pltpu.VMEM(shape, BF16), pltpu.SemaphoreType.DMA((len(steps),))],
+        input_output_aliases={1 + len(steps): 0} if rest else {},
+    )(row, *blocks, *rest)
+
+
+def pack_row(steps, row, blocks):
+    vmem = pl.BlockSpec(memory_space=pltpu.VMEM)
+    return call(
+        functools.partial(pack_kernel, steps),
+        [shaped((len(steps), MINE, ROWS, COLS), BF16)] * 8,
+        in_specs=[pl.BlockSpec(memory_space=pltpu.SMEM)] + [vmem] * len(steps),
+        out_specs=[vmem] * 8,
     )(row, *blocks)
 
 
-def place_row(steps, row, got, rest):
+def exchange_row(packed):
+    got = [packed[0]]
+    for shift in range(1, 8):
+        pairs = [(i, neighbour(i, shift)) for i in range(8)]
+        got.append(lax.ppermute(packed[shift], ROW, pairs))
+    return got
+
+
+def place_row(kernel, steps, row, got, rest):
     anywhere = pl.BlockSpec(memory_space=pl.ANY)
     return call(
-        functools.partial(place_kernel, steps),
+        functools.partial(kernel, steps),
         shaped((MINE, LEVELS, ROWS, WIDTH), BF16),
-        in_specs=[pl.BlockSpec(memory_space=pltpu.SMEM)] + [anywhere] * (1 + len(rest)),
+        in_specs=[pl.BlockSpec(memory_space=pltpu.SMEM)] + [anywhere] * len(got + rest),
         out_specs=anywhere,
         scratch_shapes=[pltpu.SemaphoreType.DMA((8 * len(steps),))],
-        input_output_aliases={2: 0} if rest else {},
-    )(row, got, *rest)
+        input_output_aliases={1 + len(got): 0} if rest else {},
+    )(row, *got, *rest)
 
 
 def local(pseudo_grad, kept_index, usage, module_params, momentum):
@@ -360,7 +423,8 @@
     used = jnp.concatenate([used, jnp.full((8,), q, jnp.int32)])
     row = lax.dynamic_slice_in_dim(usage, 32 * z, 32, 0).reshape(32, DEPTH, 2)
     row = lax.dynamic_index_in_dim(row, half, 2, keepdims=False).T.reshape(PATHS)
-    row = jnp.concatenate([row, jnp.full((8,), z, jnp.int32)])
+    place = jnp.where(jnp.arange(8) == 0, z, half * QUAD + q).astype(jnp.int32)
+    row = jnp.concatenate([row, place])
 
     bases = call(
         base_kernel,
@@ -392,7 +456,7 @@
 
     average, squares, *pieces = call(
         sum_kernel,
-        [shaped((QUAD, MINE * ROWS, COLS), BF16), shaped((16, OPTIONS, 128), F32)]
+        [shaped((QUAD, MINE * ROWS, COLS), BF16), shaped((16, 1, 128), F32)]
         + [shaped((MINE * ROWS, COLS), BF16)] * 3,
         in_specs=[smem, vmem],
         out_specs=[vmem] * 5,
@@ -401,8 +465,6 @@
         + [pltpu.SMEM((OPTIONS,), jnp.int32)],
     )(used, got)
     squares = lax.all_to_all(squares, SQUARE_GROUP, 0, 0, tiled=True)
-    pieces = [swap(piece, k + 1) for k, piece in enumerate(pieces)]
-    squares, pieces = lax.optimization_barrier((squares, pieces))
 
     fresh = call(
         fresh_kernel,
@@ -415,13 +477,15 @@
     for _ in range(2):
         before.append(along(before[-1], 1))
         after.append(along(after[-1], -1))
-    packed = pack_row(NEAR, row, [fresh, before[1], after[1], before[2], after[2]])
+    pieces, _ = lax.optimization_barrier((pieces, fresh))
+    pieces = [swap(piece, k + 1) for k, piece in enumerate(pieces)]
+    packed = pack_all(NEAR[:3], row, [fresh, before[1], after[1]], 0, [])
+    packed, pieces = lax.optimization_barrier((packed, pieces))
+    packed = pack_all(NEAR[3:], row, [before[2], after[2]], 3, [packed])
     packed, before2, after2 = lax.optimization_barrier((packed, before[2], after[2]))
     near = lax.all_to_all(packed, ROW, 0, 0, tiled=True)
     before3, after3 = along(before2, 1), along(after2, -1)
-    packed = pack_row(FAR, row, [before3, after3, along(before3, 1)])
-    packed, near, pieces = lax.optimization_barrier((packed, near, pieces))
-    far = lax.all_to_all(packed, ROW, 0, 0, tiled=True)
+    far = exchange_row(pack_row(FAR, row, [before3, after3, along(before3, 1)]))
 
     new_params, new_momentum = call(
         owner_kernel,
@@ -431,8 +495,8 @@
         scratch_shapes=[pltpu.VMEM((OPTIONS, 128), F32)],
     )(used, average, squares, inverse, module_params, momentum, *pieces)
 
-    path_params = place_row(NEAR, row, near, [])
-    path_params = place_row(FAR, row, far, [path_params])
+    path_params = place_row(place_all_kernel, NEAR, row, [near], [])
+    path_params = place_row(place_kernel, FAR, row, far, [path_params])
     return (new_params, new_momentum, path_params)
 
 

time: 112 us -> 106 us (0.946)
  waiting for transfers between devices: 49.7 us -> 33.1 us
  blocking collectives: 0 us -> 11.2 us
    all_to_all x0 -> x1, blocking collectives: none -> 11.2 us  [local(): squares = lax.all_to_all(squares, SQUARE_GROUP, 0, 0, tiled=True)]
    all_to_all x2 -> x0, starting transfers between devices: 10.3 us -> none  [the longest x1 5.94 us: local(): squares = lax.all_to_all(squares, SQUARE_GROUP, 0, 0, tiled=True)]
    ppermute x0 -> x7, starting transfers between devices: none -> 9.85 us  [exchange_row(): got.append(lax.ppermute(packed[shift], ROW, pairs))]
    all_to_all x2 -> x0, waiting for transfers between devices: 9.4 us -> none  [the longest x1 8.72 us: local(): far = lax.all_to_all(packed, ROW, 0, 0, tiled=True)]
    all_to_all x1, waiting for transfers between devices: 3.97 us -> 0.01 us  [local(): near = lax.all_to_all(packed, ROW, 0, 0, tiled=True)]
    ppermute x7, waiting for transfers between devices: 15.1 us -> 11.9 us  [along(): lax.ppermute(values, 'z', [(i, (i + k) % DEPTH) for i in range(DEPTH)])]
    ppermute x6, waiting for transfers between devices: 9.03 us -> 6.29 us  [swap(): return lax.ppermute(values, 'quad', [(i, i ^ k) for i in range(QUAD)])]
    ppermute x0 -> x7, waiting for transfers between devices: none -> 2.57 us  [exchange_row(): got.append(lax.ppermute(packed[shift], ROW, pairs))]
  transfers between devices with their start and end apart: 17 -> 22, of which waited for: 12 -> 9; matrix products, arithmetic and copies ran while one was open for 0% -> 0% of each run, Pallas kernels for 5% -> 6%
where the time goes in v3:
time: 106 us; the launch traced here: 105 us
  starting transfers between devices  41.4 us (39%)
  waiting for transfers between devices  33.1 us (31%)
  Pallas kernels  18.3 us (17%)
  blocking collectives  11.2 us (11%)
    all_to_all x1, starting transfers between devices, local(): lax.all_to_all(outgoing.reshape(DEVICES, SENT, 128), PATH, 0, 0, tiled=True)  13.1 us
    all_to_all x1, waiting for transfers between devices, local(): lax.all_to_all(outgoing.reshape(DEVICES, SENT, 128), PATH, 0, 0, tiled=True)  12.3 us
    ppermute x7, waiting for transfers between devices, along(): lax.ppermute(values, 'z', [(i, (i + k) % DEPTH) for i in range(DEPTH)])  11.9 us
    all_to_all x1, blocking collectives, local(): squares = lax.all_to_all(squares, SQUARE_GROUP, 0, 0, tiled=True)  11.2 us
    ppermute x7, starting transfers between devices, exchange_row(): got.append(lax.ppermute(packed[shift], ROW, pairs))  9.85 us
    ppermute x7, starting transfers between devices, along(): lax.ppermute(values, 'z', [(i, (i + k) % DEPTH) for i in range(DEPTH)])  8.11 us
    ppermute x6, waiting for transfers between devices, swap(): return lax.ppermute(values, 'quad', [(i, i ^ k) for i in range(QUAD)])  6.29 us
    ppermute x6, starting transfers between devices, swap(): return lax.ppermute(values, 'quad', [(i, i ^ k) for i in range(QUAD)])  6.02 us
  transfers between devices with their start and end apart: 22, of which 9 were waited for; matrix products, arithmetic and copies ran while one was open for 0% of the time, Pallas kernels for 6%

profile of v3, /device:TPU:1, one launch (start us, length us, event | category | flops | bytes accessed | tf_op | source)
XLA Modules:
  0.0 105.2 jit_solution(1679676694471353476)
XLA Ops:
  0.6 0.0 copy-start
  0.7 5.0 %shard_map.94 = bf16[16,4,40,128]{3,2,1,0:T(8,128)(2,1)} custom-call(bf16[4,16,16,1024]{3,2,1,0:T(8,128)(2,1)} %grad_any.1, s32[4,16,16,16]{3,2,1,0:T(8,128)} %kept_any.1, bf16[2,256,256]{2,1,0:T(8,128)(2,1)} %constant.38.clone.table_any), custom_call_target="tpu_custom_call" | custom-call | tf_op jit(solution)/shard_map/pallas_call | solution.py:438
  5.6 0.0 copy-start.1
  5.6 13.1 %all-to-all-start = ((bf16[64,40,128]{2,1,0:T(8,128)(2,1)}), bf16[64,40,128]{2,1,0:T(8,128)(2,1)S(1)}, u32[]{:S(2)}, u32[]{:S(2)}) async-start(bf16[64,40,128]{2,1,0:T(8,128)(2,1)} %bitcast.7), calls=%async_computation | async-start | bytes 1310720 | tf_op jit(solution)/shard_map/all_to_all | solution.py:454
  18.9 0.5 collective-permute-start
  19.4 1.3 %collective-permute-start.1 = (f32[64,256]{1,0:T(8,128)S(1)}, f32[64,256]{1,0:T(8,128)S(1)}, u32[]{:S(2)}, u32[]{:S(2)}) collective-permute-start(f32[64,256]{1,0:T(8,128)S(1)} %get-tuple-element.40), channel_id=1, source_target_pairs={{0,8},{4,12},{8,0},{12,4},{1,9},{5,13},{9,1},{13,5},{2,10},{6,14},... | collective-permute-start | bytes 196616 | tf_op jit(solution)/shard_map/ppermute | solution.py:365
  20.7 0.4 collective-permute-start.2
  21.1 0.1 constant_dynamic-slice_fusion.1
  21.2 0.1 reshape.21
  21.3 0.0 collective-permute-done.rest_1_
  21.4 2.4 %collective-permute-done.1.rest_2_ = f32[64,256]{1,0:T(8,128)S(1)} collective-permute-done((f32[64,256]{1,0:T(8,128)S(1)}, f32[64,256]{1,0:T(8,128)S(1)}, u32[]{:S(2)}, u32[]{:S(2)}) %collective-permute-start.1) | collective-permute-done | bytes 65568 | tf_op jit(solution)/shard_map/ppermute | solution.py:365
  23.8 3.1 %collective-permute-done.2.rest_3_ = f32[64,256]{1,0:T(8,128)S(1)} collective-permute-done((f32[64,256]{1,0:T(8,128)S(1)}, f32[64,256]{1,0:T(8,128)S(1)}, u32[]{:S(2)}, u32[]{:S(2)}) %collective-permute-start.2) | collective-permute-done | bytes 65568 | tf_op jit(solution)/shard_map/ppermute | solution.py:365
  26.9 12.3 %all-to-all-done.got_ref = bf16[64,40,128]{2,1,0:T(8,128)(2,1)S(1)} async-done(((bf16[64,40,128]{2,1,0:T(8,128)(2,1)}), bf16[64,40,128]{2,1,0:T(8,128)(2,1)S(1)}, u32[]{:S(2)}, u32[]{:S(2)}) %all-to-all-start) | async-done | bytes 655392 | tf_op jit(solution)/shard_map/all_to_all | solution.py:454
  39.1 3.7 %shard_map.96 = (bf16[4,64,256]{2,1,0:T(8,128)(2,1)S(1)}, f32[16,1,128]{2,1,0:T(1,128)S(1)}, bf16[64,256]{1,0:T(8,128)(2,1)S(1)}, bf16[64,256]{1,0:T(8,128)(2,1)S(1)}, bf16[64,256]{1,0:T(8,128)(2,1)S(1)}) custom-call(s32[264]{0:T(512)S(1)} %concatenate.6.usage_ref, bf16[64,40,128]{2,1,0:T(8,128)(2,1)S(1)} %all-to-all-done.got_ref), custom_call_target="tpu_custom_call" | custom-call | tf_op jit(solution)/shard_map/pallas_call | solution.py:457
  42.8 11.2 %all_to_all.15.square_ref = f32[16,1,128]{2,1,0:T(1,128)S(1)} all-to-all(f32[16,1,128]{2,1,0:T(1,128)S(1)} %get-tuple-element.44), channel_id=1, replica_groups=mesh['z'=8,'half'=2,'quad'=4,'shard'=4] {'quad','shard'}, dimensions={0} | all-to-all | bytes 16384 | tf_op jit(solution)/shard_map/all_to_all | solution.py:467
  54.0 0.9 shard_map.97.rest_0_
  54.9 0.4 collective-permute-start.3
  55.3 2.3 %collective-permute-start.4 = (bf16[256,256]{1,0:T(8,128)(2,1)S(1)}, bf16[256,256]{1,0:T(8,128)(2,1)S(1)}, u32[]{:S(2)}, u32[]{:S(2)}) collective-permute-start(bf16[256,256]{1,0:T(8,128)(2,1)S(1)} %shard_map.97.rest_0_), channel_id=1, source_target_pairs={{0,224},{32,0},{64,32},{96,64},{128,96},{160,128},{192,160},{224,1... | collective-permute-start | bytes 393224 | tf_op jit(solution)/shard_map/ppermute | solution.py:369
  57.6 2.9 %collective-permute-done.3.rest_1_ = bf16[256,256]{1,0:T(8,128)(2,1)S(1)} collective-permute-done((bf16[256,256]{1,0:T(8,128)(2,1)S(1)}, bf16[256,256]{1,0:T(8,128)(2,1)S(1)}, u32[]{:S(2)}, u32[]{:S(2)}) %collective-permute-start.3) | collective-permute-done | bytes 131104 | tf_op jit(solution)/shard_map/ppermute | solution.py:369
  60.5 0.0 collective-permute-done.4.rest_2_
  60.5 2.7 %collective-permute-start.9 = (bf16[256,256]{1,0:T(8,128)(2,1)S(1)}, bf16[256,256]{1,0:T(8,128)(2,1)S(1)}, u32[]{:S(2)}, u32[]{:S(2)}) collective-permute-start(bf16[256,256]{1,0:T(8,128)(2,1)S(1)} %collective-permute-done.4.rest_2_), channel_id=1, source_target_pairs={{0,224},{32,0},{64,32},{96,64},{128,96},{160,128},{192,160},{224,1... | collective-permute-start | bytes 393224 | tf_op jit(solution)/shard_map/ppermute | solution.py:369
  63.2 2.1 %collective-permute-start.5 = (bf16[64,256]{1,0:T(8,128)(2,1)S(1)}, bf16[64,256]{1,0:T(8,128)(2,1)S(1)}, u32[]{:S(2)}, u32[]{:S(2)}) collective-permute-start(bf16[64,256]{1,0:T(8,128)(2,1)S(1)} %get-tuple-element.53), channel_id=1, source_target_pairs={{0,4},{4,0},{8,12},{12,8},{1,5},{5,1},{9,13},{13,9},{2,6},{6,2},{1... | collective-permute-start | bytes 98312 | tf_op jit(solution)/shard_map/ppermute | solution.py:365
  65.3 0.3 collective-permute-start.6
  65.6 1.3 %collective-permute-start.7 = (bf16[64,256]{1,0:T(8,128)(2,1)S(1)}, bf16[64,256]{1,0:T(8,128)(2,1)S(1)}, u32[]{:S(2)}, u32[]{:S(2)}) collective-permute-start(bf16[64,256]{1,0:T(8,128)(2,1)S(1)} %get-tuple-element.55), channel_id=1, source_target_pairs={{0,12},{4,8},{8,4},{12,0},{1,13},{5,9},{9,5},{13,1},{2,14},{6,10},... | collective-permute-start | bytes 98312 | tf_op jit(solution)/shard_map/ppermute | solution.py:365
  67.0 1.5 %shard_map.98.rest_2_ = bf16[8,5,4,16,256]{4,3,2,1,0:T(8,128)(2,1)} custom-call(s32[264]{0:T(512)S(1)} %pad_add_fusion.row_ref, bf16[256,256]{1,0:T(8,128)(2,1)S(1)} %shard_map.97.rest_0_, bf16[256,256]{1,0:T(8,128)(2,1)S(1)} %collective-permute-done.3.rest_1_, bf16[256,256]{1,0:T(8,128)(2,1)S(1)} %collective-permute-done.4.rest_2_), custom_call_target="tpu_custom_call" | custom-call | tf_op jit(solution)/shard_map/pallas_call | solution.py:374
  68.5 0.0 collective-permute-done.6.rest_1_
  68.5 0.8 collective-permute-done.7.rest_2_
  69.3 0.0 collective-permute-done.8.rest_0_
  69.3 0.0 collective-permute-done.9.rest_1_
  69.3 1.4 %shard_map.100 = bf16[8,5,4,16,256]{4,3,2,1,0:T(8,128)(2,1)} custom-call(s32[264]{0:T(512)S(1)} %pad_add_fusion.row_ref, bf16[256,256]{1,0:T(8,128)(2,1)S(1)} %collective-permute-done.8.rest_0_, bf16[256,256]{1,0:T(8,128)(2,1)S(1)} %collective-permute-done.9.rest_1_, bf16[8,5,4,16,256]{4,3,2,1,0:T(8,128)(2,1)} %shard_map.98.rest_2_), custom_call_target="tpu_custom_call", output_to_operand_aliasing={{}: (3, {})} | custom-call | tf_op jit(solution)/shard_map/pallas_call | solution.py:374
  70.7 4.3 %all-to-all-start.2 = ((bf16[8,5,4,16,256]{4,3,2,1,0:T(8,128)(2,1)}), bf16[8,5,4,16,256]{4,3,2,1,0:T(8,128)(2,1)S(1)}, u32[]{:S(2)}, u32[]{:S(2)}) async-start(bf16[8,5,4,16,256]{4,3,2,1,0:T(8,128)(2,1)} %shard_map.100), calls=%async_computation.2 | async-start | bytes 2621440 | tf_op jit(solution)/shard_map/all_to_all | solution.py:486
  75.0 0.0 collective-permute-start.10
  75.0 2.7 %collective-permute-start.11 = (bf16[256,256]{1,0:T(8,128)(2,1)S(1)}, bf16[256,256]{1,0:T(8,128)(2,1)S(1)}, u32[]{:S(2)}, u32[]{:S(2)}) collective-permute-start(bf16[256,256]{1,0:T(8,128)(2,1)S(1)} %collective-permute-done.9.rest_1_), channel_id=1, source_target_pairs={{0,224},{32,0},{64,32},{96,64},{128,96},{160,128},{192,160},{224,1... | collective-permute-start | bytes 393224 | tf_op jit(solution)/shard_map/ppermute | solution.py:369
  77.7 3.6 %collective-permute-done.10.rest_0_ = bf16[256,256]{1,0:T(8,128)(2,1)S(1)} collective-permute-done((bf16[256,256]{1,0:T(8,128)(2,1)S(1)}, bf16[256,256]{1,0:T(8,128)(2,1)S(1)}, u32[]{:S(2)}, u32[]{:S(2)}) %collective-permute-start.10) | collective-permute-done | bytes 131104 | tf_op jit(solution)/shard_map/ppermute | solution.py:369
  81.3 5.4 %collective-permute-done.12.rest_2_ = bf16[256,256]{1,0:T(8,128)(2,1)S(1)} collective-permute-done((bf16[256,256]{1,0:T(8,128)(2,1)S(1)}, bf16[256,256]{1,0:T(8,128)(2,1)S(1)}, u32[]{:S(2)}, u32[]{:S(2)}) %collective-permute-start.12) | collective-permute-done | bytes 131104 | tf_op jit(solution)/shard_map/ppermute | solution.py:369
  86.7 0.7 shard_map.101
  87.4 1.8 %collective-permute-start.13 = (bf16[3,4,16,256]{3,2,1,0:T(8,128)(2,1)S(1)}, bf16[3,4,16,256]{3,2,1,0:T(8,128)(2,1)S(1)}, u32[]{:S(2)}, u32[]{:S(2)}) collective-permute-start(bf16[3,4,16,256]{3,2,1,0:T(8,128)(2,1)S(1)} %get-tuple-element.65), channel_id=1, source_target_pairs={{0,4},{4,0},{8,12},{12,8},{16,20},{20,16},{24,28},{28,24},{1,5},{5... | collective-permute-start | bytes 294920 | tf_op jit(solution)/shard_map/ppermute | solution.py:400
  89.2 1.3 %collective-permute-start.14 = (bf16[3,4,16,256]{3,2,1,0:T(8,128)(2,1)S(1)}, bf16[3,4,16,256]{3,2,1,0:T(8,128)(2,1)S(1)}, u32[]{:S(2)}, u32[]{:S(2)}) collective-permute-start(bf16[3,4,16,256]{3,2,1,0:T(8,128)(2,1)S(1)} %get-tuple-element.66), channel_id=1, source_target_pairs={{0,8},{4,12},{8,16},{12,20},{16,24},{20,28},{24,0},{28,4},{1,9},{5... | collective-permute-start | bytes 294920 | tf_op jit(solution)/shard_map/ppermute | solution.py:400
  90.5 1.4 %collective-permute-start.15 = (bf16[3,4,16,256]{3,2,1,0:T(8,128)(2,1)S(1)}, bf16[3,4,16,256]{3,2,1,0:T(8,128)(2,1)S(1)}, u32[]{:S(2)}, u32[]{:S(2)}) collective-permute-start(bf16[3,4,16,256]{3,2,1,0:T(8,128)(2,1)S(1)} %get-tuple-element.67), channel_id=1, source_target_pairs={{0,12},{4,8},{8,20},{12,16},{16,28},{20,24},{24,4},{28,0},{1,13},{... | collective-permute-start | bytes 294920 | tf_op jit(solution)/shard_map/ppermute | solution.py:400
  91.9 1.4 %collective-permute-start.16 = (bf16[3,4,16,256]{3,2,1,0:T(8,128)(2,1)S(1)}, bf16[3,4,16,256]{3,2,1,0:T(8,128)(2,1)S(1)}, u32[]{:S(2)}, u32[]{:S(2)}) collective-permute-start(bf16[3,4,16,256]{3,2,1,0:T(8,128)(2,1)S(1)} %get-tuple-element.68), channel_id=1, source_target_pairs={{0,16},{4,20},{8,24},{12,28},{16,0},{20,4},{24,8},{28,12},{1,17},{... | collective-permute-start | bytes 294920 | tf_op jit(solution)/shard_map/ppermute | solution.py:400
  93.3 1.9 %collective-permute-start.17 = (bf16[3,4,16,256]{3,2,1,0:T(8,128)(2,1)S(1)}, bf16[3,4,16,256]{3,2,1,0:T(8,128)(2,1)S(1)}, u32[]{:S(2)}, u32[]{:S(2)}) collective-permute-start(bf16[3,4,16,256]{3,2,1,0:T(8,128)(2,1)S(1)} %get-tuple-element.69), channel_id=1, source_target_pairs={{0,20},{4,16},{8,28},{12,24},{16,4},{20,0},{24,12},{28,8},{1,21},{... | collective-permute-start | bytes 294920 | tf_op jit(solution)/shard_map/ppermute | solution.py:400
  95.2 1.5 %collective-permute-start.18 = (bf16[3,4,16,256]{3,2,1,0:T(8,128)(2,1)S(1)}, bf16[3,4,16,256]{3,2,1,0:T(8,128)(2,1)S(1)}, u32[]{:S(2)}, u32[]{:S(2)}) collective-permute-start(bf16[3,4,16,256]{3,2,1,0:T(8,128)(2,1)S(1)} %get-tuple-element.70), channel_id=1, source_target_pairs={{0,24},{4,28},{8,0},{12,4},{16,8},{20,12},{24,16},{28,20},{1,25},{... | collective-permute-start | bytes 294920 | tf_op jit(solution)/shard_map/ppermute | solution.py:400
  96.7 0.5 collective-permute-start.19
  97.3 1.6 %shard_map.99 = (bf16[4,16,1024]{2,1,0:T(8,128)(2,1)}, f32[4,16,1024]{2,1,0:T(8,128)}) custom-call(s32[264]{0:T(512)S(1)} %concatenate.6.usage_ref, bf16[4,64,256]{2,1,0:T(8,128)(2,1)S(1)} %get-tuple-element.43.avg_ref, f32[16,1,128]{2,1,0:T(1,128)S(1)} %all_to_all.15.square_ref, bf16[2,256,256]{2,1,0:T(8,128)(2,1)S(1)} %copy-done.1, ...), custom_call_target="tpu_custom_call" | custom-call | tf_op jit(solution)/shard_map/pallas_call | solution.py:490
  98.9 1.9 %shard_map.102.rest_8_ = bf16[4,16,16,1024]{3,2,1,0:T(8,128)(2,1)} custom-call(s32[264]{0:T(512)S(1)} %pad_add_fusion.row_ref, bf16[8,5,4,16,256]{4,3,2,1,0:T(8,128)(2,1)S(1)} %all-to-all-done.2.got_ref), custom_call_target="tpu_custom_call" | custom-call | tf_op jit(solution)/shard_map/pallas_call | solution.py:406
  100.9 1.4 %collective-permute-done.17.rest_5_ = bf16[3,4,16,256]{3,2,1,0:T(8,128)(2,1)S(1)} collective-permute-done((bf16[3,4,16,256]{3,2,1,0:T(8,128)(2,1)S(1)}, bf16[3,4,16,256]{3,2,1,0:T(8,128)(2,1)S(1)}, u32[]{:S(2)}, u32[]{:S(2)}) %collective-permute-start.17) | collective-permute-done | bytes 98336 | tf_op jit(solution)/shard_map/ppermute | solution.py:400
  102.3 1.2 %collective-permute-done.19.rest_7_ = bf16[3,4,16,256]{3,2,1,0:T(8,128)(2,1)S(1)} collective-permute-done((bf16[3,4,16,256]{3,2,1,0:T(8,128)(2,1)S(1)}, bf16[3,4,16,256]{3,2,1,0:T(8,128)(2,1)S(1)}, u32[]{:S(2)}, u32[]{:S(2)}) %collective-permute-start.19) | collective-permute-done | bytes 98336 | tf_op jit(solution)/shard_map/ppermute | solution.py:400
  103.4 1.6 %shard_map.103 = bf16[4,16,16,1024]{3,2,1,0:T(8,128)(2,1)} custom-call(s32[264]{0:T(512)S(1)} %pad_add_fusion.row_ref, bf16[3,4,16,256]{3,2,1,0:T(8,128)(2,1)S(1)} %get-tuple-element.64.rest_0_, bf16[3,4,16,256]{3,2,1,0:T(8,128)(2,1)S(1)} %collective-permute-done.13.rest_1_, ...), custom_call_target="tpu_custom_call", output_to_operand_aliasing={{}: (9, {})} | custom-call | tf_op jit(solution)/shard_map/pallas_call | solution.py:406
  (22 shorter events, 0.1 us)
Async XLA Ops:
  0.6 20.5 %copy-start = (s32[256,16]{0,1:T(8,128)S(1)}, s32[256,16]{0,1:T(8,128)}, u32[]{:S(2)}) copy-start(s32[256,16]{0,1:T(8,128)} %param.9) | copy-start | bytes 49156
  0.6 18.1 %copy-start.3 = (bf16[4,16,1024]{2,1,0:T(8,128)(2,1)S(1)}, bf16[4,16,1024]{2,1,0:T(8,128)(2,1)}, u32[]{:S(2)}) copy-start(bf16[4,16,1024]{2,1,0:T(8,128)(2,1)} %params_ref.3) | copy-start | bytes 393220
  0.7 18.1 %copy-start.2 = (f32[4,16,1024]{2,1,0:T(8,128)S(1)}, f32[4,16,1024]{2,1,0:T(8,128)}, u32[]{:S(2)}) copy-start(f32[4,16,1024]{2,1,0:T(8,128)} %momentum_ref.3) | copy-start | bytes 786436
  5.6 48.4 %copy-start.1 = (bf16[2,256,256]{2,1,0:T(8,128)(2,1)S(1)}, bf16[2,256,256]{2,1,0:T(8,128)(2,1)}, u32[]{:S(2)}) copy-start(bf16[2,256,256]{2,1,0:T(8,128)(2,1)} %constant.39.clone.table_ref) | copy-start | bytes 786436
  5.6 33.5 %all-to-all-start = ((bf16[64,40,128]{2,1,0:T(8,128)(2,1)}), bf16[64,40,128]{2,1,0:T(8,128)(2,1)S(1)}, u32[]{:S(2)}, u32[]{:S(2)}) async-start(bf16[64,40,128]{2,1,0:T(8,128)(2,1)} %bitcast.7), calls=%async_computation | async-start | bytes 1310720 | tf_op jit(solution)/shard_map/all_to_all | solution.py:454
  18.9 2.5 %collective-permute-start = (f32[64,256]{1,0:T(8,128)S(1)}, f32[64,256]{1,0:T(8,128)S(1)}, u32[]{:S(2)}, u32[]{:S(2)}) collective-permute-start(f32[64,256]{1,0:T(8,128)S(1)} %get-tuple-element.39), channel_id=1, source_target_pairs={{0,4},{4,0},{8,12},{12,8},{1,5},{5,1},{9,13},{13,9},{2,6},{6,2},{1... | collective-permute-start | bytes 196616 | tf_op jit(solution)/shard_map/ppermute | solution.py:365
  19.4 4.4 %collective-permute-start.1 = (f32[64,256]{1,0:T(8,128)S(1)}, f32[64,256]{1,0:T(8,128)S(1)}, u32[]{:S(2)}, u32[]{:S(2)}) collective-permute-start(f32[64,256]{1,0:T(8,128)S(1)} %get-tuple-element.40), channel_id=1, source_target_pairs={{0,8},{4,12},{8,0},{12,4},{1,9},{5,13},{9,1},{13,5},{2,10},{6,14},... | collective-permute-start | bytes 196616 | tf_op jit(solution)/shard_map/ppermute | solution.py:365
  20.7 6.2 %collective-permute-start.2 = (f32[64,256]{1,0:T(8,128)S(1)}, f32[64,256]{1,0:T(8,128)S(1)}, u32[]{:S(2)}, u32[]{:S(2)}) collective-permute-start(f32[64,256]{1,0:T(8,128)S(1)} %get-tuple-element.41), channel_id=1, source_target_pairs={{0,12},{4,8},{8,4},{12,0},{1,13},{5,9},{9,5},{13,1},{2,14},{6,10},... | collective-permute-start | bytes 196616 | tf_op jit(solution)/shard_map/ppermute | solution.py:365
  54.9 5.6 %collective-permute-start.3 = (bf16[256,256]{1,0:T(8,128)(2,1)S(1)}, bf16[256,256]{1,0:T(8,128)(2,1)S(1)}, u32[]{:S(2)}, u32[]{:S(2)}) collective-permute-start(bf16[256,256]{1,0:T(8,128)(2,1)S(1)} %shard_map.97.rest_0_), channel_id=1, source_target_pairs={{0,32},{32,64},{64,96},{96,128},{128,160},{160,192},{192,224},{224... | collective-permute-start | bytes 393224 | tf_op jit(solution)/shard_map/ppermute | solution.py:369
  55.3 5.2 %collective-permute-start.4 = (bf16[256,256]{1,0:T(8,128)(2,1)S(1)}, bf16[256,256]{1,0:T(8,128)(2,1)S(1)}, u32[]{:S(2)}, u32[]{:S(2)}) collective-permute-start(bf16[256,256]{1,0:T(8,128)(2,1)S(1)} %shard_map.97.rest_0_), channel_id=1, source_target_pairs={{0,224},{32,0},{64,32},{96,64},{128,96},{160,128},{192,160},{224,1... | collective-permute-start | bytes 393224 | tf_op jit(solution)/shard_map/ppermute | solution.py:369
  60.5 8.7 %collective-permute-start.8 = (bf16[256,256]{1,0:T(8,128)(2,1)S(1)}, bf16[256,256]{1,0:T(8,128)(2,1)S(1)}, u32[]{:S(2)}, u32[]{:S(2)}) collective-permute-start(bf16[256,256]{1,0:T(8,128)(2,1)S(1)} %collective-permute-done.3.rest_1_), channel_id=1, source_target_pairs={{0,32},{32,64},{64,96},{96,128},{128,160},{160,192},{192,224},{224... | collective-permute-start | bytes 393224 | tf_op jit(solution)/shard_map/ppermute | solution.py:369
  60.5 8.7 %collective-permute-start.9 = (bf16[256,256]{1,0:T(8,128)(2,1)S(1)}, bf16[256,256]{1,0:T(8,128)(2,1)S(1)}, u32[]{:S(2)}, u32[]{:S(2)}) collective-permute-start(bf16[256,256]{1,0:T(8,128)(2,1)S(1)} %collective-permute-done.4.rest_2_), channel_id=1, source_target_pairs={{0,224},{32,0},{64,32},{96,64},{128,96},{160,128},{192,160},{224,1... | collective-permute-start | bytes 393224 | tf_op jit(solution)/shard_map/ppermute | solution.py:369
  63.2 5.3 %collective-permute-start.5 = (bf16[64,256]{1,0:T(8,128)(2,1)S(1)}, bf16[64,256]{1,0:T(8,128)(2,1)S(1)}, u32[]{:S(2)}, u32[]{:S(2)}) collective-permute-start(bf16[64,256]{1,0:T(8,128)(2,1)S(1)} %get-tuple-element.53), channel_id=1, source_target_pairs={{0,4},{4,0},{8,12},{12,8},{1,5},{5,1},{9,13},{13,9},{2,6},{6,2},{1... | collective-permute-start | bytes 98312 | tf_op jit(solution)/shard_map/ppermute | solution.py:365
  65.3 3.2 %collective-permute-start.6 = (bf16[64,256]{1,0:T(8,128)(2,1)S(1)}, bf16[64,256]{1,0:T(8,128)(2,1)S(1)}, u32[]{:S(2)}, u32[]{:S(2)}) collective-permute-start(bf16[64,256]{1,0:T(8,128)(2,1)S(1)} %get-tuple-element.54), channel_id=1, source_target_pairs={{0,8},{4,12},{8,0},{12,4},{1,9},{5,13},{9,1},{13,5},{2,10},{6,14},... | collective-permute-start | bytes 98312 | tf_op jit(solution)/shard_map/ppermute | solution.py:365
  65.6 3.6 %collective-permute-start.7 = (bf16[64,256]{1,0:T(8,128)(2,1)S(1)}, bf16[64,256]{1,0:T(8,128)(2,1)S(1)}, u32[]{:S(2)}, u32[]{:S(2)}) collective-permute-start(bf16[64,256]{1,0:T(8,128)(2,1)S(1)} %get-tuple-element.55), channel_id=1, source_target_pairs={{0,12},{4,8},{8,4},{12,0},{1,13},{5,9},{9,5},{13,1},{2,14},{6,10},... | collective-permute-start | bytes 98312 | tf_op jit(solution)/shard_map/ppermute | solution.py:365
  70.7 28.2 %all-to-all-start.2 = ((bf16[8,5,4,16,256]{4,3,2,1,0:T(8,128)(2,1)}), bf16[8,5,4,16,256]{4,3,2,1,0:T(8,128)(2,1)S(1)}, u32[]{:S(2)}, u32[]{:S(2)}) async-start(bf16[8,5,4,16,256]{4,3,2,1,0:T(8,128)(2,1)} %shard_map.100), calls=%async_computation.2 | async-start | bytes 2621440 | tf_op jit(solution)/shard_map/all_to_all | solution.py:486
  75.0 6.3 %collective-permute-start.10 = (bf16[256,256]{1,0:T(8,128)(2,1)S(1)}, bf16[256,256]{1,0:T(8,128)(2,1)S(1)}, u32[]{:S(2)}, u32[]{:S(2)}) collective-permute-start(bf16[256,256]{1,0:T(8,128)(2,1)S(1)} %collective-permute-done.8.rest_0_), channel_id=1, source_target_pairs={{0,32},{32,64},{64,96},{96,128},{128,160},{160,192},{192,224},{224... | collective-permute-start | bytes 393224 | tf_op jit(solution)/shard_map/ppermute | solution.py:369
  75.0 6.3 %collective-permute-start.11 = (bf16[256,256]{1,0:T(8,128)(2,1)S(1)}, bf16[256,256]{1,0:T(8,128)(2,1)S(1)}, u32[]{:S(2)}, u32[]{:S(2)}) collective-permute-start(bf16[256,256]{1,0:T(8,128)(2,1)S(1)} %collective-permute-done.9.rest_1_), channel_id=1, source_target_pairs={{0,224},{32,0},{64,32},{96,64},{128,96},{160,128},{192,160},{224,1... | collective-permute-start | bytes 393224 | tf_op jit(solution)/shard_map/ppermute | solution.py:369
  81.3 5.4 %collective-permute-start.12 = (bf16[256,256]{1,0:T(8,128)(2,1)S(1)}, bf16[256,256]{1,0:T(8,128)(2,1)S(1)}, u32[]{:S(2)}, u32[]{:S(2)}) collective-permute-start(bf16[256,256]{1,0:T(8,128)(2,1)S(1)} %collective-permute-done.10.rest_0_), channel_id=1, source_target_pairs={{0,32},{32,64},{64,96},{96,128},{128,160},{160,192},{192,224},{224... | collective-permute-start | bytes 393224 | tf_op jit(solution)/shard_map/ppermute | solution.py:369
  87.4 7.8 %collective-permute-start.13 = (bf16[3,4,16,256]{3,2,1,0:T(8,128)(2,1)S(1)}, bf16[3,4,16,256]{3,2,1,0:T(8,128)(2,1)S(1)}, u32[]{:S(2)}, u32[]{:S(2)}) collective-permute-start(bf16[3,4,16,256]{3,2,1,0:T(8,128)(2,1)S(1)} %get-tuple-element.65), channel_id=1, source_target_pairs={{0,4},{4,0},{8,12},{12,8},{16,20},{20,16},{24,28},{28,24},{1,5},{5... | collective-permute-start | bytes 294920 | tf_op jit(solution)/shard_map/ppermute | solution.py:400
  89.2 7.5 %collective-permute-start.14 = (bf16[3,4,16,256]{3,2,1,0:T(8,128)(2,1)S(1)}, bf16[3,4,16,256]{3,2,1,0:T(8,128)(2,1)S(1)}, u32[]{:S(2)}, u32[]{:S(2)}) collective-permute-start(bf16[3,4,16,256]{3,2,1,0:T(8,128)(2,1)S(1)} %get-tuple-element.66), channel_id=1, source_target_pairs={{0,8},{4,12},{8,16},{12,20},{16,24},{20,28},{24,0},{28,4},{1,9},{5... | collective-permute-start | bytes 294920 | tf_op jit(solution)/shard_map/ppermute | solution.py:400
  90.5 10.4 %collective-permute-start.15 = (bf16[3,4,16,256]{3,2,1,0:T(8,128)(2,1)S(1)}, bf16[3,4,16,256]{3,2,1,0:T(8,128)(2,1)S(1)}, u32[]{:S(2)}, u32[]{:S(2)}) collective-permute-start(bf16[3,4,16,256]{3,2,1,0:T(8,128)(2,1)S(1)} %get-tuple-element.67), channel_id=1, source_target_pairs={{0,12},{4,8},{8,20},{12,16},{16,28},{20,24},{24,4},{28,0},{1,13},{... | collective-permute-start | bytes 294920 | tf_op jit(solution)/shard_map/ppermute | solution.py:400
  91.9 8.9 %collective-permute-start.16 = (bf16[3,4,16,256]{3,2,1,0:T(8,128)(2,1)S(1)}, bf16[3,4,16,256]{3,2,1,0:T(8,128)(2,1)S(1)}, u32[]{:S(2)}, u32[]{:S(2)}) collective-permute-start(bf16[3,4,16,256]{3,2,1,0:T(8,128)(2,1)S(1)} %get-tuple-element.68), channel_id=1, source_target_pairs={{0,16},{4,20},{8,24},{12,28},{16,0},{20,4},{24,8},{28,12},{1,17},{... | collective-permute-start | bytes 294920 | tf_op jit(solution)/shard_map/ppermute | solution.py:400
  93.3 8.9 %collective-permute-start.17 = (bf16[3,4,16,256]{3,2,1,0:T(8,128)(2,1)S(1)}, bf16[3,4,16,256]{3,2,1,0:T(8,128)(2,1)S(1)}, u32[]{:S(2)}, u32[]{:S(2)}) collective-permute-start(bf16[3,4,16,256]{3,2,1,0:T(8,128)(2,1)S(1)} %get-tuple-element.69), channel_id=1, source_target_pairs={{0,20},{4,16},{8,28},{12,24},{16,4},{20,0},{24,12},{28,8},{1,21},{... | collective-permute-start | bytes 294920 | tf_op jit(solution)/shard_map/ppermute | solution.py:400
  95.2 7.0 %collective-permute-start.18 = (bf16[3,4,16,256]{3,2,1,0:T(8,128)(2,1)S(1)}, bf16[3,4,16,256]{3,2,1,0:T(8,128)(2,1)S(1)}, u32[]{:S(2)}, u32[]{:S(2)}) collective-permute-start(bf16[3,4,16,256]{3,2,1,0:T(8,128)(2,1)S(1)} %get-tuple-element.70), channel_id=1, source_target_pairs={{0,24},{4,28},{8,0},{12,4},{16,8},{20,12},{24,16},{28,20},{1,25},{... | collective-permute-start | bytes 294920 | tf_op jit(solution)/shard_map/ppermute | solution.py:400
  96.7 6.7 %collective-permute-start.19 = (bf16[3,4,16,256]{3,2,1,0:T(8,128)(2,1)S(1)}, bf16[3,4,16,256]{3,2,1,0:T(8,128)(2,1)S(1)}, u32[]{:S(2)}, u32[]{:S(2)}) collective-permute-start(bf16[3,4,16,256]{3,2,1,0:T(8,128)(2,1)S(1)} %get-tuple-element.71), channel_id=1, source_target_pairs={{0,28},{4,24},{8,4},{12,0},{16,12},{20,8},{24,20},{28,16},{1,29},{... | collective-permute-start | bytes 294920 | tf_op jit(solution)/shard_map/ppermute | solution.py:400

commit v4 on v3

--- a/solution.py
+++ b/solution.py
@@ -394,11 +394,11 @@
 
 
 def exchange_row(packed):
-    got = [packed[0]]
-    for shift in range(1, 8):
+    got = {0: packed[0]}
+    for shift in (4, 5, 2, 6, 3, 7, 1):
         pairs = [(i, neighbour(i, shift)) for i in range(8)]
-        got.append(lax.ppermute(packed[shift], ROW, pairs))
-    return got
+        got[shift] = lax.ppermute(packed[shift], ROW, pairs)
+    return [got[shift] for shift in range(8)]
 
 
 def place_row(kernel, steps, row, got, rest):
@@ -482,7 +482,7 @@
     packed = pack_all(NEAR[:3], row, [fresh, before[1], after[1]], 0, [])
     packed, pieces = lax.optimization_barrier((packed, pieces))
     packed = pack_all(NEAR[3:], row, [before[2], after[2]], 3, [packed])
-    packed, before2, after2 = lax.optimization_barrier((packed, before[2], after[2]))
+    before2, after2 = before[2], after[2]
     near = lax.all_to_all(packed, ROW, 0, 0, tiled=True)
     before3, after3 = along(before2, 1), along(after2, -1)
     far = exchange_row(pack_row(FAR, row, [before3, after3, along(before3, 1)]))

time: 106 us -> 104 us (0.981)
    ppermute x7, starting transfers between devices: 8.11 us -> 5.81 us  [along(): lax.ppermute(values, 'z', [(i, (i + k) % DEPTH) for i in range(DEPTH)])]
    all_to_all x1, starting transfers between devices: 4.33 us -> 5.4 us  [local(): near = lax.all_to_all(packed, ROW, 0, 0, tiled=True)]
where the time goes in v4:
time: 104 us
  starting transfers between devices  40.4 us (39%)
  waiting for transfers between devices  33 us (32%)
  Pallas kernels  18.3 us (18%)
  blocking collectives  11.2 us (11%)
    all_to_all x1, starting transfers between devices, local(): lax.all_to_all(outgoing.reshape(DEVICES, SENT, 128), PATH, 0, 0, tiled=True)  13.1 us
    all_to_all x1, waiting for transfers between devices, local(): lax.all_to_all(outgoing.reshape(DEVICES, SENT, 128), PATH, 0, 0, tiled=True)  12.3 us
    ppermute x7, waiting for transfers between devices, along(): lax.ppermute(values, 'z', [(i, (i + k) % DEPTH) for i in range(DEPTH)])  11.6 us
    all_to_all x1, blocking collectives, local(): squares = lax.all_to_all(squares, SQUARE_GROUP, 0, 0, tiled=True)  11.2 us
    ppermute x7, starting transfers between devices, exchange_row(): got[shift] = lax.ppermute(packed[shift], ROW, pairs)  10.2 us
    ppermute x6, waiting for transfers between devices, swap(): return lax.ppermute(values, 'quad', [(i, i ^ k) for i in range(QUAD)])  6.58 us
    ppermute x6, starting transfers between devices, swap(): return lax.ppermute(values, 'quad', [(i, i ^ k) for i in range(QUAD)])  5.89 us
    ppermute x7, starting transfers between devices, along(): lax.ppermute(values, 'z', [(i, (i + k) % DEPTH) for i in range(DEPTH)])  5.81 us
  transfers between devices with their start and end apart: 22, of which 9 were waited for; matrix products, arithmetic and copies ran while one was open for 0% of the time, Pallas kernels for 6%

profile of v4, /device:TPU:1, one launch (start us, length us, event | category | flops | bytes accessed | tf_op | source)
XLA Modules:
  0.0 104.2 jit_solution(12233652335242976225)
XLA Ops:
  0.6 0.0 copy-start
  0.7 5.0 %shard_map.94 = bf16[16,4,40,128]{3,2,1,0:T(8,128)(2,1)} custom-call(bf16[4,16,16,1024]{3,2,1,0:T(8,128)(2,1)} %grad_any.1, s32[4,16,16,16]{3,2,1,0:T(8,128)} %kept_any.1, bf16[2,256,256]{2,1,0:T(8,128)(2,1)} %constant.38.clone.table_any), custom_call_target="tpu_custom_call" | custom-call | tf_op jit(solution)/shard_map/pallas_call | solution.py:438
  5.6 0.0 copy-start.1
  5.6 13.1 %all-to-all-start = ((bf16[64,40,128]{2,1,0:T(8,128)(2,1)}), bf16[64,40,128]{2,1,0:T(8,128)(2,1)S(1)}, u32[]{:S(2)}, u32[]{:S(2)}) async-start(bf16[64,40,128]{2,1,0:T(8,128)(2,1)} %bitcast.7), calls=%async_computation | async-start | bytes 1310720 | tf_op jit(solution)/shard_map/all_to_all | solution.py:454
  18.9 0.5 collective-permute-start
  19.4 1.3 %collective-permute-start.1 = (f32[64,256]{1,0:T(8,128)S(1)}, f32[64,256]{1,0:T(8,128)S(1)}, u32[]{:S(2)}, u32[]{:S(2)}) collective-permute-start(f32[64,256]{1,0:T(8,128)S(1)} %get-tuple-element.37), channel_id=1, source_target_pairs={{0,8},{4,12},{8,0},{12,4},{1,9},{5,13},{9,1},{13,5},{2,10},{6,14},... | collective-permute-start | bytes 196616 | tf_op jit(solution)/shard_map/ppermute | solution.py:365
  20.7 0.4 collective-permute-start.2
  21.1 0.1 constant_dynamic-slice_fusion.1
  21.2 0.1 reshape.21
  21.4 2.4 %collective-permute-done.1.rest_2_ = f32[64,256]{1,0:T(8,128)S(1)} collective-permute-done((f32[64,256]{1,0:T(8,128)S(1)}, f32[64,256]{1,0:T(8,128)S(1)}, u32[]{:S(2)}, u32[]{:S(2)}) %collective-permute-start.1) | collective-permute-done | bytes 65568 | tf_op jit(solution)/shard_map/ppermute | solution.py:365
  23.8 3.1 %collective-permute-done.2.rest_3_ = f32[64,256]{1,0:T(8,128)S(1)} collective-permute-done((f32[64,256]{1,0:T(8,128)S(1)}, f32[64,256]{1,0:T(8,128)S(1)}, u32[]{:S(2)}, u32[]{:S(2)}) %collective-permute-start.2) | collective-permute-done | bytes 65568 | tf_op jit(solution)/shard_map/ppermute | solution.py:365
  26.9 12.3 %all-to-all-done.got_ref = bf16[64,40,128]{2,1,0:T(8,128)(2,1)S(1)} async-done(((bf16[64,40,128]{2,1,0:T(8,128)(2,1)}), bf16[64,40,128]{2,1,0:T(8,128)(2,1)S(1)}, u32[]{:S(2)}, u32[]{:S(2)}) %all-to-all-start) | async-done | bytes 655392 | tf_op jit(solution)/shard_map/all_to_all | solution.py:454
  39.1 3.7 %shard_map.96 = (bf16[4,64,256]{2,1,0:T(8,128)(2,1)S(1)}, f32[16,1,128]{2,1,0:T(1,128)S(1)}, bf16[64,256]{1,0:T(8,128)(2,1)S(1)}, bf16[64,256]{1,0:T(8,128)(2,1)S(1)}, bf16[64,256]{1,0:T(8,128)(2,1)S(1)}) custom-call(s32[264]{0:T(512)S(1)} %concatenate.6.usage_ref, bf16[64,40,128]{2,1,0:T(8,128)(2,1)S(1)} %all-to-all-done.got_ref), custom_call_target="tpu_custom_call" | custom-call | tf_op jit(solution)/shard_map/pallas_call | solution.py:457
  42.8 11.2 %all_to_all.15.square_ref = f32[16,1,128]{2,1,0:T(1,128)S(1)} all-to-all(f32[16,1,128]{2,1,0:T(1,128)S(1)} %get-tuple-element.41), channel_id=1, replica_groups=mesh['z'=8,'half'=2,'quad'=4,'shard'=4] {'quad','shard'}, dimensions={0} | all-to-all | bytes 16384 | tf_op jit(solution)/shard_map/all_to_all | solution.py:467
  54.0 0.9 shard_map.97.rest_0_
  54.9 0.5 collective-permute-start.4
  55.3 1.1 %collective-permute-start.3 = (bf16[256,256]{1,0:T(8,128)(2,1)S(1)}, bf16[256,256]{1,0:T(8,128)(2,1)S(1)}, u32[]{:S(2)}, u32[]{:S(2)}) collective-permute-start(bf16[256,256]{1,0:T(8,128)(2,1)S(1)} %shard_map.97.rest_0_), channel_id=1, source_target_pairs={{0,32},{32,64},{64,96},{96,128},{128,160},{160,192},{192,224},{224... | collective-permute-start | bytes 393224 | tf_op jit(solution)/shard_map/ppermute | solution.py:369
  56.4 2.9 %collective-permute-done.4.rest_2_ = bf16[256,256]{1,0:T(8,128)(2,1)S(1)} collective-permute-done((bf16[256,256]{1,0:T(8,128)(2,1)S(1)}, bf16[256,256]{1,0:T(8,128)(2,1)S(1)}, u32[]{:S(2)}, u32[]{:S(2)}) %collective-permute-start.4) | collective-permute-done | bytes 131104 | tf_op jit(solution)/shard_map/ppermute | solution.py:369
  59.3 1.6 %collective-permute-start.10 = (bf16[256,256]{1,0:T(8,128)(2,1)S(1)}, bf16[256,256]{1,0:T(8,128)(2,1)S(1)}, u32[]{:S(2)}, u32[]{:S(2)}) collective-permute-start(bf16[256,256]{1,0:T(8,128)(2,1)S(1)} %collective-permute-done.4.rest_2_), channel_id=1, source_target_pairs={{0,224},{32,0},{64,32},{96,64},{128,96},{160,128},{192,160},{224,1... | collective-permute-start | bytes 393224 | tf_op jit(solution)/shard_map/ppermute | solution.py:369
  60.9 0.0 collective-permute-done.3.rest_1_
  60.9 0.0 collective-permute-start.8
  60.9 2.0 %collective-permute-start.5 = (bf16[64,256]{1,0:T(8,128)(2,1)S(1)}, bf16[64,256]{1,0:T(8,128)(2,1)S(1)}, u32[]{:S(2)}, u32[]{:S(2)}) collective-permute-start(bf16[64,256]{1,0:T(8,128)(2,1)S(1)} %get-tuple-element.50), channel_id=1, source_target_pairs={{0,4},{4,0},{8,12},{12,8},{1,5},{5,1},{9,13},{13,9},{2,6},{6,2},{1... | collective-permute-start | bytes 98312 | tf_op jit(solution)/shard_map/ppermute | solution.py:365
  62.9 0.3 collective-permute-start.6
  63.2 1.3 %collective-permute-start.7 = (bf16[64,256]{1,0:T(8,128)(2,1)S(1)}, bf16[64,256]{1,0:T(8,128)(2,1)S(1)}, u32[]{:S(2)}, u32[]{:S(2)}) collective-permute-start(bf16[64,256]{1,0:T(8,128)(2,1)S(1)} %get-tuple-element.52), channel_id=1, source_target_pairs={{0,12},{4,8},{8,4},{12,0},{1,13},{5,9},{9,5},{13,1},{2,14},{6,10},... | collective-permute-start | bytes 98312 | tf_op jit(solution)/shard_map/ppermute | solution.py:365
  64.5 1.5 %shard_map.98.rest_2_ = bf16[8,5,4,16,256]{4,3,2,1,0:T(8,128)(2,1)} custom-call(s32[264]{0:T(512)S(1)} %pad_add_fusion.row_ref, bf16[256,256]{1,0:T(8,128)(2,1)S(1)} %shard_map.97.rest_0_, bf16[256,256]{1,0:T(8,128)(2,1)S(1)} %collective-permute-done.3.rest_1_, bf16[256,256]{1,0:T(8,128)(2,1)S(1)} %collective-permute-done.4.rest_2_), custom_call_target="tpu_custom_call" | custom-call | tf_op jit(solution)/shard_map/pallas_call | solution.py:374
  66.1 1.1 %collective-permute-done.7.rest_2_ = bf16[64,256]{1,0:T(8,128)(2,1)S(1)} collective-permute-done((bf16[64,256]{1,0:T(8,128)(2,1)S(1)}, bf16[64,256]{1,0:T(8,128)(2,1)S(1)}, u32[]{:S(2)}, u32[]{:S(2)}) %collective-permute-start.7) | collective-permute-done | bytes 32800 | tf_op jit(solution)/shard_map/ppermute | solution.py:365
  67.1 1.4 %shard_map.101 = bf16[8,5,4,16,256]{4,3,2,1,0:T(8,128)(2,1)} custom-call(s32[264]{0:T(512)S(1)} %pad_add_fusion.row_ref, bf16[256,256]{1,0:T(8,128)(2,1)S(1)} %collective-permute-done.8.rest_0_, bf16[256,256]{1,0:T(8,128)(2,1)S(1)} %collective-permute-done.10.rest_1_, bf16[8,5,4,16,256]{4,3,2,1,0:T(8,128)(2,1)} %shard_map.98.rest_2_), custom_call_target="tpu_custom_call", output_to_operand_aliasing={{}: (3, {})} | custom-call | tf_op jit(solution)/shard_map/pallas_call | solution.py:374
  68.6 5.4 %all-to-all-start.2 = ((bf16[8,5,4,16,256]{4,3,2,1,0:T(8,128)(2,1)}), bf16[8,5,4,16,256]{4,3,2,1,0:T(8,128)(2,1)S(1)}, u32[]{:S(2)}, u32[]{:S(2)}) async-start(bf16[8,5,4,16,256]{4,3,2,1,0:T(8,128)(2,1)} %shard_map.101), calls=%async_computation.2 | async-start | bytes 2621440 | tf_op jit(solution)/shard_map/all_to_all | solution.py:486
  73.9 0.0 collective-permute-start.9
  74.0 2.7 %collective-permute-start.11 = (bf16[256,256]{1,0:T(8,128)(2,1)S(1)}, bf16[256,256]{1,0:T(8,128)(2,1)S(1)}, u32[]{:S(2)}, u32[]{:S(2)}) collective-permute-start(bf16[256,256]{1,0:T(8,128)(2,1)S(1)} %collective-permute-done.10.rest_1_), channel_id=1, source_target_pairs={{0,224},{32,0},{64,32},{96,64},{128,96},{160,128},{192,160},{224,1... | collective-permute-start | bytes 393224 | tf_op jit(solution)/shard_map/ppermute | solution.py:369
  76.6 3.4 %collective-permute-done.9.rest_0_ = bf16[256,256]{1,0:T(8,128)(2,1)S(1)} collective-permute-done((bf16[256,256]{1,0:T(8,128)(2,1)S(1)}, bf16[256,256]{1,0:T(8,128)(2,1)S(1)}, u32[]{:S(2)}, u32[]{:S(2)}) %collective-permute-start.9) | collective-permute-done | bytes 131104 | tf_op jit(solution)/shard_map/ppermute | solution.py:369
  80.0 0.0 collective-permute-start.12
  80.0 5.3 %collective-permute-done.12.rest_2_ = bf16[256,256]{1,0:T(8,128)(2,1)S(1)} collective-permute-done((bf16[256,256]{1,0:T(8,128)(2,1)S(1)}, bf16[256,256]{1,0:T(8,128)(2,1)S(1)}, u32[]{:S(2)}, u32[]{:S(2)}) %collective-permute-start.12) | collective-permute-done | bytes 131104 | tf_op jit(solution)/shard_map/ppermute | solution.py:369
  85.3 0.7 shard_map.100
  86.0 2.0 %collective-permute-start.13 = (bf16[3,4,16,256]{3,2,1,0:T(8,128)(2,1)S(1)}, bf16[3,4,16,256]{3,2,1,0:T(8,128)(2,1)S(1)}, u32[]{:S(2)}, u32[]{:S(2)}) collective-permute-start(bf16[3,4,16,256]{3,2,1,0:T(8,128)(2,1)S(1)} %get-tuple-element.59), channel_id=1, source_target_pairs={{0,4},{4,0},{8,12},{12,8},{16,20},{20,16},{24,28},{28,24},{1,5},{5... | collective-permute-start | bytes 294920 | tf_op jit(solution)/shard_map/ppermute | solution.py:400
  88.0 1.4 %collective-permute-start.14 = (bf16[3,4,16,256]{3,2,1,0:T(8,128)(2,1)S(1)}, bf16[3,4,16,256]{3,2,1,0:T(8,128)(2,1)S(1)}, u32[]{:S(2)}, u32[]{:S(2)}) collective-permute-start(bf16[3,4,16,256]{3,2,1,0:T(8,128)(2,1)S(1)} %get-tuple-element.60), channel_id=1, source_target_pairs={{0,8},{4,12},{8,16},{12,20},{16,24},{20,28},{24,0},{28,4},{1,9},{5... | collective-permute-start | bytes 294920 | tf_op jit(solution)/shard_map/ppermute | solution.py:400
  89.4 1.4 %collective-permute-start.15 = (bf16[3,4,16,256]{3,2,1,0:T(8,128)(2,1)S(1)}, bf16[3,4,16,256]{3,2,1,0:T(8,128)(2,1)S(1)}, u32[]{:S(2)}, u32[]{:S(2)}) collective-permute-start(bf16[3,4,16,256]{3,2,1,0:T(8,128)(2,1)S(1)} %get-tuple-element.61), channel_id=1, source_target_pairs={{0,12},{4,8},{8,20},{12,16},{16,28},{20,24},{24,4},{28,0},{1,13},{... | collective-permute-start | bytes 294920 | tf_op jit(solution)/shard_map/ppermute | solution.py:400
  90.9 1.3 %collective-permute-start.16 = (bf16[3,4,16,256]{3,2,1,0:T(8,128)(2,1)S(1)}, bf16[3,4,16,256]{3,2,1,0:T(8,128)(2,1)S(1)}, u32[]{:S(2)}, u32[]{:S(2)}) collective-permute-start(bf16[3,4,16,256]{3,2,1,0:T(8,128)(2,1)S(1)} %get-tuple-element.62), channel_id=1, source_target_pairs={{0,16},{4,20},{8,24},{12,28},{16,0},{20,4},{24,8},{28,12},{1,17},{... | collective-permute-start | bytes 294920 | tf_op jit(solution)/shard_map/ppermute | solution.py:400
  92.2 2.0 %collective-permute-start.17 = (bf16[3,4,16,256]{3,2,1,0:T(8,128)(2,1)S(1)}, bf16[3,4,16,256]{3,2,1,0:T(8,128)(2,1)S(1)}, u32[]{:S(2)}, u32[]{:S(2)}) collective-permute-start(bf16[3,4,16,256]{3,2,1,0:T(8,128)(2,1)S(1)} %get-tuple-element.63), channel_id=1, source_target_pairs={{0,20},{4,16},{8,28},{12,24},{16,4},{20,0},{24,12},{28,8},{1,21},{... | collective-permute-start | bytes 294920 | tf_op jit(solution)/shard_map/ppermute | solution.py:400
  94.2 1.5 %collective-permute-start.18 = (bf16[3,4,16,256]{3,2,1,0:T(8,128)(2,1)S(1)}, bf16[3,4,16,256]{3,2,1,0:T(8,128)(2,1)S(1)}, u32[]{:S(2)}, u32[]{:S(2)}) collective-permute-start(bf16[3,4,16,256]{3,2,1,0:T(8,128)(2,1)S(1)} %get-tuple-element.64), channel_id=1, source_target_pairs={{0,24},{4,28},{8,0},{12,4},{16,8},{20,12},{24,16},{28,20},{1,25},{... | collective-permute-start | bytes 294920 | tf_op jit(solution)/shard_map/ppermute | solution.py:400
  95.7 0.5 collective-permute-start.19
  96.2 1.6 %shard_map.99 = (bf16[4,16,1024]{2,1,0:T(8,128)(2,1)}, f32[4,16,1024]{2,1,0:T(8,128)}) custom-call(s32[264]{0:T(512)S(1)} %concatenate.6.usage_ref, bf16[4,64,256]{2,1,0:T(8,128)(2,1)S(1)} %get-tuple-element.40.avg_ref, f32[16,1,128]{2,1,0:T(1,128)S(1)} %all_to_all.15.square_ref, bf16[2,256,256]{2,1,0:T(8,128)(2,1)S(1)} %copy-done.1, ...), custom_call_target="tpu_custom_call" | custom-call | tf_op jit(solution)/shard_map/pallas_call | solution.py:490
  97.8 0.0 all-to-all-done.2.got_ref
  97.8 1.9 %shard_map.102.rest_8_ = bf16[4,16,16,1024]{3,2,1,0:T(8,128)(2,1)} custom-call(s32[264]{0:T(512)S(1)} %pad_add_fusion.row_ref, bf16[8,5,4,16,256]{4,3,2,1,0:T(8,128)(2,1)S(1)} %all-to-all-done.2.got_ref), custom_call_target="tpu_custom_call" | custom-call | tf_op jit(solution)/shard_map/pallas_call | solution.py:406
  99.8 0.0 collective-permute-done.16.rest_4_
  99.8 1.4 %collective-permute-done.17.rest_5_ = bf16[3,4,16,256]{3,2,1,0:T(8,128)(2,1)S(1)} collective-permute-done((bf16[3,4,16,256]{3,2,1,0:T(8,128)(2,1)S(1)}, bf16[3,4,16,256]{3,2,1,0:T(8,128)(2,1)S(1)}, u32[]{:S(2)}, u32[]{:S(2)}) %collective-permute-start.17) | collective-permute-done | bytes 98336 | tf_op jit(solution)/shard_map/ppermute | solution.py:400
  101.2 1.2 %collective-permute-done.19.rest_7_ = bf16[3,4,16,256]{3,2,1,0:T(8,128)(2,1)S(1)} collective-permute-done((bf16[3,4,16,256]{3,2,1,0:T(8,128)(2,1)S(1)}, bf16[3,4,16,256]{3,2,1,0:T(8,128)(2,1)S(1)}, u32[]{:S(2)}, u32[]{:S(2)}) %collective-permute-start.19) | collective-permute-done | bytes 98336 | tf_op jit(solution)/shard_map/ppermute | solution.py:400
  102.4 1.6 %shard_map.103 = bf16[4,16,16,1024]{3,2,1,0:T(8,128)(2,1)} custom-call(s32[264]{0:T(512)S(1)} %pad_add_fusion.row_ref, bf16[3,4,16,256]{3,2,1,0:T(8,128)(2,1)S(1)} %get-tuple-element.58.rest_0_, bf16[3,4,16,256]{3,2,1,0:T(8,128)(2,1)S(1)} %collective-permute-done.13.rest_1_, ...), custom_call_target="tpu_custom_call", output_to_operand_aliasing={{}: (9, {})} | custom-call | tf_op jit(solution)/shard_map/pallas_call | solution.py:406
  (22 shorter events, 0.1 us)
Async XLA Ops:
  0.6 20.5 %copy-start = (s32[256,16]{0,1:T(8,128)S(1)}, s32[256,16]{0,1:T(8,128)}, u32[]{:S(2)}) copy-start(s32[256,16]{0,1:T(8,128)} %param.9) | copy-start | bytes 49156
  0.6 18.1 %copy-start.3 = (bf16[4,16,1024]{2,1,0:T(8,128)(2,1)S(1)}, bf16[4,16,1024]{2,1,0:T(8,128)(2,1)}, u32[]{:S(2)}) copy-start(bf16[4,16,1024]{2,1,0:T(8,128)(2,1)} %params_ref.3) | copy-start | bytes 393220
  0.7 18.1 %copy-start.2 = (f32[4,16,1024]{2,1,0:T(8,128)S(1)}, f32[4,16,1024]{2,1,0:T(8,128)}, u32[]{:S(2)}) copy-start(f32[4,16,1024]{2,1,0:T(8,128)} %momentum_ref.3) | copy-start | bytes 786436
  5.6 48.4 %copy-start.1 = (bf16[2,256,256]{2,1,0:T(8,128)(2,1)S(1)}, bf16[2,256,256]{2,1,0:T(8,128)(2,1)}, u32[]{:S(2)}) copy-start(bf16[2,256,256]{2,1,0:T(8,128)(2,1)} %constant.39.clone.table_ref) | copy-start | bytes 786436
  5.6 33.5 %all-to-all-start = ((bf16[64,40,128]{2,1,0:T(8,128)(2,1)}), bf16[64,40,128]{2,1,0:T(8,128)(2,1)S(1)}, u32[]{:S(2)}, u32[]{:S(2)}) async-start(bf16[64,40,128]{2,1,0:T(8,128)(2,1)} %bitcast.7), calls=%async_computation | async-start | bytes 1310720 | tf_op jit(solution)/shard_map/all_to_all | solution.py:454
  18.9 2.5 %collective-permute-start = (f32[64,256]{1,0:T(8,128)S(1)}, f32[64,256]{1,0:T(8,128)S(1)}, u32[]{:S(2)}, u32[]{:S(2)}) collective-permute-start(f32[64,256]{1,0:T(8,128)S(1)} %get-tuple-element.36), channel_id=1, source_target_pairs={{0,4},{4,0},{8,12},{12,8},{1,5},{5,1},{9,13},{13,9},{2,6},{6,2},{1... | collective-permute-start | bytes 196616 | tf_op jit(solution)/shard_map/ppermute | solution.py:365
  19.4 4.4 %collective-permute-start.1 = (f32[64,256]{1,0:T(8,128)S(1)}, f32[64,256]{1,0:T(8,128)S(1)}, u32[]{:S(2)}, u32[]{:S(2)}) collective-permute-start(f32[64,256]{1,0:T(8,128)S(1)} %get-tuple-element.37), channel_id=1, source_target_pairs={{0,8},{4,12},{8,0},{12,4},{1,9},{5,13},{9,1},{13,5},{2,10},{6,14},... | collective-permute-start | bytes 196616 | tf_op jit(solution)/shard_map/ppermute | solution.py:365
  20.7 6.2 %collective-permute-start.2 = (f32[64,256]{1,0:T(8,128)S(1)}, f32[64,256]{1,0:T(8,128)S(1)}, u32[]{:S(2)}, u32[]{:S(2)}) collective-permute-start(f32[64,256]{1,0:T(8,128)S(1)} %get-tuple-element.38), channel_id=1, source_target_pairs={{0,12},{4,8},{8,4},{12,0},{1,13},{5,9},{9,5},{13,1},{2,14},{6,10},... | collective-permute-start | bytes 196616 | tf_op jit(solution)/shard_map/ppermute | solution.py:365
  54.9 4.4 %collective-permute-start.4 = (bf16[256,256]{1,0:T(8,128)(2,1)S(1)}, bf16[256,256]{1,0:T(8,128)(2,1)S(1)}, u32[]{:S(2)}, u32[]{:S(2)}) collective-permute-start(bf16[256,256]{1,0:T(8,128)(2,1)S(1)} %shard_map.97.rest_0_), channel_id=1, source_target_pairs={{0,224},{32,0},{64,32},{96,64},{128,96},{160,128},{192,160},{224,1... | collective-permute-start | bytes 393224 | tf_op jit(solution)/shard_map/ppermute | solution.py:369
  55.3 5.6 %collective-permute-start.3 = (bf16[256,256]{1,0:T(8,128)(2,1)S(1)}, bf16[256,256]{1,0:T(8,128)(2,1)S(1)}, u32[]{:S(2)}, u32[]{:S(2)}) collective-permute-start(bf16[256,256]{1,0:T(8,128)(2,1)S(1)} %shard_map.97.rest_0_), channel_id=1, source_target_pairs={{0,32},{32,64},{64,96},{96,128},{128,160},{160,192},{192,224},{224... | collective-permute-start | bytes 393224 | tf_op jit(solution)/shard_map/ppermute | solution.py:369
  59.3 7.8 %collective-permute-start.10 = (bf16[256,256]{1,0:T(8,128)(2,1)S(1)}, bf16[256,256]{1,0:T(8,128)(2,1)S(1)}, u32[]{:S(2)}, u32[]{:S(2)}) collective-permute-start(bf16[256,256]{1,0:T(8,128)(2,1)S(1)} %collective-permute-done.4.rest_2_), channel_id=1, source_target_pairs={{0,224},{32,0},{64,32},{96,64},{128,96},{160,128},{192,160},{224,1... | collective-permute-start | bytes 393224 | tf_op jit(solution)/shard_map/ppermute | solution.py:369
  60.9 6.2 %collective-permute-start.8 = (bf16[256,256]{1,0:T(8,128)(2,1)S(1)}, bf16[256,256]{1,0:T(8,128)(2,1)S(1)}, u32[]{:S(2)}, u32[]{:S(2)}) collective-permute-start(bf16[256,256]{1,0:T(8,128)(2,1)S(1)} %collective-permute-done.3.rest_1_), channel_id=1, source_target_pairs={{0,32},{32,64},{64,96},{96,128},{128,160},{160,192},{192,224},{224... | collective-permute-start | bytes 393224 | tf_op jit(solution)/shard_map/ppermute | solution.py:369
  60.9 5.1 %collective-permute-start.5 = (bf16[64,256]{1,0:T(8,128)(2,1)S(1)}, bf16[64,256]{1,0:T(8,128)(2,1)S(1)}, u32[]{:S(2)}, u32[]{:S(2)}) collective-permute-start(bf16[64,256]{1,0:T(8,128)(2,1)S(1)} %get-tuple-element.50), channel_id=1, source_target_pairs={{0,4},{4,0},{8,12},{12,8},{1,5},{5,1},{9,13},{13,9},{2,6},{6,2},{1... | collective-permute-start | bytes 98312 | tf_op jit(solution)/shard_map/ppermute | solution.py:365
  62.9 3.2 %collective-permute-start.6 = (bf16[64,256]{1,0:T(8,128)(2,1)S(1)}, bf16[64,256]{1,0:T(8,128)(2,1)S(1)}, u32[]{:S(2)}, u32[]{:S(2)}) collective-permute-start(bf16[64,256]{1,0:T(8,128)(2,1)S(1)} %get-tuple-element.51), channel_id=1, source_target_pairs={{0,8},{4,12},{8,0},{12,4},{1,9},{5,13},{9,1},{13,5},{2,10},{6,14},... | collective-permute-start | bytes 98312 | tf_op jit(solution)/shard_map/ppermute | solution.py:365
  63.2 3.9 %collective-permute-start.7 = (bf16[64,256]{1,0:T(8,128)(2,1)S(1)}, bf16[64,256]{1,0:T(8,128)(2,1)S(1)}, u32[]{:S(2)}, u32[]{:S(2)}) collective-permute-start(bf16[64,256]{1,0:T(8,128)(2,1)S(1)} %get-tuple-element.52), channel_id=1, source_target_pairs={{0,12},{4,8},{8,4},{12,0},{1,13},{5,9},{9,5},{13,1},{2,14},{6,10},... | collective-permute-start | bytes 98312 | tf_op jit(solution)/shard_map/ppermute | solution.py:365
  68.6 29.3 %all-to-all-start.2 = ((bf16[8,5,4,16,256]{4,3,2,1,0:T(8,128)(2,1)}), bf16[8,5,4,16,256]{4,3,2,1,0:T(8,128)(2,1)S(1)}, u32[]{:S(2)}, u32[]{:S(2)}) async-start(bf16[8,5,4,16,256]{4,3,2,1,0:T(8,128)(2,1)} %shard_map.101), calls=%async_computation.2 | async-start | bytes 2621440 | tf_op jit(solution)/shard_map/all_to_all | solution.py:486
  73.9 6.1 %collective-permute-start.9 = (bf16[256,256]{1,0:T(8,128)(2,1)S(1)}, bf16[256,256]{1,0:T(8,128)(2,1)S(1)}, u32[]{:S(2)}, u32[]{:S(2)}) collective-permute-start(bf16[256,256]{1,0:T(8,128)(2,1)S(1)} %collective-permute-done.8.rest_0_), channel_id=1, source_target_pairs={{0,32},{32,64},{64,96},{96,128},{128,160},{160,192},{192,224},{224... | collective-permute-start | bytes 393224 | tf_op jit(solution)/shard_map/ppermute | solution.py:369
  74.0 6.1 %collective-permute-start.11 = (bf16[256,256]{1,0:T(8,128)(2,1)S(1)}, bf16[256,256]{1,0:T(8,128)(2,1)S(1)}, u32[]{:S(2)}, u32[]{:S(2)}) collective-permute-start(bf16[256,256]{1,0:T(8,128)(2,1)S(1)} %collective-permute-done.10.rest_1_), channel_id=1, source_target_pairs={{0,224},{32,0},{64,32},{96,64},{128,96},{160,128},{192,160},{224,1... | collective-permute-start | bytes 393224 | tf_op jit(solution)/shard_map/ppermute | solution.py:369
  80.0 5.3 %collective-permute-start.12 = (bf16[256,256]{1,0:T(8,128)(2,1)S(1)}, bf16[256,256]{1,0:T(8,128)(2,1)S(1)}, u32[]{:S(2)}, u32[]{:S(2)}) collective-permute-start(bf16[256,256]{1,0:T(8,128)(2,1)S(1)} %collective-permute-done.9.rest_0_), channel_id=1, source_target_pairs={{0,32},{32,64},{64,96},{96,128},{128,160},{160,192},{192,224},{224... | collective-permute-start | bytes 393224 | tf_op jit(solution)/shard_map/ppermute | solution.py:369
  86.0 8.1 %collective-permute-start.13 = (bf16[3,4,16,256]{3,2,1,0:T(8,128)(2,1)S(1)}, bf16[3,4,16,256]{3,2,1,0:T(8,128)(2,1)S(1)}, u32[]{:S(2)}, u32[]{:S(2)}) collective-permute-start(bf16[3,4,16,256]{3,2,1,0:T(8,128)(2,1)S(1)} %get-tuple-element.59), channel_id=1, source_target_pairs={{0,4},{4,0},{8,12},{12,8},{16,20},{20,16},{24,28},{28,24},{1,5},{5... | collective-permute-start | bytes 294920 | tf_op jit(solution)/shard_map/ppermute | solution.py:400
  88.0 7.6 %collective-permute-start.14 = (bf16[3,4,16,256]{3,2,1,0:T(8,128)(2,1)S(1)}, bf16[3,4,16,256]{3,2,1,0:T(8,128)(2,1)S(1)}, u32[]{:S(2)}, u32[]{:S(2)}) collective-permute-start(bf16[3,4,16,256]{3,2,1,0:T(8,128)(2,1)S(1)} %get-tuple-element.60), channel_id=1, source_target_pairs={{0,8},{4,12},{8,16},{12,20},{16,24},{20,28},{24,0},{28,4},{1,9},{5... | collective-permute-start | bytes 294920 | tf_op jit(solution)/shard_map/ppermute | solution.py:400
  89.4 10.4 %collective-permute-start.15 = (bf16[3,4,16,256]{3,2,1,0:T(8,128)(2,1)S(1)}, bf16[3,4,16,256]{3,2,1,0:T(8,128)(2,1)S(1)}, u32[]{:S(2)}, u32[]{:S(2)}) collective-permute-start(bf16[3,4,16,256]{3,2,1,0:T(8,128)(2,1)S(1)} %get-tuple-element.61), channel_id=1, source_target_pairs={{0,12},{4,8},{8,20},{12,16},{16,28},{20,24},{24,4},{28,0},{1,13},{... | collective-permute-start | bytes 294920 | tf_op jit(solution)/shard_map/ppermute | solution.py:400
  90.9 8.9 %collective-permute-start.16 = (bf16[3,4,16,256]{3,2,1,0:T(8,128)(2,1)S(1)}, bf16[3,4,16,256]{3,2,1,0:T(8,128)(2,1)S(1)}, u32[]{:S(2)}, u32[]{:S(2)}) collective-permute-start(bf16[3,4,16,256]{3,2,1,0:T(8,128)(2,1)S(1)} %get-tuple-element.62), channel_id=1, source_target_pairs={{0,16},{4,20},{8,24},{12,28},{16,0},{20,4},{24,8},{28,12},{1,17},{... | collective-permute-start | bytes 294920 | tf_op jit(solution)/shard_map/ppermute | solution.py:400
  92.2 9.1 %collective-permute-start.17 = (bf16[3,4,16,256]{3,2,1,0:T(8,128)(2,1)S(1)}, bf16[3,4,16,256]{3,2,1,0:T(8,128)(2,1)S(1)}, u32[]{:S(2)}, u32[]{:S(2)}) collective-permute-start(bf16[3,4,16,256]{3,2,1,0:T(8,128)(2,1)S(1)} %get-tuple-element.63), channel_id=1, source_target_pairs={{0,20},{4,16},{8,28},{12,24},{16,4},{20,0},{24,12},{28,8},{1,21},{... | collective-permute-start | bytes 294920 | tf_op jit(solution)/shard_map/ppermute | solution.py:400
  94.2 7.0 %collective-permute-start.18 = (bf16[3,4,16,256]{3,2,1,0:T(8,128)(2,1)S(1)}, bf16[3,4,16,256]{3,2,1,0:T(8,128)(2,1)S(1)}, u32[]{:S(2)}, u32[]{:S(2)}) collective-permute-start(bf16[3,4,16,256]{3,2,1,0:T(8,128)(2,1)S(1)} %get-tuple-element.64), channel_id=1, source_target_pairs={{0,24},{4,28},{8,0},{12,4},{16,8},{20,12},{24,16},{28,20},{1,25},{... | collective-permute-start | bytes 294920 | tf_op jit(solution)/shard_map/ppermute | solution.py:400
  95.7 6.7 %collective-permute-start.19 = (bf16[3,4,16,256]{3,2,1,0:T(8,128)(2,1)S(1)}, bf16[3,4,16,256]{3,2,1,0:T(8,128)(2,1)S(1)}, u32[]{:S(2)}, u32[]{:S(2)}) collective-permute-start(bf16[3,4,16,256]{3,2,1,0:T(8,128)(2,1)S(1)} %get-tuple-element.65), channel_id=1, source_target_pairs={{0,28},{4,24},{8,4},{12,0},{16,12},{20,8},{24,20},{28,16},{1,29},{... | collective-permute-start | bytes 294920 | tf_op jit(solution)/shard_map/ppermute | solution.py:400

commit v5 on v3

--- a/solution.py
+++ b/solution.py
@@ -31,6 +31,7 @@
 PATH = ("z", "half", "quad")
 ROW = ("half", "quad")
 DEPTH = 8
+ORDER = (0, 1, 4, 5, 2, 3, 6, 7)
 NEAR = (0, -1, 1, -2, 2)
 FAR = (-3, 3, 4)
 SQUARE_GROUP = ("quad", "shard")
@@ -211,7 +212,7 @@
                     total[rows, tile * 128 : (tile + 1) * 128] += spread
         return carry
 
-    lax.fori_loop(0, DEVICES, add, 0, unroll=16)
+    lax.fori_loop(0, DEVICES, add, 0, unroll=32)
 
     squares = []
     for o in range(OPTIONS):
@@ -262,14 +263,14 @@
 
 def pack_kernel(steps, row_ref, *rest):
     block_refs, out_refs = rest[: len(steps)], rest[len(steps) :]
-    for shift in range(8):
+    for out_ref, shift in zip(out_refs, ORDER):
         target = neighbour(row_ref[PATHS + 1], shift)
         for b, step in enumerate(steps):
             origin = (row_ref[PATHS] + (step + DEPTH)) % DEPTH
             for p in range(MINE):
                 o = row_ref[origin * 32 + target * MINE + p]
                 rows = pl.ds(pl.multiple_of(o * ROWS, ROWS), ROWS)
-                out_refs[shift][b, p] = block_refs[b][rows, :]
+                out_ref[b, p] = block_refs[b][rows, :]
 
 
 def pack_all_kernel(steps, first, row_ref, *rest):
@@ -307,11 +308,11 @@
             new_params_ref[i, :, at] = new.astype(BF16)
 
 
-def place_kernel(steps, row_ref, *rest):
-    got_refs = rest[:8]
+def place_kernel(shifts, steps, row_ref, *rest):
+    got_refs = rest[: len(shifts)]
     out_ref, sems = rest[-2:]
     copies = []
-    for shift, got_ref in enumerate(got_refs):
+    for got_ref, shift in zip(got_refs, shifts):
         source = neighbour(row_ref[PATHS + 1], 8 - (shift & 6) + (shift & 1))
         columns = pl.ds(pl.multiple_of((source & 3) * COLS, COLS), COLS)
         for b, step in enumerate(steps):
@@ -395,9 +396,9 @@
 
 def exchange_row(packed):
     got = [packed[0]]
-    for shift in range(1, 8):
+    for values, shift in zip(packed[1:], ORDER[1:]):
         pairs = [(i, neighbour(i, shift)) for i in range(8)]
-        got.append(lax.ppermute(packed[shift], ROW, pairs))
+        got.append(lax.ppermute(values, ROW, pairs))
     return got
 
 
@@ -482,11 +483,9 @@
     packed = pack_all(NEAR[:3], row, [fresh, before[1], after[1]], 0, [])
     packed, pieces = lax.optimization_barrier((packed, pieces))
     packed = pack_all(NEAR[3:], row, [before[2], after[2]], 3, [packed])
-    packed, before2, after2 = lax.optimization_barrier((packed, before[2], after[2]))
+    before2, after2 = before[2], after[2]
     near = lax.all_to_all(packed, ROW, 0, 0, tiled=True)
     before3, after3 = along(before2, 1), along(after2, -1)
-    far = exchange_row(pack_row(FAR, row, [before3, after3, along(before3, 1)]))
-
     new_params, new_momentum = call(
         owner_kernel,
         [shaped((MINE, ROWS, WIDTH), BF16), shaped((MINE, ROWS, WIDTH), F32)],
@@ -494,9 +493,12 @@
         out_specs=[vmem] * 2,
         scratch_shapes=[pltpu.VMEM((OPTIONS, 128), F32)],
     )(used, average, squares, inverse, module_params, momentum, *pieces)
+    packed = pack_row(FAR, row, [before3, after3, along(before3, 1)])
+    packed, new_params, new_momentum = lax.optimization_barrier((packed, new_params, new_momentum))
+    far = exchange_row(packed)
 
     path_params = place_row(place_all_kernel, NEAR, row, [near], [])
-    path_params = place_row(place_kernel, FAR, row, far, [path_params])
+    path_params = place_row(functools.partial(place_kernel, ORDER), FAR, row, far, [path_params])
     return (new_params, new_momentum, path_params)
 
 

time: 106 us -> 103 us (0.972)
  waiting for transfers between devices: 33.1 us -> 30.4 us
    ppermute x7, starting transfers between devices: 8.11 us -> 5.81 us  [along(): lax.ppermute(values, 'z', [(i, (i + k) % DEPTH) for i in range(DEPTH)])]
    ppermute x7, waiting for transfers between devices: 11.9 us -> 9.98 us  [along(): lax.ppermute(values, 'z', [(i, (i + k) % DEPTH) for i in range(DEPTH)])]
    ppermute x7, starting transfers between devices: 9.85 us -> 11.7 us  [exchange_row(): got.append(lax.ppermute(values, ROW, pairs))]
    all_to_all x1, starting transfers between devices: 4.33 us -> 5.4 us  [local(): near = lax.all_to_all(packed, ROW, 0, 0, tiled=True)]
  transfers between devices with their start and end apart: 22 -> 22, of which waited for: 9 -> 8; matrix products, arithmetic and copies ran while one was open for 0% -> 0% of each run, Pallas kernels for 6% -> 6%
where the time goes in v5:
time: 103 us
  starting transfers between devices  41.9 us (41%)
  waiting for transfers between devices  30.4 us (30%)
  Pallas kernels  18.2 us (18%)
  blocking collectives  11.2 us (11%)
    all_to_all x1, starting transfers between devices, local(): lax.all_to_all(outgoing.reshape(DEVICES, SENT, 128), PATH, 0, 0, tiled=True)  13.1 us
    all_to_all x1, waiting for transfers between devices, local(): lax.all_to_all(outgoing.reshape(DEVICES, SENT, 128), PATH, 0, 0, tiled=True)  12.3 us
    ppermute x7, starting transfers between devices, exchange_row(): got.append(lax.ppermute(values, ROW, pairs))  11.7 us
    all_to_all x1, blocking collectives, local(): squares = lax.all_to_all(squares, SQUARE_GROUP, 0, 0, tiled=True)  11.2 us
    ppermute x7, waiting for transfers between devices, along(): lax.ppermute(values, 'z', [(i, (i + k) % DEPTH) for i in range(DEPTH)])  9.98 us
    ppermute x6, waiting for transfers between devices, swap(): return lax.ppermute(values, 'quad', [(i, i ^ k) for i in range(QUAD)])  6.59 us
    ppermute x6, starting transfers between devices, swap(): return lax.ppermute(values, 'quad', [(i, i ^ k) for i in range(QUAD)])  5.89 us
    ppermute x7, starting transfers between devices, along(): lax.ppermute(values, 'z', [(i, (i + k) % DEPTH) for i in range(DEPTH)])  5.81 us
  transfers between devices with their start and end apart: 22, of which 8 were waited for; matrix products, arithmetic and copies ran while one was open for 0% of the time, Pallas kernels for 6%

profile of v5, /device:TPU:1, one launch (start us, length us, event | category | flops | bytes accessed | tf_op | source)
XLA Modules:
  0.0 102.9 jit_solution(11697256671993196802)
XLA Ops:
  0.6 0.0 copy-start
  0.7 5.0 %shard_map.94 = bf16[16,4,40,128]{3,2,1,0:T(8,128)(2,1)} custom-call(bf16[4,16,16,1024]{3,2,1,0:T(8,128)(2,1)} %grad_any.1, s32[4,16,16,16]{3,2,1,0:T(8,128)} %kept_any.1, bf16[2,256,256]{2,1,0:T(8,128)(2,1)} %constant.38.clone.table_any), custom_call_target="tpu_custom_call" | custom-call | tf_op jit(solution)/shard_map/pallas_call | solution.py:439
  5.6 0.0 copy-start.1
  5.6 13.1 %all-to-all-start = ((bf16[64,40,128]{2,1,0:T(8,128)(2,1)}), bf16[64,40,128]{2,1,0:T(8,128)(2,1)S(1)}, u32[]{:S(2)}, u32[]{:S(2)}) async-start(bf16[64,40,128]{2,1,0:T(8,128)(2,1)} %bitcast.7), calls=%async_computation | async-start | bytes 1310720 | tf_op jit(solution)/shard_map/all_to_all | solution.py:455
  18.8 0.5 collective-permute-start
  19.4 1.3 %collective-permute-start.1 = (f32[64,256]{1,0:T(8,128)S(1)}, f32[64,256]{1,0:T(8,128)S(1)}, u32[]{:S(2)}, u32[]{:S(2)}) collective-permute-start(f32[64,256]{1,0:T(8,128)S(1)} %get-tuple-element.47), channel_id=1, source_target_pairs={{0,8},{4,12},{8,0},{12,4},{1,9},{5,13},{9,1},{13,5},{2,10},{6,14},... | collective-permute-start | bytes 196616 | tf_op jit(solution)/shard_map/ppermute | solution.py:366
  20.7 0.4 collective-permute-start.2
  21.1 0.1 constant_dynamic-slice_fusion.2
  21.2 0.1 reshape.20
  21.3 2.4 %collective-permute-done.1.rest_2_ = f32[64,256]{1,0:T(8,128)S(1)} collective-permute-done((f32[64,256]{1,0:T(8,128)S(1)}, f32[64,256]{1,0:T(8,128)S(1)}, u32[]{:S(2)}, u32[]{:S(2)}) %collective-permute-start.1) | collective-permute-done | bytes 65568 | tf_op jit(solution)/shard_map/ppermute | solution.py:366
  23.7 3.1 %collective-permute-done.2.rest_3_ = f32[64,256]{1,0:T(8,128)S(1)} collective-permute-done((f32[64,256]{1,0:T(8,128)S(1)}, f32[64,256]{1,0:T(8,128)S(1)}, u32[]{:S(2)}, u32[]{:S(2)}) %collective-permute-start.2) | collective-permute-done | bytes 65568 | tf_op jit(solution)/shard_map/ppermute | solution.py:366
  26.9 12.3 %all-to-all-done.got_ref = bf16[64,40,128]{2,1,0:T(8,128)(2,1)S(1)} async-done(((bf16[64,40,128]{2,1,0:T(8,128)(2,1)}), bf16[64,40,128]{2,1,0:T(8,128)(2,1)S(1)}, u32[]{:S(2)}, u32[]{:S(2)}) %all-to-all-start) | async-done | bytes 655392 | tf_op jit(solution)/shard_map/all_to_all | solution.py:455
  39.1 3.5 %shard_map.96 = (bf16[4,64,256]{2,1,0:T(8,128)(2,1)S(1)}, f32[16,1,128]{2,1,0:T(1,128)S(1)}, bf16[64,256]{1,0:T(8,128)(2,1)S(1)}, bf16[64,256]{1,0:T(8,128)(2,1)S(1)}, bf16[64,256]{1,0:T(8,128)(2,1)S(1)}) custom-call(s32[264]{0:T(512)S(1)} %concatenate.7.usage_ref, bf16[64,40,128]{2,1,0:T(8,128)(2,1)S(1)} %all-to-all-done.got_ref), custom_call_target="tpu_custom_call" | custom-call | tf_op jit(solution)/shard_map/pallas_call | solution.py:458
  42.6 11.2 %all_to_all.15.square_ref = f32[16,1,128]{2,1,0:T(1,128)S(1)} all-to-all(f32[16,1,128]{2,1,0:T(1,128)S(1)} %get-tuple-element.52), channel_id=1, replica_groups=mesh['z'=8,'half'=2,'quad'=4,'shard'=4] {'quad','shard'}, dimensions={0} | all-to-all | bytes 16384 | tf_op jit(solution)/shard_map/all_to_all | solution.py:468
  53.9 0.9 shard_map.97.rest_0_
  54.7 0.5 collective-permute-start.6
  55.2 1.1 %collective-permute-start.3 = (bf16[256,256]{1,0:T(8,128)(2,1)S(1)}, bf16[256,256]{1,0:T(8,128)(2,1)S(1)}, u32[]{:S(2)}, u32[]{:S(2)}) collective-permute-start(bf16[256,256]{1,0:T(8,128)(2,1)S(1)} %shard_map.97.rest_0_), channel_id=1, source_target_pairs={{0,32},{32,64},{64,96},{96,128},{128,160},{160,192},{192,224},{224... | collective-permute-start | bytes 393224 | tf_op jit(solution)/shard_map/ppermute | solution.py:370
  56.3 2.9 %collective-permute-done.6.rest_2_ = bf16[256,256]{1,0:T(8,128)(2,1)S(1)} collective-permute-done((bf16[256,256]{1,0:T(8,128)(2,1)S(1)}, bf16[256,256]{1,0:T(8,128)(2,1)S(1)}, u32[]{:S(2)}, u32[]{:S(2)}) %collective-permute-start.6) | collective-permute-done | bytes 131104 | tf_op jit(solution)/shard_map/ppermute | solution.py:370
  59.2 1.6 %collective-permute-start.7 = (bf16[256,256]{1,0:T(8,128)(2,1)S(1)}, bf16[256,256]{1,0:T(8,128)(2,1)S(1)}, u32[]{:S(2)}, u32[]{:S(2)}) collective-permute-start(bf16[256,256]{1,0:T(8,128)(2,1)S(1)} %collective-permute-done.6.rest_2_), channel_id=1, source_target_pairs={{0,224},{32,0},{64,32},{96,64},{128,96},{160,128},{192,160},{224,1... | collective-permute-start | bytes 393224 | tf_op jit(solution)/shard_map/ppermute | solution.py:370
  60.8 0.0 collective-permute-done.3.rest_1_
  60.8 0.0 collective-permute-start.4
  60.8 2.0 %collective-permute-start.10 = (bf16[64,256]{1,0:T(8,128)(2,1)S(1)}, bf16[64,256]{1,0:T(8,128)(2,1)S(1)}, u32[]{:S(2)}, u32[]{:S(2)}) collective-permute-start(bf16[64,256]{1,0:T(8,128)(2,1)S(1)} %get-tuple-element.68), channel_id=1, source_target_pairs={{0,4},{4,0},{8,12},{12,8},{1,5},{5,1},{9,13},{13,9},{2,6},{6,2},{1... | collective-permute-start | bytes 98312 | tf_op jit(solution)/shard_map/ppermute | solution.py:366
  62.8 0.3 collective-permute-start.11
  63.1 1.3 %collective-permute-start.12 = (bf16[64,256]{1,0:T(8,128)(2,1)S(1)}, bf16[64,256]{1,0:T(8,128)(2,1)S(1)}, u32[]{:S(2)}, u32[]{:S(2)}) collective-permute-start(bf16[64,256]{1,0:T(8,128)(2,1)S(1)} %get-tuple-element.70), channel_id=1, source_target_pairs={{0,12},{4,8},{8,4},{12,0},{1,13},{5,9},{9,5},{13,1},{2,14},{6,10},... | collective-permute-start | bytes 98312 | tf_op jit(solution)/shard_map/ppermute | solution.py:366
  64.4 1.5 %shard_map.99.rest_2_ = bf16[8,5,4,16,256]{4,3,2,1,0:T(8,128)(2,1)} custom-call(s32[264]{0:T(512)S(1)} %pad_add_fusion.row_ref, bf16[256,256]{1,0:T(8,128)(2,1)S(1)} %shard_map.97.rest_0_, bf16[256,256]{1,0:T(8,128)(2,1)S(1)} %collective-permute-done.3.rest_1_, bf16[256,256]{1,0:T(8,128)(2,1)S(1)} %collective-permute-done.6.rest_2_), custom_call_target="tpu_custom_call" | custom-call | tf_op jit(solution)/shard_map/pallas_call | solution.py:375
  65.9 0.0 collective-permute-done.10.rest_0_
  65.9 0.0 collective-permute-done.11.rest_1_
  65.9 1.1 %collective-permute-done.12.rest_2_ = bf16[64,256]{1,0:T(8,128)(2,1)S(1)} collective-permute-done((bf16[64,256]{1,0:T(8,128)(2,1)S(1)}, bf16[64,256]{1,0:T(8,128)(2,1)S(1)}, u32[]{:S(2)}, u32[]{:S(2)}) %collective-permute-start.12) | collective-permute-done | bytes 32800 | tf_op jit(solution)/shard_map/ppermute | solution.py:366
  67.0 0.0 collective-permute-done.7.rest_1_
  67.0 0.0 collective-permute-done.4.rest_0_
  67.0 1.4 %shard_map.101 = bf16[8,5,4,16,256]{4,3,2,1,0:T(8,128)(2,1)} custom-call(s32[264]{0:T(512)S(1)} %pad_add_fusion.row_ref, bf16[256,256]{1,0:T(8,128)(2,1)S(1)} %collective-permute-done.4.rest_0_, bf16[256,256]{1,0:T(8,128)(2,1)S(1)} %collective-permute-done.7.rest_1_, bf16[8,5,4,16,256]{4,3,2,1,0:T(8,128)(2,1)} %shard_map.99.rest_2_), custom_call_target="tpu_custom_call", output_to_operand_aliasing={{}: (3, {})} | custom-call | tf_op jit(solution)/shard_map/pallas_call | solution.py:375
  68.4 5.4 %all-to-all-start.2 = ((bf16[8,5,4,16,256]{4,3,2,1,0:T(8,128)(2,1)}), bf16[8,5,4,16,256]{4,3,2,1,0:T(8,128)(2,1)S(1)}, u32[]{:S(2)}, u32[]{:S(2)}) async-start(bf16[8,5,4,16,256]{4,3,2,1,0:T(8,128)(2,1)} %shard_map.101), calls=%async_computation.2 | async-start | bytes 2621440 | tf_op jit(solution)/shard_map/all_to_all | solution.py:487
  73.8 0.0 collective-permute-start.5
  73.8 2.7 %collective-permute-start.8 = (bf16[256,256]{1,0:T(8,128)(2,1)S(1)}, bf16[256,256]{1,0:T(8,128)(2,1)S(1)}, u32[]{:S(2)}, u32[]{:S(2)}) collective-permute-start(bf16[256,256]{1,0:T(8,128)(2,1)S(1)} %collective-permute-done.7.rest_1_), channel_id=1, source_target_pairs={{0,224},{32,0},{64,32},{96,64},{128,96},{160,128},{192,160},{224,1... | collective-permute-start | bytes 393224 | tf_op jit(solution)/shard_map/ppermute | solution.py:370
  76.5 3.4 %collective-permute-done.5.rest_0_ = bf16[256,256]{1,0:T(8,128)(2,1)S(1)} collective-permute-done((bf16[256,256]{1,0:T(8,128)(2,1)S(1)}, bf16[256,256]{1,0:T(8,128)(2,1)S(1)}, u32[]{:S(2)}, u32[]{:S(2)}) %collective-permute-start.5) | collective-permute-done | bytes 131104 | tf_op jit(solution)/shard_map/ppermute | solution.py:370
  79.9 1.6 %shard_map.100 = (bf16[4,16,1024]{2,1,0:T(8,128)(2,1)}, f32[4,16,1024]{2,1,0:T(8,128)}) custom-call(s32[264]{0:T(512)S(1)} %concatenate.7.usage_ref, bf16[4,64,256]{2,1,0:T(8,128)(2,1)S(1)} %get-tuple-element.51.avg_ref, f32[16,1,128]{2,1,0:T(1,128)S(1)} %all_to_all.15.square_ref, bf16[2,256,256]{2,1,0:T(8,128)(2,1)S(1)} %copy-done.1, ...), custom_call_target="tpu_custom_call" | custom-call | tf_op jit(solution)/shard_map/pallas_call | solution.py:489
  81.5 3.7 %collective-permute-done.9.rest_2_ = bf16[256,256]{1,0:T(8,128)(2,1)S(1)} collective-permute-done((bf16[256,256]{1,0:T(8,128)(2,1)S(1)}, bf16[256,256]{1,0:T(8,128)(2,1)S(1)}, u32[]{:S(2)}, u32[]{:S(2)}) %collective-permute-start.9) | collective-permute-done | bytes 131104 | tf_op jit(solution)/shard_map/ppermute | solution.py:370
  85.2 0.7 shard_map.98
  85.9 2.0 %collective-permute-start.13 = (bf16[3,4,16,256]{3,2,1,0:T(8,128)(2,1)S(1)}, bf16[3,4,16,256]{3,2,1,0:T(8,128)(2,1)S(1)}, u32[]{:S(2)}, u32[]{:S(2)}) collective-permute-start(bf16[3,4,16,256]{3,2,1,0:T(8,128)(2,1)S(1)} %get-tuple-element.79), channel_id=1, source_target_pairs={{0,4},{4,0},{8,12},{12,8},{16,20},{20,16},{24,28},{28,24},{1,5},{5... | collective-permute-start | bytes 294920 | tf_op jit(solution)/shard_map/ppermute | solution.py:401
  87.9 2.9 %collective-permute-start.14 = (bf16[3,4,16,256]{3,2,1,0:T(8,128)(2,1)S(1)}, bf16[3,4,16,256]{3,2,1,0:T(8,128)(2,1)S(1)}, u32[]{:S(2)}, u32[]{:S(2)}) collective-permute-start(bf16[3,4,16,256]{3,2,1,0:T(8,128)(2,1)S(1)} %get-tuple-element.80), channel_id=1, source_target_pairs={{0,16},{4,20},{8,24},{12,28},{16,0},{20,4},{24,8},{28,12},{1,17},{... | collective-permute-start | bytes 294920 | tf_op jit(solution)/shard_map/ppermute | solution.py:401
  90.8 0.3 collective-permute-start.15
  91.1 1.4 %collective-permute-start.16 = (bf16[3,4,16,256]{3,2,1,0:T(8,128)(2,1)S(1)}, bf16[3,4,16,256]{3,2,1,0:T(8,128)(2,1)S(1)}, u32[]{:S(2)}, u32[]{:S(2)}) collective-permute-start(bf16[3,4,16,256]{3,2,1,0:T(8,128)(2,1)S(1)} %get-tuple-element.82), channel_id=1, source_target_pairs={{0,8},{4,12},{8,16},{12,20},{16,24},{20,28},{24,0},{28,4},{1,9},{5... | collective-permute-start | bytes 294920 | tf_op jit(solution)/shard_map/ppermute | solution.py:401
  92.5 1.5 %collective-permute-start.17 = (bf16[3,4,16,256]{3,2,1,0:T(8,128)(2,1)S(1)}, bf16[3,4,16,256]{3,2,1,0:T(8,128)(2,1)S(1)}, u32[]{:S(2)}, u32[]{:S(2)}) collective-permute-start(bf16[3,4,16,256]{3,2,1,0:T(8,128)(2,1)S(1)} %get-tuple-element.83), channel_id=1, source_target_pairs={{0,12},{4,8},{8,20},{12,16},{16,28},{20,24},{24,4},{28,0},{1,13},{... | collective-permute-start | bytes 294920 | tf_op jit(solution)/shard_map/ppermute | solution.py:401
  94.0 1.5 %collective-permute-start.18 = (bf16[3,4,16,256]{3,2,1,0:T(8,128)(2,1)S(1)}, bf16[3,4,16,256]{3,2,1,0:T(8,128)(2,1)S(1)}, u32[]{:S(2)}, u32[]{:S(2)}) collective-permute-start(bf16[3,4,16,256]{3,2,1,0:T(8,128)(2,1)S(1)} %get-tuple-element.84), channel_id=1, source_target_pairs={{0,24},{4,28},{8,0},{12,4},{16,8},{20,12},{24,16},{28,20},{1,25},{... | collective-permute-start | bytes 294920 | tf_op jit(solution)/shard_map/ppermute | solution.py:401
  95.5 2.1 %collective-permute-start.19 = (bf16[3,4,16,256]{3,2,1,0:T(8,128)(2,1)S(1)}, bf16[3,4,16,256]{3,2,1,0:T(8,128)(2,1)S(1)}, u32[]{:S(2)}, u32[]{:S(2)}) collective-permute-start(bf16[3,4,16,256]{3,2,1,0:T(8,128)(2,1)S(1)} %get-tuple-element.85), channel_id=1, source_target_pairs={{0,28},{4,24},{8,4},{12,0},{16,12},{20,8},{24,20},{28,16},{1,29},{... | collective-permute-start | bytes 294920 | tf_op jit(solution)/shard_map/ppermute | solution.py:401
  97.6 1.9 %shard_map.102.rest_8_ = bf16[4,16,16,1024]{3,2,1,0:T(8,128)(2,1)} custom-call(s32[264]{0:T(512)S(1)} %pad_add_fusion.row_ref, bf16[8,5,4,16,256]{4,3,2,1,0:T(8,128)(2,1)S(1)} %all-to-all-done.2.got_ref), custom_call_target="tpu_custom_call" | custom-call | tf_op jit(solution)/shard_map/pallas_call | solution.py:407
  99.6 1.5 %collective-permute-done.17.rest_5_ = bf16[3,4,16,256]{3,2,1,0:T(8,128)(2,1)S(1)} collective-permute-done((bf16[3,4,16,256]{3,2,1,0:T(8,128)(2,1)S(1)}, bf16[3,4,16,256]{3,2,1,0:T(8,128)(2,1)S(1)}, u32[]{:S(2)}, u32[]{:S(2)}) %collective-permute-start.17) | collective-permute-done | bytes 98336 | tf_op jit(solution)/shard_map/ppermute | solution.py:401
  101.1 1.6 %shard_map.103 = bf16[4,16,16,1024]{3,2,1,0:T(8,128)(2,1)} custom-call(s32[264]{0:T(512)S(1)} %pad_add_fusion.row_ref, bf16[3,4,16,256]{3,2,1,0:T(8,128)(2,1)S(1)} %get-tuple-element.78.rest_0_, bf16[3,4,16,256]{3,2,1,0:T(8,128)(2,1)S(1)} %collective-permute-done.13.rest_1_, ...), custom_call_target="tpu_custom_call", output_to_operand_aliasing={{}: (9, {})} | custom-call | tf_op jit(solution)/shard_map/pallas_call | solution.py:407
  (22 shorter events, 0.1 us)
Async XLA Ops:
  0.6 20.5 %copy-start = (s32[256,16]{0,1:T(8,128)S(1)}, s32[256,16]{0,1:T(8,128)}, u32[]{:S(2)}) copy-start(s32[256,16]{0,1:T(8,128)} %param.9) | copy-start | bytes 49156
  0.6 18.1 %copy-start.2 = (f32[4,16,1024]{2,1,0:T(8,128)S(1)}, f32[4,16,1024]{2,1,0:T(8,128)}, u32[]{:S(2)}) copy-start(f32[4,16,1024]{2,1,0:T(8,128)} %momentum_ref.3) | copy-start | bytes 786436
  0.7 18.1 %copy-start.3 = (bf16[4,16,1024]{2,1,0:T(8,128)(2,1)S(1)}, bf16[4,16,1024]{2,1,0:T(8,128)(2,1)}, u32[]{:S(2)}) copy-start(bf16[4,16,1024]{2,1,0:T(8,128)(2,1)} %params_ref.3) | copy-start | bytes 393220
  5.6 48.2 %copy-start.1 = (bf16[2,256,256]{2,1,0:T(8,128)(2,1)S(1)}, bf16[2,256,256]{2,1,0:T(8,128)(2,1)}, u32[]{:S(2)}) copy-start(bf16[2,256,256]{2,1,0:T(8,128)(2,1)} %constant.39.clone.table_ref) | copy-start | bytes 786436
  5.6 33.5 %all-to-all-start = ((bf16[64,40,128]{2,1,0:T(8,128)(2,1)}), bf16[64,40,128]{2,1,0:T(8,128)(2,1)S(1)}, u32[]{:S(2)}, u32[]{:S(2)}) async-start(bf16[64,40,128]{2,1,0:T(8,128)(2,1)} %bitcast.7), calls=%async_computation | async-start | bytes 1310720 | tf_op jit(solution)/shard_map/all_to_all | solution.py:455
  18.8 2.5 %collective-permute-start = (f32[64,256]{1,0:T(8,128)S(1)}, f32[64,256]{1,0:T(8,128)S(1)}, u32[]{:S(2)}, u32[]{:S(2)}) collective-permute-start(f32[64,256]{1,0:T(8,128)S(1)} %get-tuple-element.46), channel_id=1, source_target_pairs={{0,4},{4,0},{8,12},{12,8},{1,5},{5,1},{9,13},{13,9},{2,6},{6,2},{1... | collective-permute-start | bytes 196616 | tf_op jit(solution)/shard_map/ppermute | solution.py:366
  19.4 4.4 %collective-permute-start.1 = (f32[64,256]{1,0:T(8,128)S(1)}, f32[64,256]{1,0:T(8,128)S(1)}, u32[]{:S(2)}, u32[]{:S(2)}) collective-permute-start(f32[64,256]{1,0:T(8,128)S(1)} %get-tuple-element.47), channel_id=1, source_target_pairs={{0,8},{4,12},{8,0},{12,4},{1,9},{5,13},{9,1},{13,5},{2,10},{6,14},... | collective-permute-start | bytes 196616 | tf_op jit(solution)/shard_map/ppermute | solution.py:366
  20.7 6.2 %collective-permute-start.2 = (f32[64,256]{1,0:T(8,128)S(1)}, f32[64,256]{1,0:T(8,128)S(1)}, u32[]{:S(2)}, u32[]{:S(2)}) collective-permute-start(f32[64,256]{1,0:T(8,128)S(1)} %get-tuple-element.48), channel_id=1, source_target_pairs={{0,12},{4,8},{8,4},{12,0},{1,13},{5,9},{9,5},{13,1},{2,14},{6,10},... | collective-permute-start | bytes 196616 | tf_op jit(solution)/shard_map/ppermute | solution.py:366
  54.7 4.4 %collective-permute-start.6 = (bf16[256,256]{1,0:T(8,128)(2,1)S(1)}, bf16[256,256]{1,0:T(8,128)(2,1)S(1)}, u32[]{:S(2)}, u32[]{:S(2)}) collective-permute-start(bf16[256,256]{1,0:T(8,128)(2,1)S(1)} %shard_map.97.rest_0_), channel_id=1, source_target_pairs={{0,224},{32,0},{64,32},{96,64},{128,96},{160,128},{192,160},{224,1... | collective-permute-start | bytes 393224 | tf_op jit(solution)/shard_map/ppermute | solution.py:370
  55.2 5.6 %collective-permute-start.3 = (bf16[256,256]{1,0:T(8,128)(2,1)S(1)}, bf16[256,256]{1,0:T(8,128)(2,1)S(1)}, u32[]{:S(2)}, u32[]{:S(2)}) collective-permute-start(bf16[256,256]{1,0:T(8,128)(2,1)S(1)} %shard_map.97.rest_0_), channel_id=1, source_target_pairs={{0,32},{32,64},{64,96},{96,128},{128,160},{160,192},{192,224},{224... | collective-permute-start | bytes 393224 | tf_op jit(solution)/shard_map/ppermute | solution.py:370
  59.2 7.8 %collective-permute-start.7 = (bf16[256,256]{1,0:T(8,128)(2,1)S(1)}, bf16[256,256]{1,0:T(8,128)(2,1)S(1)}, u32[]{:S(2)}, u32[]{:S(2)}) collective-permute-start(bf16[256,256]{1,0:T(8,128)(2,1)S(1)} %collective-permute-done.6.rest_2_), channel_id=1, source_target_pairs={{0,224},{32,0},{64,32},{96,64},{128,96},{160,128},{192,160},{224,1... | collective-permute-start | bytes 393224 | tf_op jit(solution)/shard_map/ppermute | solution.py:370
  60.8 6.2 %collective-permute-start.4 = (bf16[256,256]{1,0:T(8,128)(2,1)S(1)}, bf16[256,256]{1,0:T(8,128)(2,1)S(1)}, u32[]{:S(2)}, u32[]{:S(2)}) collective-permute-start(bf16[256,256]{1,0:T(8,128)(2,1)S(1)} %collective-permute-done.3.rest_1_), channel_id=1, source_target_pairs={{0,32},{32,64},{64,96},{96,128},{128,160},{160,192},{192,224},{224... | collective-permute-start | bytes 393224 | tf_op jit(solution)/shard_map/ppermute | solution.py:370
  60.8 5.1 %collective-permute-start.10 = (bf16[64,256]{1,0:T(8,128)(2,1)S(1)}, bf16[64,256]{1,0:T(8,128)(2,1)S(1)}, u32[]{:S(2)}, u32[]{:S(2)}) collective-permute-start(bf16[64,256]{1,0:T(8,128)(2,1)S(1)} %get-tuple-element.68), channel_id=1, source_target_pairs={{0,4},{4,0},{8,12},{12,8},{1,5},{5,1},{9,13},{13,9},{2,6},{6,2},{1... | collective-permute-start | bytes 98312 | tf_op jit(solution)/shard_map/ppermute | solution.py:366
  62.8 3.2 %collective-permute-start.11 = (bf16[64,256]{1,0:T(8,128)(2,1)S(1)}, bf16[64,256]{1,0:T(8,128)(2,1)S(1)}, u32[]{:S(2)}, u32[]{:S(2)}) collective-permute-start(bf16[64,256]{1,0:T(8,128)(2,1)S(1)} %get-tuple-element.69), channel_id=1, source_target_pairs={{0,8},{4,12},{8,0},{12,4},{1,9},{5,13},{9,1},{13,5},{2,10},{6,14},... | collective-permute-start | bytes 98312 | tf_op jit(solution)/shard_map/ppermute | solution.py:366
  63.1 3.9 %collective-permute-start.12 = (bf16[64,256]{1,0:T(8,128)(2,1)S(1)}, bf16[64,256]{1,0:T(8,128)(2,1)S(1)}, u32[]{:S(2)}, u32[]{:S(2)}) collective-permute-start(bf16[64,256]{1,0:T(8,128)(2,1)S(1)} %get-tuple-element.70), channel_id=1, source_target_pairs={{0,12},{4,8},{8,4},{12,0},{1,13},{5,9},{9,5},{13,1},{2,14},{6,10},... | collective-permute-start | bytes 98312 | tf_op jit(solution)/shard_map/ppermute | solution.py:366
  68.4 29.2 %all-to-all-start.2 = ((bf16[8,5,4,16,256]{4,3,2,1,0:T(8,128)(2,1)}), bf16[8,5,4,16,256]{4,3,2,1,0:T(8,128)(2,1)S(1)}, u32[]{:S(2)}, u32[]{:S(2)}) async-start(bf16[8,5,4,16,256]{4,3,2,1,0:T(8,128)(2,1)} %shard_map.101), calls=%async_computation.2 | async-start | bytes 2621440 | tf_op jit(solution)/shard_map/all_to_all | solution.py:487
  73.8 6.1 %collective-permute-start.5 = (bf16[256,256]{1,0:T(8,128)(2,1)S(1)}, bf16[256,256]{1,0:T(8,128)(2,1)S(1)}, u32[]{:S(2)}, u32[]{:S(2)}) collective-permute-start(bf16[256,256]{1,0:T(8,128)(2,1)S(1)} %collective-permute-done.4.rest_0_), channel_id=1, source_target_pairs={{0,32},{32,64},{64,96},{96,128},{128,160},{160,192},{192,224},{224... | collective-permute-start | bytes 393224 | tf_op jit(solution)/shard_map/ppermute | solution.py:370
  73.8 7.7 %collective-permute-start.8 = (bf16[256,256]{1,0:T(8,128)(2,1)S(1)}, bf16[256,256]{1,0:T(8,128)(2,1)S(1)}, u32[]{:S(2)}, u32[]{:S(2)}) collective-permute-start(bf16[256,256]{1,0:T(8,128)(2,1)S(1)} %collective-permute-done.7.rest_1_), channel_id=1, source_target_pairs={{0,224},{32,0},{64,32},{96,64},{128,96},{160,128},{192,160},{224,1... | collective-permute-start | bytes 393224 | tf_op jit(solution)/shard_map/ppermute | solution.py:370
  79.9 5.3 %collective-permute-start.9 = (bf16[256,256]{1,0:T(8,128)(2,1)S(1)}, bf16[256,256]{1,0:T(8,128)(2,1)S(1)}, u32[]{:S(2)}, u32[]{:S(2)}) collective-permute-start(bf16[256,256]{1,0:T(8,128)(2,1)S(1)} %collective-permute-done.5.rest_0_), channel_id=1, source_target_pairs={{0,32},{32,64},{64,96},{96,128},{128,160},{160,192},{192,224},{224... | collective-permute-start | bytes 393224 | tf_op jit(solution)/shard_map/ppermute | solution.py:370
  85.9 8.1 %collective-permute-start.13 = (bf16[3,4,16,256]{3,2,1,0:T(8,128)(2,1)S(1)}, bf16[3,4,16,256]{3,2,1,0:T(8,128)(2,1)S(1)}, u32[]{:S(2)}, u32[]{:S(2)}) collective-permute-start(bf16[3,4,16,256]{3,2,1,0:T(8,128)(2,1)S(1)} %get-tuple-element.79), channel_id=1, source_target_pairs={{0,4},{4,0},{8,12},{12,8},{16,20},{20,16},{24,28},{28,24},{1,5},{5... | collective-permute-start | bytes 294920 | tf_op jit(solution)/shard_map/ppermute | solution.py:401
  87.9 7.6 %collective-permute-start.14 = (bf16[3,4,16,256]{3,2,1,0:T(8,128)(2,1)S(1)}, bf16[3,4,16,256]{3,2,1,0:T(8,128)(2,1)S(1)}, u32[]{:S(2)}, u32[]{:S(2)}) collective-permute-start(bf16[3,4,16,256]{3,2,1,0:T(8,128)(2,1)S(1)} %get-tuple-element.80), channel_id=1, source_target_pairs={{0,16},{4,20},{8,24},{12,28},{16,0},{20,4},{24,8},{28,12},{1,17},{... | collective-permute-start | bytes 294920 | tf_op jit(solution)/shard_map/ppermute | solution.py:401
  90.8 8.7 %collective-permute-start.15 = (bf16[3,4,16,256]{3,2,1,0:T(8,128)(2,1)S(1)}, bf16[3,4,16,256]{3,2,1,0:T(8,128)(2,1)S(1)}, u32[]{:S(2)}, u32[]{:S(2)}) collective-permute-start(bf16[3,4,16,256]{3,2,1,0:T(8,128)(2,1)S(1)} %get-tuple-element.81), channel_id=1, source_target_pairs={{0,20},{4,16},{8,28},{12,24},{16,4},{20,0},{24,12},{28,8},{1,21},{... | collective-permute-start | bytes 294920 | tf_op jit(solution)/shard_map/ppermute | solution.py:401
  91.1 8.4 %collective-permute-start.16 = (bf16[3,4,16,256]{3,2,1,0:T(8,128)(2,1)S(1)}, bf16[3,4,16,256]{3,2,1,0:T(8,128)(2,1)S(1)}, u32[]{:S(2)}, u32[]{:S(2)}) collective-permute-start(bf16[3,4,16,256]{3,2,1,0:T(8,128)(2,1)S(1)} %get-tuple-element.82), channel_id=1, source_target_pairs={{0,8},{4,12},{8,16},{12,20},{16,24},{20,28},{24,0},{28,4},{1,9},{5... | collective-permute-start | bytes 294920 | tf_op jit(solution)/shard_map/ppermute | solution.py:401
  92.5 8.6 %collective-permute-start.17 = (bf16[3,4,16,256]{3,2,1,0:T(8,128)(2,1)S(1)}, bf16[3,4,16,256]{3,2,1,0:T(8,128)(2,1)S(1)}, u32[]{:S(2)}, u32[]{:S(2)}) collective-permute-start(bf16[3,4,16,256]{3,2,1,0:T(8,128)(2,1)S(1)} %get-tuple-element.83), channel_id=1, source_target_pairs={{0,12},{4,8},{8,20},{12,16},{16,28},{20,24},{24,4},{28,0},{1,13},{... | collective-permute-start | bytes 294920 | tf_op jit(solution)/shard_map/ppermute | solution.py:401
  94.0 7.0 %collective-permute-start.18 = (bf16[3,4,16,256]{3,2,1,0:T(8,128)(2,1)S(1)}, bf16[3,4,16,256]{3,2,1,0:T(8,128)(2,1)S(1)}, u32[]{:S(2)}, u32[]{:S(2)}) collective-permute-start(bf16[3,4,16,256]{3,2,1,0:T(8,128)(2,1)S(1)} %get-tuple-element.84), channel_id=1, source_target_pairs={{0,24},{4,28},{8,0},{12,4},{16,8},{20,12},{24,16},{28,20},{1,25},{... | collective-permute-start | bytes 294920 | tf_op jit(solution)/shard_map/ppermute | solution.py:401
  95.5 5.6 %collective-permute-start.19 = (bf16[3,4,16,256]{3,2,1,0:T(8,128)(2,1)S(1)}, bf16[3,4,16,256]{3,2,1,0:T(8,128)(2,1)S(1)}, u32[]{:S(2)}, u32[]{:S(2)}) collective-permute-start(bf16[3,4,16,256]{3,2,1,0:T(8,128)(2,1)S(1)} %get-tuple-element.85), channel_id=1, source_target_pairs={{0,28},{4,24},{8,4},{12,0},{16,12},{20,8},{24,20},{28,16},{1,29},{... | collective-permute-start | bytes 294920 | tf_op jit(solution)/shard_map/ppermute | solution.py:401
